TPU v7x, 512 devices: a whole 4x4x16 slice. The times are simulated.
512 devices in a mesh: src: 64 (over z_lo, x, core), gx: 2 (over z_hi), gy: 4 (over y).
Axes of the slice: x: 4, y: 4, z: 16 (z_hi: 2, z_lo: 8; z = z_hi * 8 + z_lo), core: 2. Of those that a mesh axis runs over, the one named last changes fastest.
Arguments:
- conductivity: float32 [128, 64, 128], P('gx', 'gy'), may hold values from 0.1 to 10
- potential: float32 [64, 128, 64, 128], P('src', 'gx', 'gy'), may hold values from -6 to 6
- adjoint_guess: float32 [64, 128, 64, 128], P('src', 'gx', 'gy'), may hold values from -4 to 4
- observed: float32 [64, 512], P('src'), may hold values from -6 to 6
- receiver_cells: int32 [3, 512], replicated, may hold values from 0 to 127, as said below
- electrodes: int32 [3, 64], P(None, 'src'), may hold values from 0 to 127, as said below
Outputs:
- adjoint: float32 [64, 128, 64, 128], P('src', 'gx', 'gy')
- residual_rms: float32 [64], P('src')
- gradient: float32 [128, 64, 128], P('gx', 'gy')
Inputs may be any that keep to these rules, and one draw needn't show every extreme that they name: `receiver_cells`: row 0 holds x indices below 128, row 1 y indices below 64, row 2 z indices below 128. `electrodes`: row 0 holds x indices below 128, row 1 y indices below 64; row 2 is 0 (electrodes on the surface layer).
All inputs are finite; a program needn't handle non-finite values.
Results may differ from a plain program's by a relative error of at most 0.0002.
Values sent between devices are 32-bit elements; how exact they have to be, the bound alone decides.
No kernel may reach another device: no remote copies, remote signals or barrier semaphores. Data moves between devices by JAX's collectives and lax.ppermute only.
A program may use at most 64 MiB of HBM per device.

v0:
```python
import jax
import jax.numpy as jnp
from jax import lax
from jax.sharding import PartitionSpec as P

SWEEPS = 4


low_bound = 0.25
high_bound = 2.0


def extended_2(block, sides, width):
    for axis, dim in sides:
        count = lax.axis_size(axis)
        forward = [(i, i + 1) for i in range(count - 1)]
        backward = [(target, source) for source, target in forward]
        low = lax.ppermute(
            lax.slice_in_dim(block, block.shape[dim] - width, None, axis=dim), axis, forward
        )
        high = lax.ppermute(lax.slice_in_dim(block, 0, width, axis=dim), axis, backward)
        block = jnp.concatenate([low, block, high], axis=dim)
    return block


def neighbours(padded):
    return [
        padded[..., 2:, 1:-1, 1:-1],
        padded[..., :-2, 1:-1, 1:-1],
        padded[..., 1:-1, 2:, 1:-1],
        padded[..., 1:-1, :-2, 1:-1],
        padded[..., 1:-1, 1:-1, 2:],
        padded[..., 1:-1, 1:-1, :-2],
    ]


def depth_pad(extended):
    return jnp.pad(extended, ((0, 0), (0, 0), (0, 0), (1, 1)))


def apply_operator(field, face_list, diagonal):
    extended = extended_2(field, (("gx", 1), ("gy", 2)), 1)
    total = diagonal * field
    for face, near in zip(face_list, neighbours(depth_pad(extended))):
        total = total - face * near
    return total


def place_source(
    misfit, receiver_cells, electrodes, anchor_x, anchor_y, span_x, span_y, src_count, depth
):
    members = jnp.arange(src_count, dtype=jnp.int32)
    local_x = receiver_cells[0] - anchor_x
    local_y = receiver_cells[1] - anchor_y
    inside = ((local_x >= 0) & (local_x < span_x) & (local_y >= 0) & (local_y < span_y)).astype(
        jnp.float32
    )
    clip_x = jnp.clip(local_x, 0, span_x - 1)
    clip_y = jnp.clip(local_y, 0, span_y - 1)
    elec_x = electrodes[0] - anchor_x
    elec_y = electrodes[1] - anchor_y
    inside_elec = ((elec_x >= 0) & (elec_x < span_x) & (elec_y >= 0) & (elec_y < span_y)).astype(
        jnp.float32
    )
    elec_cx = jnp.clip(elec_x, 0, span_x - 1)
    elec_cy = jnp.clip(elec_y, 0, span_y - 1)
    placed = (
        jnp.zeros((src_count, span_x, span_y, depth), jnp.float32)
        .at[members[:, None], clip_x[None, :], clip_y[None, :], receiver_cells[2][None, :]]
        .add(misfit * inside[None, :])
    )
    placed = placed.at[members, elec_cx, elec_cy, electrodes[2]].add(
        -jnp.sum(misfit, axis=1) * inside_elec
    )
    return placed


def body(conductivity, potential, adjoint_guess, observed, receiver_cells, electrodes):
    theta = 0.5 * (high_bound + low_bound)
    delta = 0.5 * (high_bound - low_bound)
    sigma = theta / delta
    src_count, width_x, width_y, depth = potential.shape
    total_x = width_x * lax.axis_size("gx")
    total_y = width_y * lax.axis_size("gy")
    start_x = lax.axis_index("gx") * width_x
    start_y = lax.axis_index("gy") * width_y
    local_x = receiver_cells[0] - start_x
    local_y = receiver_cells[1] - start_y
    inside = ((local_x >= 0) & (local_x < width_x) & (local_y >= 0) & (local_y < width_y)).astype(
        jnp.float32
    )
    clip_x = jnp.clip(local_x, 0, width_x - 1)
    clip_y = jnp.clip(local_y, 0, width_y - 1)
    elec_x = electrodes[0] - start_x
    elec_y = electrodes[1] - start_y
    inside_elec = ((elec_x >= 0) & (elec_x < width_x) & (elec_y >= 0) & (elec_y < width_y)).astype(
        jnp.float32
    )
    elec_cx = jnp.clip(elec_x, 0, width_x - 1)
    elec_cy = jnp.clip(elec_y, 0, width_y - 1)
    members = jnp.arange(src_count, dtype=jnp.int32)
    rec_values = potential[:, clip_x, clip_y, receiver_cells[2]] * inside[None, :]
    elec_values = potential[members, elec_cx, elec_cy, electrodes[2]] * inside_elec
    rec_values, elec_values = lax.psum((rec_values, elec_values), ("gx", "gy"))
    misfit = rec_values - elec_values[:, None] - observed
    sig_ext = extended_2(conductivity, (("gx", 0), ("gy", 1)), 1)
    sig_padded = jnp.pad(sig_ext, ((0, 0), (0, 0), (1, 1)))
    face_list = [0.5 * (conductivity + near) for near in neighbours(sig_padded)]
    diagonal = face_list[0]
    for face in face_list[1:]:
        diagonal = diagonal + face
    adjoint_source = place_source(
        misfit, receiver_cells, electrodes, start_x, start_y, width_x, width_y, src_count, depth
    )
    solution = adjoint_guess
    residual = adjoint_source - apply_operator(solution, face_list, diagonal)
    direction = residual / (theta * diagonal)
    ratio = 1.0 / sigma
    for sweep in range(SWEEPS):
        solution = solution + direction
        residual = residual - apply_operator(direction, face_list, diagonal)
        if sweep < SWEEPS - 1:
            following = 1.0 / (2.0 * sigma - ratio)
            direction = (
                following * ratio * direction + 2.0 * following / delta * residual / diagonal
            )
            ratio = following
    cell_total = total_x * total_y * depth
    squares = lax.psum(jnp.sum(residual * residual, axis=(1, 2, 3)), ("gx", "gy"))
    residual_rms = jnp.sqrt(squares / cell_total)
    stacked = jnp.concatenate([solution, potential], axis=0)
    extended = extended_2(stacked, (("gx", 1), ("gy", 2)), 1)
    term_cell = jnp.zeros_like(potential)
    for near in neighbours(depth_pad(extended)):
        term_cell = term_cell - 0.5 * (solution - near[:src_count]) * (potential - near[src_count:])
    grad_local = jnp.sum(term_cell, axis=0)
    sens_local = jnp.sum(term_cell * term_cell, axis=0)
    total_sources = src_count * lax.axis_size("src")
    grad_sum, sens_sum = lax.psum((grad_local, sens_local), "src")
    gradient = grad_sum * lax.rsqrt(sens_sum / total_sources + 1.0)
    return (solution, residual_rms, gradient)


def solution(mesh):
    return jax.shard_map(
        body,
        mesh=mesh,
        in_specs=(
            P("gx", "gy", None),
            P("src", "gx", "gy", None),
            P("src", "gx", "gy", None),
            P("src", None),
            P(),
            P(None, "src"),
        ),
        out_specs=(P("src", "gx", "gy", None), P("src"), P("gx", "gy", None)),
        check_vma=False,
    )
```

profile of v0, /device:TPU:1, one launch (start us, length us, event | category | flops | bytes accessed | tf_op | source)
XLA Modules:
  0.0 1103.8 jit_solution(16825493092893849326)
XLA Ops:
  9.3 16.3 %collective-permute-start.1 = (f32[1,16,128]{2,1,0:T(8,128)S(1)}, f32[1,16,128]{2,1,0:T(8,128)S(1)}, u32[]{:S(2)}, u32[]{:S(2)}) collective-permute-start(f32[1,16,128]{2,1,0:T(8,128)S(1)} %get-tuple-element.70), channel_id=1, source_target_pairs={{0,4},{1,5},{2,6},{3,7},{8,12},{9,13},{10,14},{11,15},{16,20},{17,... | collective-permute-start | bytes 24584 | tf_op jit(solution)/shard_map/ppermute | solution.py:18
  27.6 12.7 %collective-permute-start.5 = (f32[1,1,16,128]{3,2,1,0:T(8,128)S(1)}, f32[1,1,16,128]{3,2,1,0:T(8,128)S(1)}, u32[]{:S(2)}, u32[]{:S(2)}) collective-permute-start(f32[1,1,16,128]{3,2,1,0:T(8,128)S(1)} %get-tuple-element.72), channel_id=1, source_target_pairs={{0,4},{1,5},{2,6},{3,7},{8,12},{9,13},{10,14},{11,15},{16,20},{17,... | collective-permute-start | bytes 24584 | tf_op jit(solution)/shard_map/ppermute | solution.py:18
  45.9 11.3 %gather_fusion = f32[512]{0:T(512)S(1)} fusion(f32[64,16,128]{2,1,0:T(8,128)} %bitcast.163, s32[512]{0:T(512)S(1)} %bitcast.162), kind=kCustom, calls=%fused_computation | custom fusion | bytes 10240 | tf_op jit(solution)/shard_map/gather | solution.py:102
  59.4 32.9 %all-reduce.8 = (f32[1,512]{1,0:T(1,128)S(1)}, f32[]{:T(128)}) all-reduce(f32[1,512]{1,0:T(1,128)S(1)} %get-tuple-element.43, f32[]{:T(128)} %bitcast.20), channel_id=1, replica_groups=mesh['src'=64,'gx'=2,'gy'=4] {'gx','gy'}, use_global_device_ids=true, to_apply=%region_0.1 | all-reduce | flops 513 | bytes 4104 | tf_op jit(solution)/shard_map/psum | solution.py:104
  95.0 30.3 %scatter_fusion = f32[64,16,128]{2,1,0:T(8,128)S(1)} fusion(f32[64,16,128]{2,1,0:T(8,128)S(1)} %broadcast.240, s32[512]{0:T(512)S(1)} %bitcast.161, f32[512]{0:T(512)S(1)} %bitcast.166), kind=kCustom, calls=%fused_computation.1 | custom fusion | flops 512 | bytes 12288 | tf_op jit(solution)/shard_map/scatter-add | solution.py:70
  131.1 4.0 collective-permute-start.7
  137.2 2.5 collective-permute-done.6
  141.7 13.0 %collective-permute-start.9 = (f32[1,1,16,128]{3,2,1,0:T(8,128)S(1)}, f32[1,1,16,128]{3,2,1,0:T(8,128)S(1)}, u32[]{:S(2)}, u32[]{:S(2)}) collective-permute-start(f32[1,1,16,128]{3,2,1,0:T(8,128)S(1)} %get-tuple-element.67), channel_id=1, source_target_pairs={{0,4},{1,5},{2,6},{3,7},{8,12},{9,13},{10,14},{11,15},{16,20},{17,... | collective-permute-start | bytes 24584 | tf_op jit(solution)/shard_map/ppermute | solution.py:18
  156.0 11.8 %collective-permute-done.8 = f32[1,1,16,128]{3,2,1,0:T(8,128)S(1)} collective-permute-done((f32[1,1,16,128]{3,2,1,0:T(8,128)S(1)}, f32[1,1,16,128]{3,2,1,0:T(8,128)S(1)}, u32[]{:S(2)}, u32[]{:S(2)}) %collective-permute-start.8) | collective-permute-done | bytes 8224 | tf_op jit(solution)/shard_map/ppermute | solution.py:21
  167.8 1.6 collective-permute-start.11
  170.8 3.7 collective-permute-done.10
  178.6 11.9 %collective-permute-done.12 = f32[1,1,16,128]{3,2,1,0:T(8,128)S(1)} collective-permute-done((f32[1,1,16,128]{3,2,1,0:T(8,128)S(1)}, f32[1,1,16,128]{3,2,1,0:T(8,128)S(1)}, u32[]{:S(2)}, u32[]{:S(2)}) %collective-permute-start.12) | collective-permute-done | bytes 8224 | tf_op jit(solution)/shard_map/ppermute | solution.py:21
  190.5 1.9 collective-permute-start.15
  193.7 3.7 collective-permute-done.14
  198.1 2.3 fusion.93
  200.5 1.6 collective-permute-start.17
  203.4 11.9 %collective-permute-done.16 = f32[1,1,16,128]{3,2,1,0:T(8,128)S(1)} collective-permute-done((f32[1,1,16,128]{3,2,1,0:T(8,128)S(1)}, f32[1,1,16,128]{3,2,1,0:T(8,128)S(1)}, u32[]{:S(2)}, u32[]{:S(2)}) %collective-permute-start.16) | collective-permute-done | bytes 8224 | tf_op jit(solution)/shard_map/ppermute | solution.py:21
  215.3 1.9 collective-permute-start.19
  218.7 3.2 collective-permute-done.18
  224.3 1.9 collective-permute-start.25
  227.5 12.0 %collective-permute-done.24 = f32[2,1,16,128]{3,2,1,0:T(8,128)S(1)} collective-permute-done((f32[2,1,16,128]{3,2,1,0:T(8,128)S(1)}, f32[2,1,16,128]{3,2,1,0:T(8,128)S(1)}, u32[]{:S(2)}, u32[]{:S(2)}) %collective-permute-start.24) | collective-permute-done | bytes 16416 | tf_op jit(solution)/shard_map/ppermute | solution.py:21
  239.6 1.9 collective-permute-start.27
  242.9 3.7 collective-permute-done.26
  246.6 3.0 select_maximum_fusion
  249.6 2.7 multiply_bitcast_fusion
  252.4 1.7 collective-permute-start.21
  255.4 11.9 %collective-permute-done.20 = f32[1,1,16,128]{3,2,1,0:T(8,128)S(1)} collective-permute-done((f32[1,1,16,128]{3,2,1,0:T(8,128)S(1)}, f32[1,1,16,128]{3,2,1,0:T(8,128)S(1)}, u32[]{:S(2)}, u32[]{:S(2)}) %collective-permute-start.20) | collective-permute-done | bytes 8224 | tf_op jit(solution)/shard_map/ppermute | solution.py:21
  267.3 1.9 collective-permute-start.23
  270.5 3.4 collective-permute-done.22
  276.0 30.5 %psum.37 = f32[1]{0:T(128)} all-reduce(f32[1]{0:T(128)} %bitcast.35), channel_id=1, replica_groups=mesh['src'=64,'gx'=2,'gy'=4] {'gx','gy'}, use_global_device_ids=true, to_apply=%region_6.7 | all-reduce | flops 1 | bytes 8 | tf_op jit(solution)/shard_map/psum | solution.py:129
  307.2 786.5 %all-reduce.11.cloned.1.call-done = (f32[64,16,128]{2,1,0:T(8,128)}, f32[64,16,128]{2,1,0:T(8,128)}) async-done(((f32[64,16,128]{2,1,0:T(8,128)}, f32[64,16,128]{2,1,0:T(8,128)}), (f32[64,16,128]{2,1,0:T(8,128)}, f32[64,16,128]{2,1,0:T(8,128)})) %all-reduce.11.cloned.1.call-update) | async-done | bytes 1048592 | tf_op jit(solution)/shard_map/psum | solution.py:139
  1093.7 2.1 rsqrt_multiply_fusion
  (107 shorter events, 39.2 us)
Async XLA Ops:
  7.2 86.4 %copy-start.13 = (s32[4]{0:T(128)S(1)}, s32[4]{0:T(128)}, u32[]{:S(2)}) copy-start(s32[4]{0:T(128)} %constant.92.clone.1) | copy-start | bytes 52
  7.2 85.1 %copy-start.12 = (f32[1,512]{1,0:T(1,128)S(1)}, f32[1,512]{1,0:T(1,128)}, u32[]{:S(2)}) copy-start(f32[1,512]{1,0:T(1,128)} %param.11) | copy-start | bytes 6148
  7.2 1086.5 %all-reduce.11.cloned.1.call-start = ((), (), s32[]{:S(2)}) async-start(), calls=%async_computation | async-start | bytes 2097152 | tf_op jit(solution)/shard_map/psum | solution.py:139
  8.0 120.0 %collective-permute-start = (f32[1,16,128]{2,1,0:T(8,128)S(1)}, f32[1,16,128]{2,1,0:T(8,128)S(1)}, u32[]{:S(2)}, u32[]{:S(2)}) collective-permute-start(f32[1,16,128]{2,1,0:T(8,128)S(1)} %get-tuple-element.69), channel_id=1, source_target_pairs={{4,0},{5,1},{6,2},{7,3},{12,8},{13,9},{14,10},{15,11},{20,16},{21,... | collective-permute-start | bytes 24584 | tf_op jit(solution)/shard_map/ppermute | solution.py:21
  9.3 118.6 %collective-permute-start.1 = (f32[1,16,128]{2,1,0:T(8,128)S(1)}, f32[1,16,128]{2,1,0:T(8,128)S(1)}, u32[]{:S(2)}, u32[]{:S(2)}) collective-permute-start(f32[1,16,128]{2,1,0:T(8,128)S(1)} %get-tuple-element.70), channel_id=1, source_target_pairs={{0,4},{1,5},{2,6},{3,7},{8,12},{9,13},{10,14},{11,15},{16,20},{17,... | collective-permute-start | bytes 24584 | tf_op jit(solution)/shard_map/ppermute | solution.py:18
  26.3 104.7 %collective-permute-start.4 = (f32[1,1,16,128]{3,2,1,0:T(8,128)S(1)}, f32[1,1,16,128]{3,2,1,0:T(8,128)S(1)}, u32[]{:S(2)}, u32[]{:S(2)}) collective-permute-start(f32[1,1,16,128]{3,2,1,0:T(8,128)S(1)} %get-tuple-element.71), channel_id=1, source_target_pairs={{4,0},{5,1},{6,2},{7,3},{12,8},{13,9},{14,10},{15,11},{20,16},{21,... | collective-permute-start | bytes 24584 | tf_op jit(solution)/shard_map/ppermute | solution.py:21
  27.6 100.5 %collective-permute-start.5 = (f32[1,1,16,128]{3,2,1,0:T(8,128)S(1)}, f32[1,1,16,128]{3,2,1,0:T(8,128)S(1)}, u32[]{:S(2)}, u32[]{:S(2)}) collective-permute-start(f32[1,1,16,128]{3,2,1,0:T(8,128)S(1)} %get-tuple-element.72), channel_id=1, source_target_pairs={{0,4},{1,5},{2,6},{3,7},{8,12},{9,13},{10,14},{11,15},{16,20},{17,... | collective-permute-start | bytes 24584 | tf_op jit(solution)/shard_map/ppermute | solution.py:18
  128.1 8.3 collective-permute-start.3
  129.7 6.7 collective-permute-start.2
  131.1 6.1 collective-permute-start.7
  135.1 4.7 collective-permute-start.6
  141.6 81.0 %copy-start.3 = (f32[64,16,128]{2,1,0:T(8,128)}, f32[64,16,128]{2,1,0:T(8,128)S(1)}, u32[]{:S(2)}) copy-start(f32[64,16,128]{2,1,0:T(8,128)S(1)} %get-tuple-element.41) | copy-start | bytes 1572868
  141.7 14.3 %collective-permute-start.9 = (f32[1,1,16,128]{3,2,1,0:T(8,128)S(1)}, f32[1,1,16,128]{3,2,1,0:T(8,128)S(1)}, u32[]{:S(2)}, u32[]{:S(2)}) collective-permute-start(f32[1,1,16,128]{3,2,1,0:T(8,128)S(1)} %get-tuple-element.67), channel_id=1, source_target_pairs={{0,4},{1,5},{2,6},{3,7},{8,12},{9,13},{10,14},{11,15},{16,20},{17,... | collective-permute-start | bytes 24584 | tf_op jit(solution)/shard_map/ppermute | solution.py:18
  154.7 13.1 %collective-permute-start.8 = (f32[1,1,16,128]{3,2,1,0:T(8,128)S(1)}, f32[1,1,16,128]{3,2,1,0:T(8,128)S(1)}, u32[]{:S(2)}, u32[]{:S(2)}) collective-permute-start(f32[1,1,16,128]{3,2,1,0:T(8,128)S(1)} %get-tuple-element.68), channel_id=1, source_target_pairs={{4,0},{5,1},{6,2},{7,3},{12,8},{13,9},{14,10},{15,11},{20,16},{21,... | collective-permute-start | bytes 24584 | tf_op jit(solution)/shard_map/ppermute | solution.py:21
  167.8 2.9 collective-permute-start.11
  169.4 5.0 collective-permute-start.10
  175.9 2.6 collective-permute-start.13
  177.2 13.2 %collective-permute-start.12 = (f32[1,1,16,128]{3,2,1,0:T(8,128)S(1)}, f32[1,1,16,128]{3,2,1,0:T(8,128)S(1)}, u32[]{:S(2)}, u32[]{:S(2)}) collective-permute-start(f32[1,1,16,128]{3,2,1,0:T(8,128)S(1)} %get-tuple-element.66), channel_id=1, source_target_pairs={{4,0},{5,1},{6,2},{7,3},{12,8},{13,9},{14,10},{15,11},{20,16},{21,... | collective-permute-start | bytes 24584 | tf_op jit(solution)/shard_map/ppermute | solution.py:21
  190.5 3.2 collective-permute-start.15
  192.4 5.0 collective-permute-start.14
  200.5 2.9 collective-permute-start.17
  202.1 13.2 %collective-permute-start.16 = (f32[1,1,16,128]{3,2,1,0:T(8,128)S(1)}, f32[1,1,16,128]{3,2,1,0:T(8,128)S(1)}, u32[]{:S(2)}, u32[]{:S(2)}) collective-permute-start(f32[1,1,16,128]{3,2,1,0:T(8,128)S(1)} %get-tuple-element.64), channel_id=1, source_target_pairs={{4,0},{5,1},{6,2},{7,3},{12,8},{13,9},{14,10},{15,11},{20,16},{21,... | collective-permute-start | bytes 24584 | tf_op jit(solution)/shard_map/ppermute | solution.py:21
  215.3 3.4 collective-permute-start.19
  217.2 4.7 collective-permute-start.18
  224.3 3.2 collective-permute-start.25
  226.2 13.3 %collective-permute-start.24 = (f32[2,1,16,128]{3,2,1,0:T(8,128)S(1)}, f32[2,1,16,128]{3,2,1,0:T(8,128)S(1)}, u32[]{:S(2)}, u32[]{:S(2)}) collective-permute-start(f32[2,1,16,128]{3,2,1,0:T(8,128)S(1)} %get-tuple-element.48), channel_id=1, source_target_pairs={{4,0},{5,1},{6,2},{7,3},{12,8},{13,9},{14,10},{15,11},{20,16},{21,... | collective-permute-start | bytes 49160 | tf_op jit(solution)/shard_map/ppermute | solution.py:21
  239.6 3.3 collective-permute-start.27
  241.5 5.0 collective-permute-start.26
  252.4 3.0 collective-permute-start.21
  254.1 13.2 %collective-permute-start.20 = (f32[1,1,16,128]{3,2,1,0:T(8,128)S(1)}, f32[1,1,16,128]{3,2,1,0:T(8,128)S(1)}, u32[]{:S(2)}, u32[]{:S(2)}) collective-permute-start(f32[1,1,16,128]{3,2,1,0:T(8,128)S(1)} %get-tuple-element.62), channel_id=1, source_target_pairs={{4,0},{5,1},{6,2},{7,3},{12,8},{13,9},{14,10},{15,11},{20,16},{21,... | collective-permute-start | bytes 24584 | tf_op jit(solution)/shard_map/ppermute | solution.py:21
  267.3 3.2 collective-permute-start.23
  269.2 4.7 collective-permute-start.22
  (11 other events, 344.5 us)
Sparse Core Ops, SparseCore 0:
  252.5 841.2 all-reduce.10
where the time goes:
time: 1100 us
  waiting for transfers between devices  866 us (79%)
  starting transfers between devices  81.6 us (7%)
  blocking collectives  63.4 us (6%)
  other arithmetic  53.3 us (5%)
  between operations  23.1 us (2%)
  local copies, waits for them, and re-layouts  16.3 us (1%)
    psum x1, waiting for transfers between devices, body(): grad_sum, sens_sum = lax.psum((grad_local, sens_local), 'src')  787 us
    ppermute x14, waiting for transfers between devices, extended_2(): lax.ppermute(lax.slice_in_dim(block, 0, width, axis=dim), axis, backward)  79.4 us
    ppermute x14, starting transfers between devices, extended_2(): lax.ppermute(lax.slice_in_dim(block, block.shape[dim] - width, None, axis...  63.3 us
    psum x1, blocking collectives, body(): rec_values, elec_values = lax.psum((rec_values, elec_values), ('gx', 'gy'))  32.9 us
    psum x1, blocking collectives, body(): lax.psum(jnp.sum(residual * residual, axis=(1, 2, 3)), ('gx', 'gy'))  30.5 us
    scatter-add x1, other arithmetic, place_source(): placed = jnp.zeros((src_count, span_x, span_y, depth), jnp.float32).at[me...  30.3 us
  transfers between devices with their start and end apart: 29, of which 12 were waited for; matrix products, arithmetic and copies ran while one was open for 5% of the time, Pallas kernels for 0%

commit v1 on v0

v1 whole, which is shorter than its diff:
```python
import jax
import jax.numpy as jnp
from jax import lax
from jax.experimental import pallas as pl
from jax.experimental.pallas import tpu as pltpu
from jax.sharding import PartitionSpec as P

SWEEPS = 4
LOW, HIGH = 0.25, 2.0
THETA = 0.5 * (HIGH + LOW)
DELTA = 0.5 * (HIGH - LOW)
SIGMA = THETA / DELTA

WX, WY, DEPTH = 64, 16, 128
NREC = 512
HALO = SWEEPS + 1
EX = WX + 2 * HALO
EY = WY + 16
LINE = 8
PLANE = 8
f32, bf16, i32 = jnp.float32, jnp.bfloat16, jnp.int32


def split3(value):
    top = value.astype(bf16)
    rest = value - top.astype(f32)
    middle = rest.astype(bf16)
    low = (rest - middle.astype(f32)).astype(bf16)
    return top, middle, low


def gather_kernel(rec, elec, pot, guess, cond, out):
    gx, gy = lax.axis_index("gx"), lax.axis_index("gy")
    base = jnp.where(gx == 0, WX - HALO, 0)
    for k in range(HALO):
        for half in range(2):
            out[2 * k + half] = guess[base + k, 8 * half : 8 * half + 8]
            out[10 + 2 * k + half] = cond[base + k, 8 * half : 8 * half + 8]
    face = jnp.where(gx == 0, WX - 1, 0)
    out[20] = pot[face, 0:8]
    out[21] = pot[face, 8:16]
    lx = rec[0:1, :] - gx * WX
    ly = rec[1:2, :] - gy * WY
    inside = (lx >= 0) & (lx < WX) & (ly >= 0) & (ly < WY)
    row = jnp.where(inside, lx * WY + ly, -1)
    hot = jnp.where(lax.broadcasted_iota(i32, (WX * WY, NREC), 0) == row, 1.0, 0.0).astype(bf16)
    turned = jnp.transpose(pot[...].reshape(WX * WY, DEPTH))
    parts = [jnp.dot(part, hot, preferred_element_type=f32) for part in split3(turned)]
    values = parts[0] + (parts[1] + parts[2])
    level = lax.broadcasted_iota(i32, (DEPTH, NREC), 0) == rec[2:3, :]
    picked = jnp.sum(jnp.where(level, values, 0.0), axis=0, keepdims=True)
    for k in range(NREC // DEPTH):
        out[22, k : k + 1, :] = picked[:, DEPTH * k : DEPTH * (k + 1)]
    ex = elec[0, 0] - gx * WX
    ey = elec[1, 0] - gy * WY
    held = (ex >= 0) & (ex < WX) & (ey >= 0) & (ey < WY)
    cx = jnp.clip(ex, 0, WX - 1)
    cy = jnp.clip(ey, 0, WY - 1)
    plane = pot[cx]
    here = (lax.broadcasted_iota(i32, (WY, DEPTH), 0) == cy) & (
        lax.broadcasted_iota(i32, (WY, DEPTH), 1) == elec[2, 0]
    )
    there = jnp.sum(jnp.where(here & held, plane, 0.0), axis=0, keepdims=True)
    out[22, 4:5, :] = jnp.broadcast_to(jnp.sum(there, axis=1, keepdims=True), (1, DEPTH))
    out[22, 5:8, :] = jnp.zeros((3, DEPTH), f32)


def pack_kernel(mine, theirs, pot, guess, cond, up, down, partial):
    sub = lax.broadcasted_iota(i32, (8, DEPTH), 0)

    def step(i, _):
        up[i, 0] = jnp.where(sub < 3, pltpu.roll(pot[i, 8:16], 1, 0), guess[i, 8:16])
        up[i, 1] = cond[i, 8:16]
        down[i, 0] = jnp.where(sub >= 5, pltpu.roll(pot[i, 0:8], 7, 0), guess[i, 0:8])
        down[i, 1] = cond[i, 0:8]
        return 0

    lax.fori_loop(0, WX, step, 0, unroll=4)
    for k in range(HALO):
        down[WX + k, 0] = theirs[2 * k]
        down[WX + k, 1] = theirs[10 + 2 * k]
        up[WX + k, 0] = theirs[2 * k + 1]
        up[WX + k, 1] = theirs[10 + 2 * k + 1]
    total = mine[22] + theirs[22]
    up[WX + HALO, 0] = total
    up[WX + HALO, 1] = total
    down[WX + HALO, 0] = total
    down[WX + HALO, 1] = total
    partial[...] = total


def smooth_kernel(
    rec, elec, obs, pot, guess, cond, across, from_low, from_high, own_sum, far_sum,
    adjoint, term, squares,
    c, v, r, d0, d1, fx, fy, fz, diag, inv, phi,
):
    gx, gy = lax.axis_index("gx"), lax.axis_index("gy")
    sub = lax.broadcasted_iota(i32, (8, DEPTH), 0)
    lane = lax.broadcasted_iota(i32, (EY, DEPTH), 1)
    last, first = lane == DEPTH - 1, lane == 0
    low_on, high_on = (gy > 0), (gy < lax.axis_size("gy") - 1)
    low_keep, high_keep = low_on & (sub >= 3), high_on & (sub < 5)

    def lay(i, source):
        tile = from_low[source, 0]
        v[i, 0:8] = jnp.where(low_keep, tile, 0.0)
        phi[i, 0:8] = jnp.where(low_on & (sub == 7), pltpu.roll(tile, 7, 0), 0.0)
        c[i, 0:8] = jnp.where(low_keep, from_low[source, 1], 0.0)
        tile = from_high[source, 0]
        v[i, 24:32] = jnp.where(high_keep, tile, 0.0)
        phi[i, 24:32] = jnp.where(high_on & (sub == 0), pltpu.roll(tile, 1, 0), 0.0)
        c[i, 24:32] = jnp.where(high_keep, from_high[source, 1], 0.0)

    def own(i, _):
        lay(i + HALO, i)
        v[i + HALO, 8:24] = guess[i]
        phi[i + HALO, 8:24] = pot[i]
        c[i + HALO, 8:24] = cond[i]
        return 0

    lax.fori_loop(0, WX, own, 0, unroll=2)
    blank = jnp.zeros((EY, DEPTH), f32)
    empty = jnp.where(gx == 0, 0, WX + HALO)
    there = jnp.where(gx == 0, WX + HALO, 0)
    for k in range(HALO):
        for ref in (v, phi, c):
            ref[empty + k] = blank
        lay(there + k, WX + k)
        for half in range(2):
            span = slice(8 + 8 * half, 16 + 8 * half)
            v[there + k, span] = across[2 * k + half]
            c[there + k, span] = across[10 + 2 * k + half]
            phi[there + k, span] = across[20 + half]

    def coefficients(i, _):
        here = c[i]
        fx[i] = 0.5 * (here + c[jnp.minimum(i + 1, EX - 1)])
        side = 0.5 * (here + pltpu.roll(here, EY - 1, 0))
        fy[i] = side
        near = jnp.where(last, 0.0, pltpu.roll(here, DEPTH - 1, 1))
        deep = 0.5 * (here + near)
        back = jnp.where(first, 0.5 * here, pltpu.roll(deep, 1, 1))
        fz[i] = jnp.where(last, 0.0, deep)
        before = 0.5 * (here + c[jnp.maximum(i - 1, 0)])
        total = fx[i] + before + side + pltpu.roll(side, 1, 0) + deep + back
        diag[i] = total
        inv[i] = jnp.where(here > 0.0, 1.0 / total, 0.0)
        return 0

    lax.fori_loop(0, EX, coefficients, 0, unroll=2)

    lx = rec[0:1, :] - gx * WX + HALO
    ly = rec[1:2, :] - gy * WY + 8
    near = (lx >= 0) & (lx < EX) & (ly >= 0) & (ly < EY)
    row = jnp.where(near, lx * EY + ly, -1)
    total = own_sum[...] + far_sum[...] + from_low[WX + HALO, 0] + from_high[WX + HALO, 0]
    anchor = total[4:5, :]
    pieces = [
        total[k : k + 1, :] - anchor - obs[:, DEPTH * k : DEPTH * (k + 1)]
        for k in range(NREC // DEPTH)
    ]
    misfit = jnp.concatenate(pieces, axis=1)
    whole = jnp.sum(misfit, axis=1, keepdims=True)
    level = lax.broadcasted_iota(i32, (DEPTH, NREC), 0) == rec[2:3, :]
    weights = jnp.concatenate(split3(jnp.where(level, misfit, 0.0)), axis=0)
    rows_at_once = 2

    def scatter(i, _):
        start = i * rows_at_once
        ids = lax.broadcasted_iota(i32, (rows_at_once * EY, NREC), 0) + start * EY
        hot = jnp.where(ids == row, 1.0, 0.0).astype(bf16)
        got = lax.dot_general(
            hot, weights, (((1,), (1,)), ((), ())), preferred_element_type=f32
        )
        placed = got[:, :DEPTH] + (got[:, DEPTH : 2 * DEPTH] + got[:, 2 * DEPTH :])
        r[pl.ds(start, rows_at_once)] = placed.reshape(rows_at_once, EY, DEPTH)
        return 0

    lax.fori_loop(0, EX // rows_at_once, scatter, 0)
    ex = elec[0, 0] - gx * WX + HALO
    ey = elec[1, 0] - gy * WY + 8
    held = (ex >= 0) & (ex < EX) & (ey >= 0) & (ey < EY)
    cx = jnp.clip(ex, 0, EX - 1)
    spot = (lax.broadcasted_iota(i32, (EY, DEPTH), 0) == ey) & (lane == elec[2, 0]) & held
    r[cx] = r[cx] - jnp.where(spot, whole, 0.0)

    def applied(ref, i):
        here = ref[i]
        out = diag[i] * here - fx[i] * ref[i + 1] - fx[i - 1] * ref[i - 1]
        side = fy[i]
        out = out - side * pltpu.roll(here, EY - 1, 0) - pltpu.roll(side * here, 1, 0)
        deep = fz[i]
        return out - deep * pltpu.roll(here, DEPTH - 1, 1) - pltpu.roll(deep * here, 1, 1)

    def begin(i, _):
        left = r[i] - applied(v, i)
        r[i] = left
        d0[i] = left * inv[i] * (1.0 / THETA)
        return 0

    lax.fori_loop(1, EX - 1, begin, 0, unroll=2)
    ratio = 1.0 / SIGMA
    source, target = d0, d1
    for sweep in range(SWEEPS - 1):
        following = 1.0 / (2.0 * SIGMA - ratio)
        keep, gain = following * ratio, 2.0 * following / DELTA

        def advance(i, _, source=source, target=target, keep=keep, gain=gain):
            here = source[i]
            v[i] = v[i] + here
            left = r[i] - applied(source, i)
            r[i] = left
            target[i] = keep * here + gain * (left * inv[i])
            return 0

        lax.fori_loop(2 + sweep, EX - 2 - sweep, advance, 0, unroll=2)
        ratio = following
        source, target = target, source

    v[HALO - 1] = v[HALO - 1] + source[HALO - 1]
    v[WX + HALO] = v[WX + HALO] + source[WX + HALO]

    def finish(i, acc):
        k = i + HALO
        here = source[k]
        new = v[k] + here
        v[k] = new
        adjoint[i] = new[8:24]
        left = (r[k] - applied(source, k))[8:24]
        return acc + left * left

    acc = lax.fori_loop(0, WX, finish, jnp.zeros((WY, DEPTH), f32), unroll=2)
    squares[...] = acc[0:8] + acc[8:16]

    def product(i, _):
        k = i + HALO
        a, p = v[k], phi[k]
        out = (a - v[k + 1]) * (p - phi[k + 1]) + (a - v[k - 1]) * (p - phi[k - 1])
        side = (a - pltpu.roll(a, EY - 1, 0)) * (p - pltpu.roll(p, EY - 1, 0))
        out = out + side + pltpu.roll(side, 1, 0)
        deep = (a - jnp.where(last, 0.0, pltpu.roll(a, DEPTH - 1, 1))) * (
            p - jnp.where(last, 0.0, pltpu.roll(p, DEPTH - 1, 1))
        )
        out = out + deep + jnp.where(first, a * p, pltpu.roll(deep, 1, 1))
        term[i] = -0.5 * out[8:24]
        return 0

    lax.fori_loop(0, WX, product, 0, unroll=2)


def plane_kernel(parts, own, got, out, acc):
    for q in range(LINE):
        total = parts[0, q]
        square = total * total
        for k in range(1, PLANE):
            more = parts[k, q]
            total = total + more
            square = square + more * more
        out[q, 0] = total
        out[q, 1] = square
    acc[...] = own[...] + got[...]


def scale_kernel(sources, parts, own, got, out, acc):
    total, square = parts[0, 0], parts[0, 1]
    for q in range(1, LINE):
        total = total + parts[q, 0]
        square = square + parts[q, 1]
    value = total * lax.rsqrt(square / sources + 1.0)
    for q in range(LINE):
        out[q] = value
    acc[...] = own[...] + got[...]


def spread_kernel(cells, rows, own, got, out, rms):
    value = rows[...]
    for k in range(PLANE):
        out[k] = value
    total = jnp.sum(own[...] + got[...], axis=0, keepdims=True)
    rms[...] = jnp.broadcast_to(
        jnp.sqrt(jnp.sum(total, axis=1, keepdims=True) / cells), (1, DEPTH)
    )


VM = pl.BlockSpec(memory_space=pltpu.VMEM)
SM = pl.BlockSpec(memory_space=pltpu.SMEM)


def call(kernel, shapes, specs, *args, scratch=(), flops=0, moved=0):
    return pl.pallas_call(
        kernel,
        out_shape=[jax.ShapeDtypeStruct(shape, f32) for shape in shapes],
        in_specs=specs,
        out_specs=[VM] * len(shapes),
        scratch_shapes=list(scratch),
        compiler_params=pltpu.CompilerParams(vmem_limit_bytes=48 * 1024 * 1024),
        cost_estimate=pl.CostEstimate(flops=flops, bytes_accessed=moved, transcendentals=0),
    )(*args)


def body(conductivity, potential, adjoint_guess, observed, receiver_cells, electrodes):
    sources = lax.axis_size("src")
    pot, guess = potential[0], adjoint_guess[0]
    tile = (8, DEPTH)
    swap_x = [(0, 1), (1, 0)]
    (mine,) = call(
        gather_kernel, [(23, 8, DEPTH)], [VM, SM, VM, VM, VM],
        receiver_cells, electrodes, pot, guess, conductivity,
    )
    theirs = lax.ppermute(mine, "gx", swap_x)
    faces = (WX + HALO + 1, 2, 8, DEPTH)
    up, down, partial = call(
        pack_kernel, [faces, faces, tile], [VM] * 5, mine, theirs, pot, guess, conductivity
    )
    ring = lambda step: [(i, (i + step) % 4) for i in range(4)]
    from_low = lax.ppermute(up, "gy", ring(1))
    from_high = lax.ppermute(down, "gy", ring(3))
    far = lax.ppermute(partial, "gy", ring(2))
    block = (WX, WY, DEPTH)
    adjoint, term, squares = call(
        smooth_kernel, [block, block, tile], [VM, SM] + [VM] * 9,
        receiver_cells, electrodes, observed, pot, guess, conductivity,
        theirs, from_low, from_high, partial, far,
        scratch=[pltpu.VMEM((EX, EY, DEPTH), f32)] * 11,
    )
    planes = [[z * PLANE + k for k in range(PLANE)] for z in range(LINE)]
    lines = [[z * PLANE + k for z in range(LINE)] for k in range(PLANE)]

    def exchange(value, groups):
        return lax.all_to_all(value, "src", 0, 0, axis_index_groups=groups, tiled=True)

    other = lax.ppermute(squares, "gx", swap_x)
    got = exchange(term.reshape(PLANE, LINE, WY, DEPTH), planes)
    sums, squares = call(
        plane_kernel, [(LINE, 2, WY, DEPTH), tile], [VM] * 3, got, squares, other
    )
    other = lax.ppermute(squares, "gy", [(0, 1), (1, 0), (2, 3), (3, 2)])
    got = exchange(sums, lines)
    scaled, squares = call(
        lambda *refs: scale_kernel(sources, *refs),
        [(LINE, WY, DEPTH), tile], [VM] * 3, got, squares, other,
    )
    other = lax.ppermute(squares, "gy", [(0, 2), (2, 0), (1, 3), (3, 1)])
    got = exchange(scaled, lines)
    cells = WX * lax.axis_size("gx") * WY * lax.axis_size("gy") * DEPTH
    spread, rms = call(
        lambda *refs: spread_kernel(cells, *refs),
        [(PLANE, LINE, WY, DEPTH), (1, DEPTH)], [VM] * 3, got, squares, other,
    )
    gradient = exchange(spread, planes).reshape(block)
    return adjoint[None], rms[0, :1], gradient


def solution(mesh):
    return jax.shard_map(
        body,
        mesh=mesh,
        in_specs=(
            P("gx", "gy", None),
            P("src", "gx", "gy", None),
            P("src", "gx", "gy", None),
            P("src", None),
            P(),
            P(None, "src"),
        ),
        out_specs=(P("src", "gx", "gy", None), P("src"), P("gx", "gy", None)),
        check_vma=False,
    )
```

time: 1100 us -> 160 us (0.15)
  waiting for transfers between devices: 866 us -> 22.2 us
  other arithmetic: 53.3 us -> 0 us
  blocking collectives: 63.4 us -> 16.7 us
  Pallas kernels: 0 us -> 41.3 us
  between operations: 23.1 us -> 0.73 us
    psum x1 -> x0, waiting for transfers between devices: 787 us -> none  [body(): grad_sum, sens_sum = lax.psum((grad_local, sens_local), 'src')]
    ppermute x28 -> x7, waiting for transfers between devices: 79.5 us -> 13 us  [the longest x1 6.96 us: body(): far = lax.ppermute(partial, 'gy', ring(2))]
    psum x2 -> x0, blocking collectives: 63.4 us -> none  [the longest x1 32.9 us: body(): rec_values, elec_values = lax.psum((rec_values, elec_values), ('gx', 'gy'))]
    pallas_call x0 -> x6, Pallas kernels: none -> 41.3 us  [call(): pl.pallas_call(kernel, out_shape=[jax.ShapeDtypeStruct(shape, f32) for sh...]
    ppermute x28 -> x7, starting transfers between devices: 81.5 us -> 46.8 us  [the longest x1 16.3 us: body(): theirs = lax.ppermute(mine, 'gx', swap_x)]
    scatter-add x1 -> x0, other arithmetic: 30.3 us -> none  [place_source(): placed = jnp.zeros((src_count, span_x, span_y, depth), jnp.float32).at[me...]
    all_to_all x0 -> x3, starting transfers between devices: none -> 26.2 us  [exchange(): lax.all_to_all(value, 'src', 0, 0, axis_index_groups=groups, tiled=True)]
    all_to_all x0 -> x1, blocking collectives: none -> 16.7 us  [exchange(): lax.all_to_all(value, 'src', 0, 0, axis_index_groups=groups, tiled=True)]
  transfers between devices with their start and end apart: 29 -> 10, of which waited for: 12 -> 8; matrix products, arithmetic and copies ran while one was open for 5% -> 0% of each run, Pallas kernels for 0% -> 0%
where the time goes in v1:
time: 160 us; the launch traced here: 159 us
  starting transfers between devices  73 us (46%)
  Pallas kernels  41.3 us (26%)
  waiting for transfers between devices  22.2 us (14%)
  blocking collectives  16.7 us (10%)
  local copies, waits for them, and re-layouts  5.37 us (3%)
    pallas_call x6, Pallas kernels, call(): pl.pallas_call(kernel, out_shape=[jax.ShapeDtypeStruct(shape, f32) for sh...  41.3 us
    all_to_all x3, starting transfers between devices, exchange(): lax.all_to_all(value, 'src', 0, 0, axis_index_groups=groups, tiled=True)  26.2 us
    all_to_all x1, blocking collectives, exchange(): lax.all_to_all(value, 'src', 0, 0, axis_index_groups=groups, tiled=True)  16.7 us
    ppermute x1, starting transfers between devices, body(): theirs = lax.ppermute(mine, 'gx', swap_x)  16.3 us
    ppermute x1, starting transfers between devices, body(): other = lax.ppermute(squares, 'gx', swap_x)  11.8 us
    all_to_all x3, waiting for transfers between devices, exchange(): lax.all_to_all(value, 'src', 0, 0, axis_index_groups=groups, tiled=True)  9.23 us
    ppermute x1, waiting for transfers between devices, body(): far = lax.ppermute(partial, 'gy', ring(2))  6.96 us
    unnamed x18, local copies, waits for them, and re-layouts  5.37 us
  transfers between devices with their start and end apart: 10, of which 8 were waited for; matrix products, arithmetic and copies ran while one was open for 0% of the time, Pallas kernels for 0%

profile of v1, /device:TPU:1, one launch (start us, length us, event | category | flops | bytes accessed | tf_op | source)
XLA Modules:
  0.0 159.3 jit_solution(2844228297065800830)
XLA Ops:
  0.6 0.7 copy.10.elec
  1.4 1.0 copy-done
  2.4 1.0 copy-done.2
  3.5 1.0 copy-done.4
  4.5 0.7 copy-done.6
  5.2 1.4 shard_map.85.mine
  6.6 16.3 %collective-permute-start = (f32[23,8,128]{2,1,0:T(8,128)S(1)}, f32[23,8,128]{2,1,0:T(8,128)S(1)}, u32[]{:S(2)}, u32[]{:S(2)}) collective-permute-start(f32[23,8,128]{2,1,0:T(8,128)S(1)} %shard_map.85.mine), channel_id=1, source_target_pairs={{0,4},{4,0},{1,5},{5,1},{2,6},{6,2},{3,7},{7,3},{8,12},{12,8},{9,1... | collective-permute-start | bytes 282632 | tf_op jit(solution)/shard_map/ppermute | solution.py:310
  22.9 2.2 %collective-permute-done.theirs.across = f32[23,8,128]{2,1,0:T(8,128)S(1)} collective-permute-done((f32[23,8,128]{2,1,0:T(8,128)S(1)}, f32[23,8,128]{2,1,0:T(8,128)S(1)}, u32[]{:S(2)}, u32[]{:S(2)}) %collective-permute-start) | collective-permute-done | bytes 94240 | tf_op jit(solution)/shard_map/ppermute | solution.py:310
  25.1 0.1 shard_map.86
  25.3 0.0 copy-start.7
  25.3 3.4 %collective-permute-start.1 = (f32[70,2,8,128]{3,2,1,0:T(8,128)S(1)}, f32[70,2,8,128]{3,2,1,0:T(8,128)S(1)}, u32[]{:S(2)}, u32[]{:S(2)}) collective-permute-start(f32[70,2,8,128]{3,2,1,0:T(8,128)S(1)} %get-tuple-element.15), channel_id=1, source_target_pairs={{0,1},{1,2},{2,3},{3,0},{4,5},{5,6},{6,7},{7,4},{8,9},{9,10},{10,1... | collective-permute-start | bytes 1720328 | tf_op jit(solution)/shard_map/ppermute | solution.py:316
  28.7 3.4 %collective-permute-start.2 = (f32[70,2,8,128]{3,2,1,0:T(8,128)S(1)}, f32[70,2,8,128]{3,2,1,0:T(8,128)S(1)}, u32[]{:S(2)}, u32[]{:S(2)}) collective-permute-start(f32[70,2,8,128]{3,2,1,0:T(8,128)S(1)} %get-tuple-element.16), channel_id=1, source_target_pairs={{0,3},{1,0},{2,1},{3,2},{4,7},{5,4},{6,5},{7,6},{8,11},{9,8},{10,9... | collective-permute-start | bytes 1720328 | tf_op jit(solution)/shard_map/ppermute | solution.py:317
  32.0 3.5 %collective-permute-start.3 = (f32[8,128]{1,0:T(8,128)S(1)}, f32[8,128]{1,0:T(8,128)S(1)}, u32[]{:S(2)}, u32[]{:S(2)}) collective-permute-start(f32[8,128]{1,0:T(8,128)S(1)} %get-tuple-element.17.own_sum), channel_id=1, source_target_pairs={{0,2},{1,3},{2,0},{3,1},{4,6},{5,7},{6,4},{7,5},{8,10},{9,11},{10,... | collective-permute-start | bytes 12296 | tf_op jit(solution)/shard_map/ppermute | solution.py:318
  35.6 7.0 %collective-permute-done.3.far_sum = f32[8,128]{1,0:T(8,128)S(1)} collective-permute-done((f32[8,128]{1,0:T(8,128)S(1)}, f32[8,128]{1,0:T(8,128)S(1)}, u32[]{:S(2)}, u32[]{:S(2)}) %collective-permute-start.3) | collective-permute-done | bytes 4128 | tf_op jit(solution)/shard_map/ppermute | solution.py:318
  42.6 0.2 collective-permute-done.2.from_high
  42.8 37.7 %shard_map.87 = (f32[64,16,128]{2,1,0:T(8,128)}, f32[64,16,128]{2,1,0:T(8,128)}, f32[8,128]{1,0:T(8,128)S(1)}) custom-call(s32[3,512]{1,0:T(4,128)S(1)} %copy-done.6, s32[3,1]{1,0:T(4,128)S(1)} %copy.10.elec, f32[1,512]{1,0:T(1,128)S(1)} %copy-done.7, f32[64,16,128]{2,1,0:T(8,128)S(1)} %bitcast.9, f32[64,16,128]{2,1,0:T(8,128)S(1)} %bitcast.12, ...), custom_call_target="tpu_custom_call" | custom-call | tf_op jit(solution)/shard_map/pallas_call | solution.py:290
  80.5 7.5 %all-to-all-start = ((f32[8,8,16,128]{3,2,1,0:T(8,128)}), f32[8,8,16,128]{3,2,1,0:T(8,128)S(1)}, u32[]{:S(2)}, u32[]{:S(2)}) async-start(f32[8,8,16,128]{3,2,1,0:T(8,128)} %bitcast.3), calls=%async_computation | async-start | bytes 1048576 | tf_op jit(solution)/shard_map/all_to_all | solution.py:330
  88.0 11.8 %collective-permute-start.4 = (f32[8,128]{1,0:T(8,128)S(1)}, f32[8,128]{1,0:T(8,128)S(1)}, u32[]{:S(2)}, u32[]{:S(2)}) collective-permute-start(f32[8,128]{1,0:T(8,128)S(1)} %get-tuple-element.20.own), channel_id=1, source_target_pairs={{0,4},{4,0},{1,5},{5,1},{2,6},{6,2},{3,7},{7,3},{8,12},{12,8},{9,1... | collective-permute-start | bytes 12296 | tf_op jit(solution)/shard_map/ppermute | solution.py:332
  99.8 1.3 collective-permute-done.4.got
  101.1 0.7 shard_map.88
  101.8 13.4 %all-to-all-start.1 = ((f32[8,2,16,128]{3,2,1,0:T(8,128)}), f32[8,2,16,128]{3,2,1,0:T(8,128)S(1)}, u32[]{:S(2)}, u32[]{:S(2)}) async-start(f32[8,2,16,128]{3,2,1,0:T(8,128)} %get-tuple-element.21), calls=%async_computation.1 | async-start | bytes 262144 | tf_op jit(solution)/shard_map/all_to_all | solution.py:330
  115.2 4.0 %collective-permute-start.5 = (f32[8,128]{1,0:T(8,128)S(1)}, f32[8,128]{1,0:T(8,128)S(1)}, u32[]{:S(2)}, u32[]{:S(2)}) collective-permute-start(f32[8,128]{1,0:T(8,128)S(1)} %get-tuple-element.22.refs_1_), channel_id=1, source_target_pairs={{0,1},{1,0},{2,3},{3,2},{4,5},{5,4},{6,7},{7,6},{8,9},{9,8},{10,11... | collective-permute-start | bytes 12296 | tf_op jit(solution)/shard_map/ppermute | solution.py:337
  119.2 1.0 collective-permute-done.5.refs_2_
  120.2 5.3 %all-to-all-done.1.refs_0_ = f32[8,2,16,128]{3,2,1,0:T(8,128)S(1)} async-done(((f32[8,2,16,128]{3,2,1,0:T(8,128)}), f32[8,2,16,128]{3,2,1,0:T(8,128)S(1)}, u32[]{:S(2)}, u32[]{:S(2)}) %all-to-all-start.1) | async-done | bytes 131104 | tf_op jit(solution)/shard_map/all_to_all | solution.py:330
  125.5 0.7 shard_map.89
  126.1 5.3 %all-to-all-start.2 = ((f32[8,16,128]{2,1,0:T(8,128)}), f32[8,16,128]{2,1,0:T(8,128)S(1)}, u32[]{:S(2)}, u32[]{:S(2)}) async-start(f32[8,16,128]{2,1,0:T(8,128)} %get-tuple-element.23), calls=%async_computation.2 | async-start | bytes 131072 | tf_op jit(solution)/shard_map/all_to_all | solution.py:330
  131.4 4.5 %collective-permute-start.6 = (f32[8,128]{1,0:T(8,128)S(1)}, f32[8,128]{1,0:T(8,128)S(1)}, u32[]{:S(2)}, u32[]{:S(2)}) collective-permute-start(f32[8,128]{1,0:T(8,128)S(1)} %get-tuple-element.24.refs_1_), channel_id=1, source_target_pairs={{0,2},{2,0},{1,3},{3,1},{4,6},{6,4},{5,7},{7,5},{8,10},{10,8},{9,1... | collective-permute-start | bytes 12296 | tf_op jit(solution)/shard_map/ppermute | solution.py:343
  136.0 1.3 collective-permute-done.6.refs_2_
  137.3 3.9 %all-to-all-done.2.refs_0_ = f32[8,16,128]{2,1,0:T(8,128)S(1)} async-done(((f32[8,16,128]{2,1,0:T(8,128)}), f32[8,16,128]{2,1,0:T(8,128)S(1)}, u32[]{:S(2)}, u32[]{:S(2)}) %all-to-all-start.2) | async-done | bytes 65568 | tf_op jit(solution)/shard_map/all_to_all | solution.py:330
  141.2 0.6 shard_map.90
  141.8 16.7 %all_to_all.20 = f32[8,8,16,128]{3,2,1,0:T(8,128)S(1)} all-to-all(f32[8,8,16,128]{3,2,1,0:T(8,128)S(1)} %get-tuple-element.26), channel_id=1, replica_groups={{0,8,16,24,32,40,48,56},{64,72,80,88,96,104,112,120},{128,136,144,152,1..., dimensions={0} | all-to-all | bytes 1048576 | tf_op jit(solution)/shard_map/all_to_all | solution.py:330
  158.5 0.8 copy.12
  (13 shorter events, 0.0 us)
Async XLA Ops:
  1.4 1.0 copy-start
  2.4 1.0 copy-start.2
  3.5 1.0 copy-start.4
  4.5 0.7 copy-start.6
  5.2 19.9 %copy-start.1 = (f32[1,64,16,128]{3,2,1,0:T(8,128)S(1)}, f32[1,64,16,128]{3,2,1,0:T(8,128)}, u32[]{:S(2)}) copy-start(f32[1,64,16,128]{3,2,1,0:T(8,128)} %param.7) | copy-start | bytes 1572868
  5.2 19.9 %copy-start.3 = (f32[1,64,16,128]{3,2,1,0:T(8,128)S(1)}, f32[1,64,16,128]{3,2,1,0:T(8,128)}, u32[]{:S(2)}) copy-start(f32[1,64,16,128]{3,2,1,0:T(8,128)} %param.8) | copy-start | bytes 1572868
  5.2 19.9 %copy-start.5 = (f32[64,16,128]{2,1,0:T(8,128)S(1)}, f32[64,16,128]{2,1,0:T(8,128)}, u32[]{:S(2)}) copy-start(f32[64,16,128]{2,1,0:T(8,128)} %cond.5) | copy-start | bytes 1572868
  6.6 18.5 %collective-permute-start = (f32[23,8,128]{2,1,0:T(8,128)S(1)}, f32[23,8,128]{2,1,0:T(8,128)S(1)}, u32[]{:S(2)}, u32[]{:S(2)}) collective-permute-start(f32[23,8,128]{2,1,0:T(8,128)S(1)} %shard_map.85.mine), channel_id=1, source_target_pairs={{0,4},{4,0},{1,5},{5,1},{2,6},{6,2},{3,7},{7,3},{8,12},{12,8},{9,1... | collective-permute-start | bytes 282632 | tf_op jit(solution)/shard_map/ppermute | solution.py:310
  25.3 17.5 %copy-start.7 = (f32[1,512]{1,0:T(1,128)S(1)}, f32[1,512]{1,0:T(1,128)}, u32[]{:S(2)}) copy-start(f32[1,512]{1,0:T(1,128)} %obs.1) | copy-start | bytes 6148
  25.3 17.3 %collective-permute-start.1 = (f32[70,2,8,128]{3,2,1,0:T(8,128)S(1)}, f32[70,2,8,128]{3,2,1,0:T(8,128)S(1)}, u32[]{:S(2)}, u32[]{:S(2)}) collective-permute-start(f32[70,2,8,128]{3,2,1,0:T(8,128)S(1)} %get-tuple-element.15), channel_id=1, source_target_pairs={{0,1},{1,2},{2,3},{3,0},{4,5},{5,6},{6,7},{7,4},{8,9},{9,10},{10,1... | collective-permute-start | bytes 1720328 | tf_op jit(solution)/shard_map/ppermute | solution.py:316
  28.7 14.1 %collective-permute-start.2 = (f32[70,2,8,128]{3,2,1,0:T(8,128)S(1)}, f32[70,2,8,128]{3,2,1,0:T(8,128)S(1)}, u32[]{:S(2)}, u32[]{:S(2)}) collective-permute-start(f32[70,2,8,128]{3,2,1,0:T(8,128)S(1)} %get-tuple-element.16), channel_id=1, source_target_pairs={{0,3},{1,0},{2,1},{3,2},{4,7},{5,4},{6,5},{7,6},{8,11},{9,8},{10,9... | collective-permute-start | bytes 1720328 | tf_op jit(solution)/shard_map/ppermute | solution.py:317
  32.0 10.5 %collective-permute-start.3 = (f32[8,128]{1,0:T(8,128)S(1)}, f32[8,128]{1,0:T(8,128)S(1)}, u32[]{:S(2)}, u32[]{:S(2)}) collective-permute-start(f32[8,128]{1,0:T(8,128)S(1)} %get-tuple-element.17.own_sum), channel_id=1, source_target_pairs={{0,2},{1,3},{2,0},{3,1},{4,6},{5,7},{6,4},{7,5},{8,10},{9,11},{10,... | collective-permute-start | bytes 12296 | tf_op jit(solution)/shard_map/ppermute | solution.py:318
  80.5 20.6 %all-to-all-start = ((f32[8,8,16,128]{3,2,1,0:T(8,128)}), f32[8,8,16,128]{3,2,1,0:T(8,128)S(1)}, u32[]{:S(2)}, u32[]{:S(2)}) async-start(f32[8,8,16,128]{3,2,1,0:T(8,128)} %bitcast.3), calls=%async_computation | async-start | bytes 1048576 | tf_op jit(solution)/shard_map/all_to_all | solution.py:330
  88.0 13.1 %collective-permute-start.4 = (f32[8,128]{1,0:T(8,128)S(1)}, f32[8,128]{1,0:T(8,128)S(1)}, u32[]{:S(2)}, u32[]{:S(2)}) collective-permute-start(f32[8,128]{1,0:T(8,128)S(1)} %get-tuple-element.20.own), channel_id=1, source_target_pairs={{0,4},{4,0},{1,5},{5,1},{2,6},{6,2},{3,7},{7,3},{8,12},{12,8},{9,1... | collective-permute-start | bytes 12296 | tf_op jit(solution)/shard_map/ppermute | solution.py:332
  101.8 23.7 %all-to-all-start.1 = ((f32[8,2,16,128]{3,2,1,0:T(8,128)}), f32[8,2,16,128]{3,2,1,0:T(8,128)S(1)}, u32[]{:S(2)}, u32[]{:S(2)}) async-start(f32[8,2,16,128]{3,2,1,0:T(8,128)} %get-tuple-element.21), calls=%async_computation.1 | async-start | bytes 262144 | tf_op jit(solution)/shard_map/all_to_all | solution.py:330
  115.2 5.0 %collective-permute-start.5 = (f32[8,128]{1,0:T(8,128)S(1)}, f32[8,128]{1,0:T(8,128)S(1)}, u32[]{:S(2)}, u32[]{:S(2)}) collective-permute-start(f32[8,128]{1,0:T(8,128)S(1)} %get-tuple-element.22.refs_1_), channel_id=1, source_target_pairs={{0,1},{1,0},{2,3},{3,2},{4,5},{5,4},{6,7},{7,6},{8,9},{9,8},{10,11... | collective-permute-start | bytes 12296 | tf_op jit(solution)/shard_map/ppermute | solution.py:337
  126.1 15.1 %all-to-all-start.2 = ((f32[8,16,128]{2,1,0:T(8,128)}), f32[8,16,128]{2,1,0:T(8,128)S(1)}, u32[]{:S(2)}, u32[]{:S(2)}) async-start(f32[8,16,128]{2,1,0:T(8,128)} %get-tuple-element.23), calls=%async_computation.2 | async-start | bytes 131072 | tf_op jit(solution)/shard_map/all_to_all | solution.py:330
  131.4 5.8 %collective-permute-start.6 = (f32[8,128]{1,0:T(8,128)S(1)}, f32[8,128]{1,0:T(8,128)S(1)}, u32[]{:S(2)}, u32[]{:S(2)}) collective-permute-start(f32[8,128]{1,0:T(8,128)S(1)} %get-tuple-element.24.refs_1_), channel_id=1, source_target_pairs={{0,2},{2,0},{1,3},{3,1},{4,6},{6,4},{5,7},{7,5},{8,10},{10,8},{9,1... | collective-permute-start | bytes 12296 | tf_op jit(solution)/shard_map/ppermute | solution.py:343

commit v2 on v1

--- a/solution.py
+++ b/solution.py
@@ -18,6 +18,8 @@
 EY = WY + 16
 LINE = 8
 PLANE = 8
+ROWS = 36
+SCATTERS = 2
 f32, bf16, i32 = jnp.float32, jnp.bfloat16, jnp.int32
 
 
@@ -27,6 +29,30 @@
     middle = rest.astype(bf16)
     low = (rest - middle.astype(f32)).astype(bf16)
     return top, middle, low
+
+
+def ahead(i):
+    return pl.ds(i.start + 1, i.size)
+
+
+def behind(i):
+    return pl.ds(i.start - 1, i.size)
+
+
+def shifted(i):
+    return pl.ds(i.start - HALO, i.size)
+
+
+def over_rows(low, high, step):
+    count, rest = divmod(high - low, ROWS)
+
+    def turn(k, _):
+        step(pl.ds(low + k * ROWS, ROWS))
+        return 0
+
+    lax.fori_loop(0, count, turn, 0)
+    if rest:
+        step(pl.ds(high - rest, rest))
 
 
 def gather_kernel(rec, elec, pot, guess, cond, out):
@@ -96,8 +122,6 @@
 ):
     gx, gy = lax.axis_index("gx"), lax.axis_index("gy")
     sub = lax.broadcasted_iota(i32, (8, DEPTH), 0)
-    lane = lax.broadcasted_iota(i32, (EY, DEPTH), 1)
-    last, first = lane == DEPTH - 1, lane == 0
     low_on, high_on = (gy > 0), (gy < lax.axis_size("gy") - 1)
     low_keep, high_keep = low_on & (sub >= 3), high_on & (sub < 5)
 
@@ -132,22 +156,25 @@
             c[there + k, span] = across[10 + 2 * k + half]
             phi[there + k, span] = across[20 + half]
 
-    def coefficients(i, _):
+    lane = lax.broadcasted_iota(i32, (1, EY, DEPTH), 2)
+    last, first = lane == DEPTH - 1, lane == 0
+    fx[0] = 0.5 * (c[0] + c[1])
+
+    def coefficients(i):
         here = c[i]
-        fx[i] = 0.5 * (here + c[jnp.minimum(i + 1, EX - 1)])
-        side = 0.5 * (here + pltpu.roll(here, EY - 1, 0))
+        after = 0.5 * (here + c[ahead(i)])
+        before = 0.5 * (c[behind(i)] + here)
+        side = 0.5 * (here + pltpu.roll(here, EY - 1, 1))
+        deep = 0.5 * (here + jnp.where(last, 0.0, pltpu.roll(here, DEPTH - 1, 2)))
+        back = jnp.where(first, 0.5 * here, pltpu.roll(deep, 1, 2))
+        total = after + before + side + pltpu.roll(side, 1, 1) + deep + back
+        fx[i] = after
         fy[i] = side
-        near = jnp.where(last, 0.0, pltpu.roll(here, DEPTH - 1, 1))
-        deep = 0.5 * (here + near)
-        back = jnp.where(first, 0.5 * here, pltpu.roll(deep, 1, 1))
         fz[i] = jnp.where(last, 0.0, deep)
-        before = 0.5 * (here + c[jnp.maximum(i - 1, 0)])
-        total = fx[i] + before + side + pltpu.roll(side, 1, 0) + deep + back
         diag[i] = total
         inv[i] = jnp.where(here > 0.0, 1.0 / total, 0.0)
-        return 0
-
-    lax.fori_loop(0, EX, coefficients, 0, unroll=2)
+
+    over_rows(1, EX - 1, coefficients)
 
     lx = rec[0:1, :] - gx * WX + HALO
     ly = rec[1:2, :] - gy * WY + 8
@@ -163,89 +190,87 @@
     whole = jnp.sum(misfit, axis=1, keepdims=True)
     level = lax.broadcasted_iota(i32, (DEPTH, NREC), 0) == rec[2:3, :]
     weights = jnp.concatenate(split3(jnp.where(level, misfit, 0.0)), axis=0)
-    rows_at_once = 2
-
-    def scatter(i, _):
-        start = i * rows_at_once
-        ids = lax.broadcasted_iota(i32, (rows_at_once * EY, NREC), 0) + start * EY
+    span = EX // SCATTERS
+    for k in range(SCATTERS):
+        ids = lax.broadcasted_iota(i32, (span * EY, NREC), 0) + k * span * EY
         hot = jnp.where(ids == row, 1.0, 0.0).astype(bf16)
         got = lax.dot_general(
             hot, weights, (((1,), (1,)), ((), ())), preferred_element_type=f32
         )
         placed = got[:, :DEPTH] + (got[:, DEPTH : 2 * DEPTH] + got[:, 2 * DEPTH :])
-        r[pl.ds(start, rows_at_once)] = placed.reshape(rows_at_once, EY, DEPTH)
-        return 0
-
-    lax.fori_loop(0, EX // rows_at_once, scatter, 0)
+        r[k * span : (k + 1) * span] = placed.reshape(span, EY, DEPTH)
+
     ex = elec[0, 0] - gx * WX + HALO
     ey = elec[1, 0] - gy * WY + 8
     held = (ex >= 0) & (ex < EX) & (ey >= 0) & (ey < EY)
     cx = jnp.clip(ex, 0, EX - 1)
-    spot = (lax.broadcasted_iota(i32, (EY, DEPTH), 0) == ey) & (lane == elec[2, 0]) & held
+    spot = (
+        (lax.broadcasted_iota(i32, (EY, DEPTH), 0) == ey)
+        & (lax.broadcasted_iota(i32, (EY, DEPTH), 1) == elec[2, 0])
+        & held
+    )
     r[cx] = r[cx] - jnp.where(spot, whole, 0.0)
 
     def applied(ref, i):
         here = ref[i]
-        out = diag[i] * here - fx[i] * ref[i + 1] - fx[i - 1] * ref[i - 1]
+        out = diag[i] * here - fx[i] * ref[ahead(i)] - fx[behind(i)] * ref[behind(i)]
         side = fy[i]
-        out = out - side * pltpu.roll(here, EY - 1, 0) - pltpu.roll(side * here, 1, 0)
+        out = out - side * pltpu.roll(here, EY - 1, 1) - pltpu.roll(side * here, 1, 1)
         deep = fz[i]
-        return out - deep * pltpu.roll(here, DEPTH - 1, 1) - pltpu.roll(deep * here, 1, 1)
-
-    def begin(i, _):
+        return out - deep * pltpu.roll(here, DEPTH - 1, 2) - pltpu.roll(deep * here, 1, 2)
+
+    def begin(i):
         left = r[i] - applied(v, i)
         r[i] = left
         d0[i] = left * inv[i] * (1.0 / THETA)
-        return 0
-
-    lax.fori_loop(1, EX - 1, begin, 0, unroll=2)
+
+    over_rows(1, EX - 1, begin)
     ratio = 1.0 / SIGMA
     source, target = d0, d1
     for sweep in range(SWEEPS - 1):
         following = 1.0 / (2.0 * SIGMA - ratio)
         keep, gain = following * ratio, 2.0 * following / DELTA
 
-        def advance(i, _, source=source, target=target, keep=keep, gain=gain):
+        def advance(i, source=source, target=target, keep=keep, gain=gain):
             here = source[i]
-            v[i] = v[i] + here
             left = r[i] - applied(source, i)
+            new = v[i] + here
+            v[i] = new
             r[i] = left
             target[i] = keep * here + gain * (left * inv[i])
-            return 0
-
-        lax.fori_loop(2 + sweep, EX - 2 - sweep, advance, 0, unroll=2)
+
+        over_rows(2 + sweep, EX - 2 - sweep, advance)
         ratio = following
         source, target = target, source
 
     v[HALO - 1] = v[HALO - 1] + source[HALO - 1]
     v[WX + HALO] = v[WX + HALO] + source[WX + HALO]
-
-    def finish(i, acc):
-        k = i + HALO
-        here = source[k]
-        new = v[k] + here
-        v[k] = new
-        adjoint[i] = new[8:24]
-        left = (r[k] - applied(source, k))[8:24]
-        return acc + left * left
-
-    acc = lax.fori_loop(0, WX, finish, jnp.zeros((WY, DEPTH), f32), unroll=2)
-    squares[...] = acc[0:8] + acc[8:16]
-
-    def product(i, _):
-        k = i + HALO
-        a, p = v[k], phi[k]
-        out = (a - v[k + 1]) * (p - phi[k + 1]) + (a - v[k - 1]) * (p - phi[k - 1])
-        side = (a - pltpu.roll(a, EY - 1, 0)) * (p - pltpu.roll(p, EY - 1, 0))
-        out = out + side + pltpu.roll(side, 1, 0)
-        deep = (a - jnp.where(last, 0.0, pltpu.roll(a, DEPTH - 1, 1))) * (
-            p - jnp.where(last, 0.0, pltpu.roll(p, DEPTH - 1, 1))
+    squares[...] = jnp.zeros((8, DEPTH), f32)
+
+    def finish(i):
+        here = source[i]
+        left = r[i] - applied(source, i)
+        new = v[i] + here
+        v[i] = new
+        adjoint[shifted(i)] = new[:, 8:24]
+        left = left[:, 8:24]
+        left = left * left
+        squares[...] += jnp.sum(left[:, :8] + left[:, 8:], axis=0)
+
+    over_rows(HALO, WX + HALO, finish)
+
+    def product(i):
+        a, p = v[i], phi[i]
+        out = (a - v[ahead(i)]) * (p - phi[ahead(i)]) + (a - v[behind(i)]) * (p - phi[behind(i)])
+        side = (a - pltpu.roll(a, EY - 1, 1)) * (p - pltpu.roll(p, EY - 1, 1))
+        out = out + side + pltpu.roll(side, 1, 1)
+        deep = (a - jnp.where(last, 0.0, pltpu.roll(a, DEPTH - 1, 2))) * (
+            p - jnp.where(last, 0.0, pltpu.roll(p, DEPTH - 1, 2))
         )
-        out = out + deep + jnp.where(first, a * p, pltpu.roll(deep, 1, 1))
-        term[i] = -0.5 * out[8:24]
-        return 0
-
-    lax.fori_loop(0, WX, product, 0, unroll=2)
+        out = out + deep + jnp.where(first, a * p, pltpu.roll(deep, 1, 2))
+        term[shifted(i)] = -0.5 * out[:, 8:24]
+
+    over_rows(HALO, WX + HALO, product)
 
 
 def plane_kernel(parts, own, got, out, acc):

time: 160 us -> 132 us (0.82)
  Pallas kernels: 41.3 us -> 13 us
    pallas_call x6, Pallas kernels: 41.3 us -> 13 us  [call(): pl.pallas_call(kernel, out_shape=[jax.ShapeDtypeStruct(shape, f32) for sh...]
where the time goes in v2:
time: 132 us; the launch traced here: 131 us
  starting transfers between devices  73 us (55%)
  waiting for transfers between devices  22.2 us (17%)
  blocking collectives  16.7 us (13%)
  Pallas kernels  13 us (10%)
  local copies, waits for them, and re-layouts  5.37 us (4%)
    all_to_all x3, starting transfers between devices, exchange(): lax.all_to_all(value, 'src', 0, 0, axis_index_groups=groups, tiled=True)  26.2 us
    all_to_all x1, blocking collectives, exchange(): lax.all_to_all(value, 'src', 0, 0, axis_index_groups=groups, tiled=True)  16.7 us
    ppermute x1, starting transfers between devices, body(): theirs = lax.ppermute(mine, 'gx', swap_x)  16.3 us
    pallas_call x6, Pallas kernels, call(): pl.pallas_call(kernel, out_shape=[jax.ShapeDtypeStruct(shape, f32) for sh...  13 us
    ppermute x1, starting transfers between devices, body(): other = lax.ppermute(squares, 'gx', swap_x)  11.8 us
    all_to_all x3, waiting for transfers between devices, exchange(): lax.all_to_all(value, 'src', 0, 0, axis_index_groups=groups, tiled=True)  9.23 us
    ppermute x1, waiting for transfers between devices, body(): far = lax.ppermute(partial, 'gy', ring(2))  6.96 us
    unnamed x18, local copies, waits for them, and re-layouts  5.37 us
  transfers between devices with their start and end apart: 10, of which 8 were waited for; matrix products, arithmetic and copies ran while one was open for 0% of the time, Pallas kernels for 0%

profile of v2, /device:TPU:1, one launch (start us, length us, event | category | flops | bytes accessed | tf_op | source)
XLA Modules:
  0.0 131.0 jit_solution(1454856952033611772)
XLA Ops:
  0.6 0.7 copy.10.elec
  1.4 1.0 copy-done
  2.4 1.0 copy-done.2
  3.5 1.0 copy-done.4
  4.5 0.7 copy-done.6
  5.2 1.4 %shard_map.85.mine = f32[23,8,128]{2,1,0:T(8,128)S(1)} custom-call(s32[3,512]{1,0:T(4,128)S(1)} %copy-done.6, s32[3,1]{1,0:T(4,128)S(1)} %copy.10.elec, f32[64,16,128]{2,1,0:T(8,128)S(1)} %bitcast.7, f32[64,16,128]{2,1,0:T(8,128)S(1)} %bitcast.10, f32[64,16,128]{2,1,0:T(8,128)S(1)} %copy-done.4), custom_call_target="tpu_custom_call" | custom-call | tf_op jit(solution)/shard_map/pallas_call | solution.py:315
  6.6 16.3 %collective-permute-start = (f32[23,8,128]{2,1,0:T(8,128)S(1)}, f32[23,8,128]{2,1,0:T(8,128)S(1)}, u32[]{:S(2)}, u32[]{:S(2)}) collective-permute-start(f32[23,8,128]{2,1,0:T(8,128)S(1)} %shard_map.85.mine), channel_id=1, source_target_pairs={{0,4},{4,0},{1,5},{5,1},{2,6},{6,2},{3,7},{7,3},{8,12},{12,8},{9,1... | collective-permute-start | bytes 282632 | tf_op jit(solution)/shard_map/ppermute | solution.py:335
  22.9 2.2 %collective-permute-done.theirs.across = f32[23,8,128]{2,1,0:T(8,128)S(1)} collective-permute-done((f32[23,8,128]{2,1,0:T(8,128)S(1)}, f32[23,8,128]{2,1,0:T(8,128)S(1)}, u32[]{:S(2)}, u32[]{:S(2)}) %collective-permute-start) | collective-permute-done | bytes 94240 | tf_op jit(solution)/shard_map/ppermute | solution.py:335
  25.1 0.1 shard_map.86
  25.3 0.0 copy-start.7
  25.3 3.4 %collective-permute-start.1 = (f32[70,2,8,128]{3,2,1,0:T(8,128)S(1)}, f32[70,2,8,128]{3,2,1,0:T(8,128)S(1)}, u32[]{:S(2)}, u32[]{:S(2)}) collective-permute-start(f32[70,2,8,128]{3,2,1,0:T(8,128)S(1)} %get-tuple-element.15), channel_id=1, source_target_pairs={{0,1},{1,2},{2,3},{3,0},{4,5},{5,6},{6,7},{7,4},{8,9},{9,10},{10,1... | collective-permute-start | bytes 1720328 | tf_op jit(solution)/shard_map/ppermute | solution.py:341
  28.7 3.4 %collective-permute-start.2 = (f32[70,2,8,128]{3,2,1,0:T(8,128)S(1)}, f32[70,2,8,128]{3,2,1,0:T(8,128)S(1)}, u32[]{:S(2)}, u32[]{:S(2)}) collective-permute-start(f32[70,2,8,128]{3,2,1,0:T(8,128)S(1)} %get-tuple-element.16), channel_id=1, source_target_pairs={{0,3},{1,0},{2,1},{3,2},{4,7},{5,4},{6,5},{7,6},{8,11},{9,8},{10,9... | collective-permute-start | bytes 1720328 | tf_op jit(solution)/shard_map/ppermute | solution.py:342
  32.0 3.5 %collective-permute-start.3 = (f32[8,128]{1,0:T(8,128)S(1)}, f32[8,128]{1,0:T(8,128)S(1)}, u32[]{:S(2)}, u32[]{:S(2)}) collective-permute-start(f32[8,128]{1,0:T(8,128)S(1)} %get-tuple-element.17.own_sum), channel_id=1, source_target_pairs={{0,2},{1,3},{2,0},{3,1},{4,6},{5,7},{6,4},{7,5},{8,10},{9,11},{10,... | collective-permute-start | bytes 12296 | tf_op jit(solution)/shard_map/ppermute | solution.py:343
  35.6 7.0 %collective-permute-done.3.far_sum = f32[8,128]{1,0:T(8,128)S(1)} collective-permute-done((f32[8,128]{1,0:T(8,128)S(1)}, f32[8,128]{1,0:T(8,128)S(1)}, u32[]{:S(2)}, u32[]{:S(2)}) %collective-permute-start.3) | collective-permute-done | bytes 4128 | tf_op jit(solution)/shard_map/ppermute | solution.py:343
  42.6 0.2 collective-permute-done.2.from_high
  42.8 9.5 %shard_map.87 = (f32[64,16,128]{2,1,0:T(8,128)}, f32[64,16,128]{2,1,0:T(8,128)}, f32[8,128]{1,0:T(8,128)S(1)}) custom-call(s32[3,512]{1,0:T(4,128)S(1)} %copy-done.6, s32[3,1]{1,0:T(4,128)S(1)} %copy.10.elec, f32[1,512]{1,0:T(1,128)S(1)} %copy-done.7, f32[64,16,128]{2,1,0:T(8,128)S(1)} %bitcast.9, f32[64,16,128]{2,1,0:T(8,128)S(1)} %bitcast.12, ...), custom_call_target="tpu_custom_call" | custom-call | tf_op jit(solution)/shard_map/pallas_call | solution.py:315
  52.2 7.5 %all-to-all-start = ((f32[8,8,16,128]{3,2,1,0:T(8,128)}), f32[8,8,16,128]{3,2,1,0:T(8,128)S(1)}, u32[]{:S(2)}, u32[]{:S(2)}) async-start(f32[8,8,16,128]{3,2,1,0:T(8,128)} %bitcast.3), calls=%async_computation | async-start | bytes 1048576 | tf_op jit(solution)/shard_map/all_to_all | solution.py:355
  59.8 11.8 %collective-permute-start.4 = (f32[8,128]{1,0:T(8,128)S(1)}, f32[8,128]{1,0:T(8,128)S(1)}, u32[]{:S(2)}, u32[]{:S(2)}) collective-permute-start(f32[8,128]{1,0:T(8,128)S(1)} %get-tuple-element.20.own), channel_id=1, source_target_pairs={{0,4},{4,0},{1,5},{5,1},{2,6},{6,2},{3,7},{7,3},{8,12},{12,8},{9,1... | collective-permute-start | bytes 12296 | tf_op jit(solution)/shard_map/ppermute | solution.py:357
  71.5 1.3 collective-permute-done.4.got
  72.8 0.7 shard_map.88
  73.5 13.4 %all-to-all-start.1 = ((f32[8,2,16,128]{3,2,1,0:T(8,128)}), f32[8,2,16,128]{3,2,1,0:T(8,128)S(1)}, u32[]{:S(2)}, u32[]{:S(2)}) async-start(f32[8,2,16,128]{3,2,1,0:T(8,128)} %get-tuple-element.21), calls=%async_computation.1 | async-start | bytes 262144 | tf_op jit(solution)/shard_map/all_to_all | solution.py:355
  86.9 4.0 %collective-permute-start.5 = (f32[8,128]{1,0:T(8,128)S(1)}, f32[8,128]{1,0:T(8,128)S(1)}, u32[]{:S(2)}, u32[]{:S(2)}) collective-permute-start(f32[8,128]{1,0:T(8,128)S(1)} %get-tuple-element.22.refs_1_), channel_id=1, source_target_pairs={{0,1},{1,0},{2,3},{3,2},{4,5},{5,4},{6,7},{7,6},{8,9},{9,8},{10,11... | collective-permute-start | bytes 12296 | tf_op jit(solution)/shard_map/ppermute | solution.py:362
  90.9 1.0 collective-permute-done.5.refs_2_
  91.9 5.3 %all-to-all-done.1.refs_0_ = f32[8,2,16,128]{3,2,1,0:T(8,128)S(1)} async-done(((f32[8,2,16,128]{3,2,1,0:T(8,128)}), f32[8,2,16,128]{3,2,1,0:T(8,128)S(1)}, u32[]{:S(2)}, u32[]{:S(2)}) %all-to-all-start.1) | async-done | bytes 131104 | tf_op jit(solution)/shard_map/all_to_all | solution.py:355
  97.2 0.7 shard_map.89
  97.9 5.3 %all-to-all-start.2 = ((f32[8,16,128]{2,1,0:T(8,128)}), f32[8,16,128]{2,1,0:T(8,128)S(1)}, u32[]{:S(2)}, u32[]{:S(2)}) async-start(f32[8,16,128]{2,1,0:T(8,128)} %get-tuple-element.23), calls=%async_computation.2 | async-start | bytes 131072 | tf_op jit(solution)/shard_map/all_to_all | solution.py:355
  103.2 4.5 %collective-permute-start.6 = (f32[8,128]{1,0:T(8,128)S(1)}, f32[8,128]{1,0:T(8,128)S(1)}, u32[]{:S(2)}, u32[]{:S(2)}) collective-permute-start(f32[8,128]{1,0:T(8,128)S(1)} %get-tuple-element.24.refs_1_), channel_id=1, source_target_pairs={{0,2},{2,0},{1,3},{3,1},{4,6},{6,4},{5,7},{7,5},{8,10},{10,8},{9,1... | collective-permute-start | bytes 12296 | tf_op jit(solution)/shard_map/ppermute | solution.py:368
  107.7 1.3 %collective-permute-done.6.refs_2_ = f32[8,128]{1,0:T(8,128)S(1)} collective-permute-done((f32[8,128]{1,0:T(8,128)S(1)}, f32[8,128]{1,0:T(8,128)S(1)}, u32[]{:S(2)}, u32[]{:S(2)}) %collective-permute-start.6) | collective-permute-done | bytes 4128 | tf_op jit(solution)/shard_map/ppermute | solution.py:368
  109.0 3.9 %all-to-all-done.2.refs_0_ = f32[8,16,128]{2,1,0:T(8,128)S(1)} async-done(((f32[8,16,128]{2,1,0:T(8,128)}), f32[8,16,128]{2,1,0:T(8,128)S(1)}, u32[]{:S(2)}, u32[]{:S(2)}) %all-to-all-start.2) | async-done | bytes 65568 | tf_op jit(solution)/shard_map/all_to_all | solution.py:355
  112.9 0.6 shard_map.90
  113.6 16.7 %all_to_all.20 = f32[8,8,16,128]{3,2,1,0:T(8,128)S(1)} all-to-all(f32[8,8,16,128]{3,2,1,0:T(8,128)S(1)} %get-tuple-element.26), channel_id=1, replica_groups={{0,8,16,24,32,40,48,56},{64,72,80,88,96,104,112,120},{128,136,144,152,1..., dimensions={0} | all-to-all | bytes 1048576 | tf_op jit(solution)/shard_map/all_to_all | solution.py:355
  130.2 0.8 copy.12
  (13 shorter events, 0.0 us)
Async XLA Ops:
  1.4 1.0 copy-start
  2.4 1.0 copy-start.2
  3.5 1.0 copy-start.4
  4.5 0.7 copy-start.6
  5.2 19.9 %copy-start.1 = (f32[1,64,16,128]{3,2,1,0:T(8,128)S(1)}, f32[1,64,16,128]{3,2,1,0:T(8,128)}, u32[]{:S(2)}) copy-start(f32[1,64,16,128]{3,2,1,0:T(8,128)} %param.7) | copy-start | bytes 1572868
  5.2 19.9 %copy-start.3 = (f32[1,64,16,128]{3,2,1,0:T(8,128)S(1)}, f32[1,64,16,128]{3,2,1,0:T(8,128)}, u32[]{:S(2)}) copy-start(f32[1,64,16,128]{3,2,1,0:T(8,128)} %param.8) | copy-start | bytes 1572868
  5.2 19.9 %copy-start.5 = (f32[64,16,128]{2,1,0:T(8,128)S(1)}, f32[64,16,128]{2,1,0:T(8,128)}, u32[]{:S(2)}) copy-start(f32[64,16,128]{2,1,0:T(8,128)} %cond.5) | copy-start | bytes 1572868
  6.6 18.5 %collective-permute-start = (f32[23,8,128]{2,1,0:T(8,128)S(1)}, f32[23,8,128]{2,1,0:T(8,128)S(1)}, u32[]{:S(2)}, u32[]{:S(2)}) collective-permute-start(f32[23,8,128]{2,1,0:T(8,128)S(1)} %shard_map.85.mine), channel_id=1, source_target_pairs={{0,4},{4,0},{1,5},{5,1},{2,6},{6,2},{3,7},{7,3},{8,12},{12,8},{9,1... | collective-permute-start | bytes 282632 | tf_op jit(solution)/shard_map/ppermute | solution.py:335
  25.3 17.5 %copy-start.7 = (f32[1,512]{1,0:T(1,128)S(1)}, f32[1,512]{1,0:T(1,128)}, u32[]{:S(2)}) copy-start(f32[1,512]{1,0:T(1,128)} %obs.1) | copy-start | bytes 6148
  25.3 17.3 %collective-permute-start.1 = (f32[70,2,8,128]{3,2,1,0:T(8,128)S(1)}, f32[70,2,8,128]{3,2,1,0:T(8,128)S(1)}, u32[]{:S(2)}, u32[]{:S(2)}) collective-permute-start(f32[70,2,8,128]{3,2,1,0:T(8,128)S(1)} %get-tuple-element.15), channel_id=1, source_target_pairs={{0,1},{1,2},{2,3},{3,0},{4,5},{5,6},{6,7},{7,4},{8,9},{9,10},{10,1... | collective-permute-start | bytes 1720328 | tf_op jit(solution)/shard_map/ppermute | solution.py:341
  28.7 14.1 %collective-permute-start.2 = (f32[70,2,8,128]{3,2,1,0:T(8,128)S(1)}, f32[70,2,8,128]{3,2,1,0:T(8,128)S(1)}, u32[]{:S(2)}, u32[]{:S(2)}) collective-permute-start(f32[70,2,8,128]{3,2,1,0:T(8,128)S(1)} %get-tuple-element.16), channel_id=1, source_target_pairs={{0,3},{1,0},{2,1},{3,2},{4,7},{5,4},{6,5},{7,6},{8,11},{9,8},{10,9... | collective-permute-start | bytes 1720328 | tf_op jit(solution)/shard_map/ppermute | solution.py:342
  32.0 10.5 %collective-permute-start.3 = (f32[8,128]{1,0:T(8,128)S(1)}, f32[8,128]{1,0:T(8,128)S(1)}, u32[]{:S(2)}, u32[]{:S(2)}) collective-permute-start(f32[8,128]{1,0:T(8,128)S(1)} %get-tuple-element.17.own_sum), channel_id=1, source_target_pairs={{0,2},{1,3},{2,0},{3,1},{4,6},{5,7},{6,4},{7,5},{8,10},{9,11},{10,... | collective-permute-start | bytes 12296 | tf_op jit(solution)/shard_map/ppermute | solution.py:343
  52.2 20.6 %all-to-all-start = ((f32[8,8,16,128]{3,2,1,0:T(8,128)}), f32[8,8,16,128]{3,2,1,0:T(8,128)S(1)}, u32[]{:S(2)}, u32[]{:S(2)}) async-start(f32[8,8,16,128]{3,2,1,0:T(8,128)} %bitcast.3), calls=%async_computation | async-start | bytes 1048576 | tf_op jit(solution)/shard_map/all_to_all | solution.py:355
  59.8 13.1 %collective-permute-start.4 = (f32[8,128]{1,0:T(8,128)S(1)}, f32[8,128]{1,0:T(8,128)S(1)}, u32[]{:S(2)}, u32[]{:S(2)}) collective-permute-start(f32[8,128]{1,0:T(8,128)S(1)} %get-tuple-element.20.own), channel_id=1, source_target_pairs={{0,4},{4,0},{1,5},{5,1},{2,6},{6,2},{3,7},{7,3},{8,12},{12,8},{9,1... | collective-permute-start | bytes 12296 | tf_op jit(solution)/shard_map/ppermute | solution.py:357
  73.5 23.7 %all-to-all-start.1 = ((f32[8,2,16,128]{3,2,1,0:T(8,128)}), f32[8,2,16,128]{3,2,1,0:T(8,128)S(1)}, u32[]{:S(2)}, u32[]{:S(2)}) async-start(f32[8,2,16,128]{3,2,1,0:T(8,128)} %get-tuple-element.21), calls=%async_computation.1 | async-start | bytes 262144 | tf_op jit(solution)/shard_map/all_to_all | solution.py:355
  86.9 5.0 %collective-permute-start.5 = (f32[8,128]{1,0:T(8,128)S(1)}, f32[8,128]{1,0:T(8,128)S(1)}, u32[]{:S(2)}, u32[]{:S(2)}) collective-permute-start(f32[8,128]{1,0:T(8,128)S(1)} %get-tuple-element.22.refs_1_), channel_id=1, source_target_pairs={{0,1},{1,0},{2,3},{3,2},{4,5},{5,4},{6,7},{7,6},{8,9},{9,8},{10,11... | collective-permute-start | bytes 12296 | tf_op jit(solution)/shard_map/ppermute | solution.py:362
  97.9 15.1 %all-to-all-start.2 = ((f32[8,16,128]{2,1,0:T(8,128)}), f32[8,16,128]{2,1,0:T(8,128)S(1)}, u32[]{:S(2)}, u32[]{:S(2)}) async-start(f32[8,16,128]{2,1,0:T(8,128)} %get-tuple-element.23), calls=%async_computation.2 | async-start | bytes 131072 | tf_op jit(solution)/shard_map/all_to_all | solution.py:355
  103.2 5.8 %collective-permute-start.6 = (f32[8,128]{1,0:T(8,128)S(1)}, f32[8,128]{1,0:T(8,128)S(1)}, u32[]{:S(2)}, u32[]{:S(2)}) collective-permute-start(f32[8,128]{1,0:T(8,128)S(1)} %get-tuple-element.24.refs_1_), channel_id=1, source_target_pairs={{0,2},{2,0},{1,3},{3,1},{4,6},{6,4},{5,7},{7,5},{8,10},{10,8},{9,1... | collective-permute-start | bytes 12296 | tf_op jit(solution)/shard_map/ppermute | solution.py:368

commit v3 on v2

--- a/solution.py
+++ b/solution.py
@@ -20,6 +20,8 @@
 PLANE = 8
 ROWS = 36
 SCATTERS = 2
+LOADS = 8
+GRANT = 63_800_000
 f32, bf16, i32 = jnp.float32, jnp.bfloat16, jnp.int32
 
 
@@ -55,106 +57,125 @@
         step(pl.ds(high - rest, rest))
 
 
-def gather_kernel(rec, elec, pot, guess, cond, out):
+def gather_kernel(elec, rec_in, pot_in, guess, cond, out, rec, pot, sems):
     gx, gy = lax.axis_index("gx"), lax.axis_index("gy")
     base = jnp.where(gx == 0, WX - HALO, 0)
-    for k in range(HALO):
-        for half in range(2):
-            out[2 * k + half] = guess[base + k, 8 * half : 8 * half + 8]
-            out[10 + 2 * k + half] = cond[base + k, 8 * half : 8 * half + 8]
-    face = jnp.where(gx == 0, WX - 1, 0)
-    out[20] = pot[face, 0:8]
-    out[21] = pot[face, 8:16]
+    step = WX // LOADS
+    pairs = [(rec_in, rec)]
+    for k in range(LOADS):
+        pairs.append((pot_in.at[pl.ds(k * step, step)], pot.at[pl.ds(k * step, step)]))
+    pairs.append((guess.at[pl.ds(base, HALO)], out.at[pl.ds(0, HALO)]))
+    pairs.append((cond.at[pl.ds(base, HALO)], out.at[pl.ds(HALO, HALO)]))
+    loads = [
+        pltpu.make_async_copy(source, target, sems.at[k])
+        for k, (source, target) in enumerate(pairs)
+    ]
+    for load in loads:
+        load.start()
+    loads[0].wait()
     lx = rec[0:1, :] - gx * WX
     ly = rec[1:2, :] - gy * WY
     inside = (lx >= 0) & (lx < WX) & (ly >= 0) & (ly < WY)
     row = jnp.where(inside, lx * WY + ly, -1)
     hot = jnp.where(lax.broadcasted_iota(i32, (WX * WY, NREC), 0) == row, 1.0, 0.0).astype(bf16)
+    for load in loads[1:]:
+        load.wait()
     turned = jnp.transpose(pot[...].reshape(WX * WY, DEPTH))
     parts = [jnp.dot(part, hot, preferred_element_type=f32) for part in split3(turned)]
     values = parts[0] + (parts[1] + parts[2])
     level = lax.broadcasted_iota(i32, (DEPTH, NREC), 0) == rec[2:3, :]
     picked = jnp.sum(jnp.where(level, values, 0.0), axis=0, keepdims=True)
     for k in range(NREC // DEPTH):
-        out[22, k : k + 1, :] = picked[:, DEPTH * k : DEPTH * (k + 1)]
+        out[2 * HALO + 1, k : k + 1, :] = picked[:, DEPTH * k : DEPTH * (k + 1)]
     ex = elec[0, 0] - gx * WX
-    ey = elec[1, 0] - gy * WY
+    ey = elec[0, 1] - gy * WY
     held = (ex >= 0) & (ex < WX) & (ey >= 0) & (ey < WY)
     cx = jnp.clip(ex, 0, WX - 1)
     cy = jnp.clip(ey, 0, WY - 1)
     plane = pot[cx]
     here = (lax.broadcasted_iota(i32, (WY, DEPTH), 0) == cy) & (
-        lax.broadcasted_iota(i32, (WY, DEPTH), 1) == elec[2, 0]
+        lax.broadcasted_iota(i32, (WY, DEPTH), 1) == elec[0, 2]
     )
     there = jnp.sum(jnp.where(here & held, plane, 0.0), axis=0, keepdims=True)
-    out[22, 4:5, :] = jnp.broadcast_to(jnp.sum(there, axis=1, keepdims=True), (1, DEPTH))
-    out[22, 5:8, :] = jnp.zeros((3, DEPTH), f32)
+    value = jnp.sum(there, axis=1, keepdims=True)
+    out[2 * HALO + 1, 4:5, :] = jnp.broadcast_to(value, (1, DEPTH))
+    out[2 * HALO + 1, 5:16, :] = jnp.zeros((11, DEPTH), f32)
+    out[2 * HALO] = pot[jnp.where(gx == 0, WX - 1, 0)]
+
+
+def spare(n):
+    return WX // 2 + n // 3, n % 3
 
 
 def pack_kernel(mine, theirs, pot, guess, cond, up, down, partial):
-    sub = lax.broadcasted_iota(i32, (8, DEPTH), 0)
-
-    def step(i, _):
-        up[i, 0] = jnp.where(sub < 3, pltpu.roll(pot[i, 8:16], 1, 0), guess[i, 8:16])
-        up[i, 1] = cond[i, 8:16]
-        down[i, 0] = jnp.where(sub >= 5, pltpu.roll(pot[i, 0:8], 7, 0), guess[i, 0:8])
-        down[i, 1] = cond[i, 0:8]
-        return 0
-
-    lax.fori_loop(0, WX, step, 0, unroll=4)
-    for k in range(HALO):
-        down[WX + k, 0] = theirs[2 * k]
-        down[WX + k, 1] = theirs[10 + 2 * k]
-        up[WX + k, 0] = theirs[2 * k + 1]
-        up[WX + k, 1] = theirs[10 + 2 * k + 1]
-    total = mine[22] + theirs[22]
-    up[WX + HALO, 0] = total
-    up[WX + HALO, 1] = total
-    down[WX + HALO, 0] = total
-    down[WX + HALO, 1] = total
+    sub = lax.broadcasted_iota(i32, (1, 8, DEPTH), 1)
+    own = slice(0, WX // 2)
+    for out, span, keep, turn in ((up, slice(8, 16), sub >= 3, 3), (down, slice(0, 8), sub < 5, 7)):
+        g, p, c = (ref[:, span].reshape(WX // 2, 2, 8, DEPTH) for ref in (guess, pot, cond))
+        at_pot = sub == (2 if turn == 3 else 7)
+        roll = lambda value, by: pltpu.roll(value, by, 1)
+        rest = jnp.where(at_pot, roll(p[:, 0], turn), roll(c[:, 1], 2))
+        out[own, 0] = jnp.where(keep, g[:, 0], roll(c[:, 1], 5))
+        out[own, 1] = jnp.where(keep, g[:, 1], rest)
+        out[own, 2] = jnp.where(keep, c[:, 0], roll(p[:, 1], turn))
+    total = mine[2 * HALO + 1, 0:8] + theirs[2 * HALO + 1, 0:8]
+    for n in range(2 * HALO):
+        down[spare(n)] = theirs[n, 0:8]
+        up[spare(n)] = theirs[n, 8:16]
+    for n in range(2 * HALO, 12):
+        up[spare(n)] = total
+        down[spare(n)] = total
     partial[...] = total
 
 
 def smooth_kernel(
     rec, elec, obs, pot, guess, cond, across, from_low, from_high, own_sum, far_sum,
     adjoint, term, squares,
-    c, v, r, d0, d1, fx, fy, fz, diag, inv, phi,
+    c, v, r, d0, d1, fx, fy, fz, diag, inv, phi, final, sem,
 ):
     gx, gy = lax.axis_index("gx"), lax.axis_index("gy")
     sub = lax.broadcasted_iota(i32, (8, DEPTH), 0)
     low_on, high_on = (gy > 0), (gy < lax.axis_size("gy") - 1)
     low_keep, high_keep = low_on & (sub >= 3), high_on & (sub < 5)
-
-    def lay(i, source):
-        tile = from_low[source, 0]
-        v[i, 0:8] = jnp.where(low_keep, tile, 0.0)
-        phi[i, 0:8] = jnp.where(low_on & (sub == 7), pltpu.roll(tile, 7, 0), 0.0)
-        c[i, 0:8] = jnp.where(low_keep, from_low[source, 1], 0.0)
-        tile = from_high[source, 0]
-        v[i, 24:32] = jnp.where(high_keep, tile, 0.0)
-        phi[i, 24:32] = jnp.where(high_on & (sub == 0), pltpu.roll(tile, 1, 0), 0.0)
-        c[i, 24:32] = jnp.where(high_keep, from_high[source, 1], 0.0)
+    roll = lambda value, by: pltpu.roll(value, by, 0)
 
     def own(i, _):
-        lay(i + HALO, i)
-        v[i + HALO, 8:24] = guess[i]
-        phi[i + HALO, 8:24] = pot[i]
-        c[i + HALO, 8:24] = cond[i]
+        x = 2 * i + HALO
+        first, second, third = from_low[i, 0], from_low[i, 1], from_low[i, 2]
+        mixed = jnp.where(sub >= 6, roll(second, 6), roll(first, 3))
+        v[x, 0:8] = jnp.where(low_keep, first, 0.0)
+        v[x + 1, 0:8] = jnp.where(low_keep, second, 0.0)
+        c[x, 0:8] = jnp.where(low_keep, third, 0.0)
+        c[x + 1, 0:8] = jnp.where(low_keep, mixed, 0.0)
+        phi[x, 0:8] = jnp.where(low_keep, roll(second, 5), 0.0)
+        phi[x + 1, 0:8] = jnp.where(low_keep, roll(third, 5), 0.0)
+        first, second, third = from_high[i, 0], from_high[i, 1], from_high[i, 2]
+        mixed = jnp.where(sub < 3, roll(first, 3), roll(second, 6))
+        v[x, 24:32] = jnp.where(high_keep, first, 0.0)
+        v[x + 1, 24:32] = jnp.where(high_keep, second, 0.0)
+        c[x, 24:32] = jnp.where(high_keep, third, 0.0)
+        c[x + 1, 24:32] = jnp.where(high_keep, mixed, 0.0)
+        phi[x, 24:32] = jnp.where(high_keep, roll(second, 1), 0.0)
+        phi[x + 1, 24:32] = jnp.where(high_keep, roll(third, 1), 0.0)
+        for k in range(2):
+            v[x + k, 8:24] = guess[2 * i + k]
+            phi[x + k, 8:24] = pot[2 * i + k]
+            c[x + k, 8:24] = cond[2 * i + k]
         return 0
 
-    lax.fori_loop(0, WX, own, 0, unroll=2)
+    lax.fori_loop(0, WX // 2, own, 0, unroll=2)
     blank = jnp.zeros((EY, DEPTH), f32)
     empty = jnp.where(gx == 0, 0, WX + HALO)
     there = jnp.where(gx == 0, WX + HALO, 0)
     for k in range(HALO):
         for ref in (v, phi, c):
             ref[empty + k] = blank
-        lay(there + k, WX + k)
-        for half in range(2):
-            span = slice(8 + 8 * half, 16 + 8 * half)
-            v[there + k, span] = across[2 * k + half]
-            c[there + k, span] = across[10 + 2 * k + half]
-            phi[there + k, span] = across[20 + half]
+        for ref, n in ((v, k), (c, HALO + k)):
+            ref[there + k, 0:8] = jnp.where(low_keep, from_low[spare(n)], 0.0)
+            ref[there + k, 8:24] = across[n]
+            ref[there + k, 24:32] = jnp.where(high_keep, from_high[spare(n)], 0.0)
+        phi[there + k] = blank
+    phi[jnp.where(gx == 0, WX + HALO, HALO - 1), 8:24] = across[2 * HALO]
 
     lane = lax.broadcasted_iota(i32, (1, EY, DEPTH), 2)
     last, first = lane == DEPTH - 1, lane == 0
@@ -180,7 +201,7 @@
     ly = rec[1:2, :] - gy * WY + 8
     near = (lx >= 0) & (lx < EX) & (ly >= 0) & (ly < EY)
     row = jnp.where(near, lx * EY + ly, -1)
-    total = own_sum[...] + far_sum[...] + from_low[WX + HALO, 0] + from_high[WX + HALO, 0]
+    total = own_sum[...] + far_sum[...] + from_low[spare(2 * HALO)] + from_high[spare(2 * HALO)]
     anchor = total[4:5, :]
     pieces = [
         total[k : k + 1, :] - anchor - obs[:, DEPTH * k : DEPTH * (k + 1)]
@@ -201,12 +222,12 @@
         r[k * span : (k + 1) * span] = placed.reshape(span, EY, DEPTH)
 
     ex = elec[0, 0] - gx * WX + HALO
-    ey = elec[1, 0] - gy * WY + 8
+    ey = elec[0, 1] - gy * WY + 8
     held = (ex >= 0) & (ex < EX) & (ey >= 0) & (ey < EY)
     cx = jnp.clip(ex, 0, EX - 1)
     spot = (
         (lax.broadcasted_iota(i32, (EY, DEPTH), 0) == ey)
-        & (lax.broadcasted_iota(i32, (EY, DEPTH), 1) == elec[2, 0])
+        & (lax.broadcasted_iota(i32, (EY, DEPTH), 1) == elec[0, 2])
         & held
     )
     r[cx] = r[cx] - jnp.where(spot, whole, 0.0)
@@ -252,12 +273,14 @@
         left = r[i] - applied(source, i)
         new = v[i] + here
         v[i] = new
-        adjoint[shifted(i)] = new[:, 8:24]
+        final[shifted(i)] = new[:, 8:24]
         left = left[:, 8:24]
         left = left * left
         squares[...] += jnp.sum(left[:, :8] + left[:, 8:], axis=0)
 
     over_rows(HALO, WX + HALO, finish)
+    store = pltpu.make_async_copy(final, adjoint, sem)
+    store.start()
 
     def product(i):
         a, p = v[i], phi[i]
@@ -271,6 +294,7 @@
         term[shifted(i)] = -0.5 * out[:, 8:24]
 
     over_rows(HALO, WX + HALO, product)
+    store.wait()
 
 
 def plane_kernel(parts, own, got, out, acc):
@@ -286,7 +310,7 @@
     acc[...] = own[...] + got[...]
 
 
-def scale_kernel(sources, parts, own, got, out, acc):
+def scale_kernel(sources, parts, out):
     total, square = parts[0, 0], parts[0, 1]
     for q in range(1, LINE):
         total = total + parts[q, 0]
@@ -294,13 +318,16 @@
     value = total * lax.rsqrt(square / sources + 1.0)
     for q in range(LINE):
         out[q] = value
-    acc[...] = own[...] + got[...]
-
-
-def spread_kernel(cells, rows, own, got, out, rms):
+
+
+def spread_kernel(rows, own, got, out, acc):
     value = rows[...]
     for k in range(PLANE):
         out[k] = value
+    acc[...] = own[...] + got[...]
+
+
+def rms_kernel(cells, own, got, rms):
     total = jnp.sum(own[...] + got[...], axis=0, keepdims=True)
     rms[...] = jnp.broadcast_to(
         jnp.sqrt(jnp.sum(total, axis=1, keepdims=True) / cells), (1, DEPTH)
@@ -309,31 +336,38 @@
 
 VM = pl.BlockSpec(memory_space=pltpu.VMEM)
 SM = pl.BlockSpec(memory_space=pltpu.SMEM)
-
-
-def call(kernel, shapes, specs, *args, scratch=(), flops=0, moved=0):
+HB = pl.BlockSpec(memory_space=pl.ANY)
+
+
+def call(kernel, shapes, specs, *args, scratch=(), limit=48 * 1024 * 1024, outs=None):
     return pl.pallas_call(
         kernel,
         out_shape=[jax.ShapeDtypeStruct(shape, f32) for shape in shapes],
         in_specs=specs,
-        out_specs=[VM] * len(shapes),
+        out_specs=outs or [VM] * len(shapes),
         scratch_shapes=list(scratch),
-        compiler_params=pltpu.CompilerParams(vmem_limit_bytes=48 * 1024 * 1024),
-        cost_estimate=pl.CostEstimate(flops=flops, bytes_accessed=moved, transcendentals=0),
+        compiler_params=pltpu.CompilerParams(vmem_limit_bytes=limit),
     )(*args)
 
 
 def body(conductivity, potential, adjoint_guess, observed, receiver_cells, electrodes):
     sources = lax.axis_size("src")
     pot, guess = potential[0], adjoint_guess[0]
+    elec = jnp.transpose(electrodes)
     tile = (8, DEPTH)
     swap_x = [(0, 1), (1, 0)]
     (mine,) = call(
-        gather_kernel, [(23, 8, DEPTH)], [VM, SM, VM, VM, VM],
-        receiver_cells, electrodes, pot, guess, conductivity,
+        gather_kernel, [(2 * HALO + 2, WY, DEPTH)], [SM, HB, HB, HB, HB],
+        elec, receiver_cells, pot, guess, conductivity,
+        scratch=[
+            pltpu.VMEM((3, NREC), i32),
+            pltpu.VMEM((WX, WY, DEPTH), f32),
+            pltpu.SemaphoreType.DMA((3 + LOADS,)),
+        ],
+        limit=GRANT,
     )
     theirs = lax.ppermute(mine, "gx", swap_x)
-    faces = (WX + HALO + 1, 2, 8, DEPTH)
+    faces = (WX // 2 + 4, 3, 8, DEPTH)
     up, down, partial = call(
         pack_kernel, [faces, faces, tile], [VM] * 5, mine, theirs, pot, guess, conductivity
     )
@@ -344,9 +378,11 @@
     block = (WX, WY, DEPTH)
     adjoint, term, squares = call(
         smooth_kernel, [block, block, tile], [VM, SM] + [VM] * 9,
-        receiver_cells, electrodes, observed, pot, guess, conductivity,
+        receiver_cells, elec, observed, pot, guess, conductivity,
         theirs, from_low, from_high, partial, far,
-        scratch=[pltpu.VMEM((EX, EY, DEPTH), f32)] * 11,
+        scratch=[pltpu.VMEM((EX, EY, DEPTH), f32)] * 11
+        + [pltpu.VMEM(block, f32), pltpu.SemaphoreType.DMA],
+        outs=[HB, VM, VM],
     )
     planes = [[z * PLANE + k for k in range(PLANE)] for z in range(LINE)]
     lines = [[z * PLANE + k for z in range(LINE)] for k in range(PLANE)]
@@ -359,20 +395,21 @@
     sums, squares = call(
         plane_kernel, [(LINE, 2, WY, DEPTH), tile], [VM] * 3, got, squares, other
     )
+    got = exchange(sums, lines)
+    (scaled,) = call(
+        lambda *refs: scale_kernel(sources, *refs), [(LINE, WY, DEPTH)], [VM], got
+    )
     other = lax.ppermute(squares, "gy", [(0, 1), (1, 0), (2, 3), (3, 2)])
-    got = exchange(sums, lines)
-    scaled, squares = call(
-        lambda *refs: scale_kernel(sources, *refs),
-        [(LINE, WY, DEPTH), tile], [VM] * 3, got, squares, other,
+    got = exchange(scaled, lines)
+    spread, squares = call(
+        spread_kernel, [(PLANE, LINE, WY, DEPTH), tile], [VM] * 3, got, squares, other
     )
     other = lax.ppermute(squares, "gy", [(0, 2), (2, 0), (1, 3), (3, 1)])
-    got = exchange(scaled, lines)
+    gradient = exchange(spread, planes).reshape(block)
     cells = WX * lax.axis_size("gx") * WY * lax.axis_size("gy") * DEPTH
-    spread, rms = call(
-        lambda *refs: spread_kernel(cells, *refs),
-        [(PLANE, LINE, WY, DEPTH), (1, DEPTH)], [VM] * 3, got, squares, other,
-    )
-    gradient = exchange(spread, planes).reshape(block)
+    (rms,) = call(
+        lambda *refs: rms_kernel(cells, *refs), [(1, DEPTH)], [VM] * 2, squares, other
+    )
     return adjoint[None], rms[0, :1], gradient
 
 

time: 132 us -> 127 us (0.962)
  blocking collectives: 16.7 us -> 23.7 us
  starting transfers between devices: 73 us -> 66.9 us
  waiting for transfers between devices: 22.2 us -> 18.3 us
  local copies, waits for them, and re-layouts: 5.37 us -> 1.71 us
  Pallas kernels: 13 us -> 15.1 us
    all_to_all x1, blocking collectives: 16.7 us -> 23.7 us  [exchange(): lax.all_to_all(value, 'src', 0, 0, axis_index_groups=groups, tiled=True)]
    all_to_all x3, starting transfers between devices: 26.2 us -> 20 us  [exchange(): lax.all_to_all(value, 'src', 0, 0, axis_index_groups=groups, tiled=True)]
    unnamed x18 -> x15, local copies, waits for them, and re-layouts: 5.37 us -> 1.71 us
    ppermute x1, waiting for transfers between devices: 6.96 us -> 4.14 us  [body(): far = lax.ppermute(partial, 'gy', ring(2))]
    pallas_call x6 -> x7, Pallas kernels: 13 us -> 15.1 us  [call(): pl.pallas_call(kernel, out_shape=[jax.ShapeDtypeStruct(shape, f32) for sh...]
    all_to_all x3, waiting for transfers between devices: 9.23 us -> 7.72 us  [exchange(): lax.all_to_all(value, 'src', 0, 0, axis_index_groups=groups, tiled=True)]
where the time goes in v3:
time: 127 us
  starting transfers between devices  66.9 us (53%)
  blocking collectives  23.7 us (19%)
  waiting for transfers between devices  18.3 us (14%)
  Pallas kernels  15.1 us (12%)
  local copies, waits for them, and re-layouts  1.71 us (1%)
    all_to_all x1, blocking collectives, exchange(): lax.all_to_all(value, 'src', 0, 0, axis_index_groups=groups, tiled=True)  23.7 us
    all_to_all x3, starting transfers between devices, exchange(): lax.all_to_all(value, 'src', 0, 0, axis_index_groups=groups, tiled=True)  20 us
    ppermute x1, starting transfers between devices, body(): theirs = lax.ppermute(mine, 'gx', swap_x)  16.3 us
    pallas_call x7, Pallas kernels, call(): pl.pallas_call(kernel, out_shape=[jax.ShapeDtypeStruct(shape, f32) for sh...  15.1 us
    ppermute x1, starting transfers between devices, body(): other = lax.ppermute(squares, 'gx', swap_x)  11.8 us
    all_to_all x3, waiting for transfers between devices, exchange(): lax.all_to_all(value, 'src', 0, 0, axis_index_groups=groups, tiled=True)  7.72 us
    ppermute x1, starting transfers between devices, body(): other = lax.ppermute(squares, 'gy', [(0, 2), (2, 0), (1, 3), (3, 1)])  4.52 us
    ppermute x1, waiting for transfers between devices, body(): far = lax.ppermute(partial, 'gy', ring(2))  4.14 us
  transfers between devices with their start and end apart: 10, of which 8 were waited for; matrix products, arithmetic and copies ran while one was open for 0% of the time, Pallas kernels for 0%

profile of v3, /device:TPU:1, one launch (start us, length us, event | category | flops | bytes accessed | tf_op | source)
XLA Modules:
  0.0 126.5 jit_solution(8781954567398082113)
XLA Ops:
  0.7 3.3 %shard_map.85.mine = f32[12,16,128]{2,1,0:T(8,128)} custom-call(s32[1,3]{1,0:T(1,128)} %bitcast.14, s32[3,512]{1,0:T(4,128)} %rec.1, f32[64,16,128]{2,1,0:T(8,128)} %bitcast.8, f32[64,16,128]{2,1,0:T(8,128)} %bitcast.11, f32[64,16,128]{2,1,0:T(8,128)} %cond.5), custom_call_target="tpu_custom_call" | custom-call | tf_op jit(solution)/shard_map/pallas_call | solution.py:343
  4.0 16.3 %collective-permute-start = (f32[12,16,128]{2,1,0:T(8,128)}, f32[12,16,128]{2,1,0:T(8,128)S(1)}, u32[]{:S(2)}, u32[]{:S(2)}) collective-permute-start(f32[12,16,128]{2,1,0:T(8,128)} %shard_map.85.mine), channel_id=1, source_target_pairs={{0,4},{4,0},{1,5},{5,1},{2,6},{6,2},{3,7},{7,3},{8,12},{12,8},{9,1... | collective-permute-start | bytes 294920 | tf_op jit(solution)/shard_map/ppermute | solution.py:369
  20.2 2.5 %collective-permute-done.theirs.across = f32[12,16,128]{2,1,0:T(8,128)S(1)} collective-permute-done((f32[12,16,128]{2,1,0:T(8,128)}, f32[12,16,128]{2,1,0:T(8,128)S(1)}, u32[]{:S(2)}, u32[]{:S(2)}) %collective-permute-start) | collective-permute-done | bytes 98336 | tf_op jit(solution)/shard_map/ppermute | solution.py:369
  22.8 0.0 copy-start.3
  22.8 0.9 copy-done.3
  23.7 0.1 shard_map.86
  23.8 0.0 copy-start.5
  23.8 3.4 %collective-permute-start.1 = (f32[36,3,8,128]{3,2,1,0:T(8,128)S(1)}, f32[36,3,8,128]{3,2,1,0:T(8,128)S(1)}, u32[]{:S(2)}, u32[]{:S(2)}) collective-permute-start(f32[36,3,8,128]{3,2,1,0:T(8,128)S(1)} %get-tuple-element.13), channel_id=1, source_target_pairs={{0,1},{1,2},{2,3},{3,0},{4,5},{5,6},{6,7},{7,4},{8,9},{9,10},{10,1... | collective-permute-start | bytes 1327112 | tf_op jit(solution)/shard_map/ppermute | solution.py:375
  27.2 0.0 copy-start.6
  27.2 3.4 %collective-permute-start.2 = (f32[36,3,8,128]{3,2,1,0:T(8,128)S(1)}, f32[36,3,8,128]{3,2,1,0:T(8,128)S(1)}, u32[]{:S(2)}, u32[]{:S(2)}) collective-permute-start(f32[36,3,8,128]{3,2,1,0:T(8,128)S(1)} %get-tuple-element.14), channel_id=1, source_target_pairs={{0,3},{1,0},{2,1},{3,2},{4,7},{5,4},{6,5},{7,6},{8,11},{9,8},{10,9... | collective-permute-start | bytes 1327112 | tf_op jit(solution)/shard_map/ppermute | solution.py:376
  30.6 3.5 %collective-permute-start.3 = (f32[8,128]{1,0:T(8,128)S(1)}, f32[8,128]{1,0:T(8,128)S(1)}, u32[]{:S(2)}, u32[]{:S(2)}) collective-permute-start(f32[8,128]{1,0:T(8,128)S(1)} %get-tuple-element.15.own_sum), channel_id=1, source_target_pairs={{0,2},{1,3},{2,0},{3,1},{4,6},{5,7},{6,4},{7,5},{8,10},{9,11},{10,... | collective-permute-start | bytes 12296 | tf_op jit(solution)/shard_map/ppermute | solution.py:377
  34.2 4.1 %collective-permute-done.3.far_sum = f32[8,128]{1,0:T(8,128)S(1)} collective-permute-done((f32[8,128]{1,0:T(8,128)S(1)}, f32[8,128]{1,0:T(8,128)S(1)}, u32[]{:S(2)}, u32[]{:S(2)}) %collective-permute-start.3) | collective-permute-done | bytes 4128 | tf_op jit(solution)/shard_map/ppermute | solution.py:377
  38.3 0.0 collective-permute-done.1.from_low
  38.3 0.3 collective-permute-done.2.from_high
  38.6 9.6 %shard_map.87 = (f32[64,16,128]{2,1,0:T(8,128)}, f32[64,16,128]{2,1,0:T(8,128)}, f32[8,128]{1,0:T(8,128)S(1)}) custom-call(s32[3,512]{1,0:T(4,128)S(1)} %copy-done.4, s32[1,3]{1,0:T(1,128)S(1)} %bitcast.15, f32[1,512]{1,0:T(1,128)S(1)} %copy-done.5, f32[64,16,128]{2,1,0:T(8,128)S(1)} %bitcast.10, f32[64,16,128]{2,1,0:T(8,128)S(1)} %bitcast.13, ...), custom_call_target="tpu_custom_call" | custom-call | tf_op jit(solution)/shard_map/pallas_call | solution.py:343
  48.2 7.5 %all-to-all-start = ((f32[8,8,16,128]{3,2,1,0:T(8,128)}), f32[8,8,16,128]{3,2,1,0:T(8,128)S(1)}, u32[]{:S(2)}, u32[]{:S(2)}) async-start(f32[8,8,16,128]{3,2,1,0:T(8,128)} %bitcast.4), calls=%async_computation | async-start | bytes 1048576 | tf_op jit(solution)/shard_map/all_to_all | solution.py:391
  55.7 11.8 %collective-permute-start.4 = (f32[8,128]{1,0:T(8,128)S(1)}, f32[8,128]{1,0:T(8,128)S(1)}, u32[]{:S(2)}, u32[]{:S(2)}) collective-permute-start(f32[8,128]{1,0:T(8,128)S(1)} %get-tuple-element.18.own), channel_id=1, source_target_pairs={{0,4},{4,0},{1,5},{5,1},{2,6},{6,2},{3,7},{7,3},{8,12},{12,8},{9,1... | collective-permute-start | bytes 12296 | tf_op jit(solution)/shard_map/ppermute | solution.py:393
  67.5 1.3 %collective-permute-done.4.got = f32[8,128]{1,0:T(8,128)S(1)} collective-permute-done((f32[8,128]{1,0:T(8,128)S(1)}, f32[8,128]{1,0:T(8,128)S(1)}, u32[]{:S(2)}, u32[]{:S(2)}) %collective-permute-start.4) | collective-permute-done | bytes 4128 | tf_op jit(solution)/shard_map/ppermute | solution.py:393
  68.7 0.1 shard_map.88
  68.8 23.7 %all_to_all.20.refs_0_ = f32[8,2,16,128]{3,2,1,0:T(8,128)S(1)} all-to-all(f32[8,2,16,128]{3,2,1,0:T(8,128)S(1)} %get-tuple-element.19), channel_id=1, replica_groups={{0,64,128,192,256,320,384,448},{8,72,136,200,264,328,392,456},{16,80,14..., dimensions={0} | all-to-all | bytes 262144 | tf_op jit(solution)/shard_map/all_to_all | solution.py:391
  92.5 0.7 shard_map.89
  93.2 5.3 %all-to-all-start.2 = ((f32[8,16,128]{2,1,0:T(8,128)}), f32[8,16,128]{2,1,0:T(8,128)S(1)}, u32[]{:S(2)}, u32[]{:S(2)}) async-start(f32[8,16,128]{2,1,0:T(8,128)} %shard_map.89), calls=%async_computation.2 | async-start | bytes 131072 | tf_op jit(solution)/shard_map/all_to_all | solution.py:391
  98.5 4.0 %collective-permute-start.5 = (f32[8,128]{1,0:T(8,128)S(1)}, f32[8,128]{1,0:T(8,128)S(1)}, u32[]{:S(2)}, u32[]{:S(2)}) collective-permute-start(f32[8,128]{1,0:T(8,128)S(1)} %get-tuple-element.20.own), channel_id=1, source_target_pairs={{0,1},{1,0},{2,3},{3,2},{4,5},{5,4},{6,7},{7,6},{8,9},{9,8},{10,11... | collective-permute-start | bytes 12296 | tf_op jit(solution)/shard_map/ppermute | solution.py:402
  102.4 1.1 collective-permute-done.5.got
  103.5 4.7 %all-to-all-done.2.rows = f32[8,16,128]{2,1,0:T(8,128)S(1)} async-done(((f32[8,16,128]{2,1,0:T(8,128)}), f32[8,16,128]{2,1,0:T(8,128)S(1)}, u32[]{:S(2)}, u32[]{:S(2)}) %all-to-all-start.2) | async-done | bytes 65568 | tf_op jit(solution)/shard_map/all_to_all | solution.py:391
  108.2 0.8 shard_map.90
  109.1 7.2 %all-to-all-start.3 = ((f32[8,8,16,128]{3,2,1,0:T(8,128)}), f32[8,8,16,128]{3,2,1,0:T(8,128)S(1)}, u32[]{:S(2)}, u32[]{:S(2)}) async-start(f32[8,8,16,128]{3,2,1,0:T(8,128)} %get-tuple-element.22), calls=%async_computation.3 | async-start | bytes 1048576 | tf_op jit(solution)/shard_map/all_to_all | solution.py:391
  116.3 4.5 %collective-permute-start.6 = (f32[8,128]{1,0:T(8,128)S(1)}, f32[8,128]{1,0:T(8,128)S(1)}, u32[]{:S(2)}, u32[]{:S(2)}) collective-permute-start(f32[8,128]{1,0:T(8,128)S(1)} %get-tuple-element.21.refs_0_), channel_id=1, source_target_pairs={{0,2},{2,0},{1,3},{3,1},{4,6},{6,4},{5,7},{7,5},{8,10},{10,8},{9,1... | collective-permute-start | bytes 12296 | tf_op jit(solution)/shard_map/ppermute | solution.py:407
  120.8 1.3 %collective-permute-done.6.refs_1_ = f32[8,128]{1,0:T(8,128)S(1)} collective-permute-done((f32[8,128]{1,0:T(8,128)S(1)}, f32[8,128]{1,0:T(8,128)S(1)}, u32[]{:S(2)}, u32[]{:S(2)}) %collective-permute-start.6) | collective-permute-done | bytes 4128 | tf_op jit(solution)/shard_map/ppermute | solution.py:407
  122.1 0.6 shard_map.91
  122.7 3.0 %all-to-all-done.3 = f32[8,8,16,128]{3,2,1,0:T(8,128)S(1)} async-done(((f32[8,8,16,128]{3,2,1,0:T(8,128)}), f32[8,8,16,128]{3,2,1,0:T(8,128)S(1)}, u32[]{:S(2)}, u32[]{:S(2)}) %all-to-all-start.3) | async-done | bytes 524320 | tf_op jit(solution)/shard_map/all_to_all | solution.py:391
  125.7 0.8 copy.10
  (11 shorter events, 0.0 us)
Async XLA Ops:
  0.6 22.1 %copy-start = (f32[1,64,16,128]{3,2,1,0:T(8,128)S(1)}, f32[1,64,16,128]{3,2,1,0:T(8,128)}, u32[]{:S(2)}) copy-start(f32[1,64,16,128]{3,2,1,0:T(8,128)} %param.7) | copy-start | bytes 1572868
  0.6 22.1 %copy-start.1 = (f32[1,64,16,128]{3,2,1,0:T(8,128)S(1)}, f32[1,64,16,128]{3,2,1,0:T(8,128)}, u32[]{:S(2)}) copy-start(f32[1,64,16,128]{3,2,1,0:T(8,128)} %param.8) | copy-start | bytes 1572868
  0.7 22.1 %copy-start.2 = (f32[64,16,128]{2,1,0:T(8,128)S(1)}, f32[64,16,128]{2,1,0:T(8,128)}, u32[]{:S(2)}) copy-start(f32[64,16,128]{2,1,0:T(8,128)} %cond.5) | copy-start | bytes 1572868
  4.0 18.8 %collective-permute-start = (f32[12,16,128]{2,1,0:T(8,128)}, f32[12,16,128]{2,1,0:T(8,128)S(1)}, u32[]{:S(2)}, u32[]{:S(2)}) collective-permute-start(f32[12,16,128]{2,1,0:T(8,128)} %shard_map.85.mine), channel_id=1, source_target_pairs={{0,4},{4,0},{1,5},{5,1},{2,6},{6,2},{3,7},{7,3},{8,12},{12,8},{9,1... | collective-permute-start | bytes 294920 | tf_op jit(solution)/shard_map/ppermute | solution.py:369
  22.8 0.9 copy-start.3
  23.7 14.9 %copy-start.4 = (s32[3,512]{1,0:T(4,128)S(1)}, s32[3,512]{1,0:T(4,128)}, u32[]{:S(2)}) copy-start(s32[3,512]{1,0:T(4,128)} %rec.1) | copy-start | bytes 18436
  23.8 14.8 %copy-start.5 = (f32[1,512]{1,0:T(1,128)S(1)}, f32[1,512]{1,0:T(1,128)}, u32[]{:S(2)}) copy-start(f32[1,512]{1,0:T(1,128)} %obs.1) | copy-start | bytes 6148
  23.8 14.5 %collective-permute-start.1 = (f32[36,3,8,128]{3,2,1,0:T(8,128)S(1)}, f32[36,3,8,128]{3,2,1,0:T(8,128)S(1)}, u32[]{:S(2)}, u32[]{:S(2)}) collective-permute-start(f32[36,3,8,128]{3,2,1,0:T(8,128)S(1)} %get-tuple-element.13), channel_id=1, source_target_pairs={{0,1},{1,2},{2,3},{3,0},{4,5},{5,6},{6,7},{7,4},{8,9},{9,10},{10,1... | collective-permute-start | bytes 1327112 | tf_op jit(solution)/shard_map/ppermute | solution.py:375
  27.2 11.3 %copy-start.6 = (s32[3,1]{0,1:T(1,128)S(1)}, s32[3,1]{0,1:T(1,128)}, u32[]{:S(2)}) copy-start(s32[3,1]{0,1:T(1,128)} %param.11) | copy-start | bytes 40
  27.2 11.3 %collective-permute-start.2 = (f32[36,3,8,128]{3,2,1,0:T(8,128)S(1)}, f32[36,3,8,128]{3,2,1,0:T(8,128)S(1)}, u32[]{:S(2)}, u32[]{:S(2)}) collective-permute-start(f32[36,3,8,128]{3,2,1,0:T(8,128)S(1)} %get-tuple-element.14), channel_id=1, source_target_pairs={{0,3},{1,0},{2,1},{3,2},{4,7},{5,4},{6,5},{7,6},{8,11},{9,8},{10,9... | collective-permute-start | bytes 1327112 | tf_op jit(solution)/shard_map/ppermute | solution.py:376
  30.6 7.7 %collective-permute-start.3 = (f32[8,128]{1,0:T(8,128)S(1)}, f32[8,128]{1,0:T(8,128)S(1)}, u32[]{:S(2)}, u32[]{:S(2)}) collective-permute-start(f32[8,128]{1,0:T(8,128)S(1)} %get-tuple-element.15.own_sum), channel_id=1, source_target_pairs={{0,2},{1,3},{2,0},{3,1},{4,6},{5,7},{6,4},{7,5},{8,10},{9,11},{10,... | collective-permute-start | bytes 12296 | tf_op jit(solution)/shard_map/ppermute | solution.py:377
  48.2 20.6 %all-to-all-start = ((f32[8,8,16,128]{3,2,1,0:T(8,128)}), f32[8,8,16,128]{3,2,1,0:T(8,128)S(1)}, u32[]{:S(2)}, u32[]{:S(2)}) async-start(f32[8,8,16,128]{3,2,1,0:T(8,128)} %bitcast.4), calls=%async_computation | async-start | bytes 1048576 | tf_op jit(solution)/shard_map/all_to_all | solution.py:391
  55.7 13.1 %collective-permute-start.4 = (f32[8,128]{1,0:T(8,128)S(1)}, f32[8,128]{1,0:T(8,128)S(1)}, u32[]{:S(2)}, u32[]{:S(2)}) collective-permute-start(f32[8,128]{1,0:T(8,128)S(1)} %get-tuple-element.18.own), channel_id=1, source_target_pairs={{0,4},{4,0},{1,5},{5,1},{2,6},{6,2},{3,7},{7,3},{8,12},{12,8},{9,1... | collective-permute-start | bytes 12296 | tf_op jit(solution)/shard_map/ppermute | solution.py:393
  93.2 15.1 %all-to-all-start.2 = ((f32[8,16,128]{2,1,0:T(8,128)}), f32[8,16,128]{2,1,0:T(8,128)S(1)}, u32[]{:S(2)}, u32[]{:S(2)}) async-start(f32[8,16,128]{2,1,0:T(8,128)} %shard_map.89), calls=%async_computation.2 | async-start | bytes 131072 | tf_op jit(solution)/shard_map/all_to_all | solution.py:391
  98.5 5.1 %collective-permute-start.5 = (f32[8,128]{1,0:T(8,128)S(1)}, f32[8,128]{1,0:T(8,128)S(1)}, u32[]{:S(2)}, u32[]{:S(2)}) collective-permute-start(f32[8,128]{1,0:T(8,128)S(1)} %get-tuple-element.20.own), channel_id=1, source_target_pairs={{0,1},{1,0},{2,3},{3,2},{4,5},{5,4},{6,7},{7,6},{8,9},{9,8},{10,11... | collective-permute-start | bytes 12296 | tf_op jit(solution)/shard_map/ppermute | solution.py:402
  109.1 16.7 %all-to-all-start.3 = ((f32[8,8,16,128]{3,2,1,0:T(8,128)}), f32[8,8,16,128]{3,2,1,0:T(8,128)S(1)}, u32[]{:S(2)}, u32[]{:S(2)}) async-start(f32[8,8,16,128]{3,2,1,0:T(8,128)} %get-tuple-element.22), calls=%async_computation.3 | async-start | bytes 1048576 | tf_op jit(solution)/shard_map/all_to_all | solution.py:391
  116.3 5.8 %collective-permute-start.6 = (f32[8,128]{1,0:T(8,128)S(1)}, f32[8,128]{1,0:T(8,128)S(1)}, u32[]{:S(2)}, u32[]{:S(2)}) collective-permute-start(f32[8,128]{1,0:T(8,128)S(1)} %get-tuple-element.21.refs_0_), channel_id=1, source_target_pairs={{0,2},{2,0},{1,3},{3,1},{4,6},{6,4},{5,7},{7,5},{8,10},{10,8},{9,1... | collective-permute-start | bytes 12296 | tf_op jit(solution)/shard_map/ppermute | solution.py:407

commit v4 on v3

--- a/solution.py
+++ b/solution.py
@@ -55,6 +55,44 @@
     lax.fori_loop(0, count, turn, 0)
     if rest:
         step(pl.ds(high - rest, rest))
+
+
+def sides(gy):
+    return gy > 0, gy < lax.axis_size("gy") - 1
+
+
+def corner(near, low):
+    sub = lax.broadcasted_iota(i32, (8, DEPTH), 0)
+    tiles = []
+    for n in range(2):
+        if low:
+            second = jnp.where(sub == 0, pltpu.roll(near(n, 4), 1, 0), pltpu.roll(near(n, 2), 4, 0))
+            tiles.append(jnp.where(sub >= 4, near(n, 1), second))
+        else:
+            second = jnp.where(sub == 7, pltpu.roll(near(n, 4), 7, 0), pltpu.roll(near(n, 2), 4, 0))
+            tiles.append(jnp.where(sub < 4, near(n, 1), second))
+    if low:
+        tiles.append(jnp.where(sub >= 6, near(0, 3), pltpu.roll(near(1, 3), 6, 0)))
+    else:
+        tiles.append(jnp.where(sub < 2, near(0, 3), pltpu.roll(near(1, 3), 2, 0)))
+    return tiles
+
+
+def uncorner(tiles, low):
+    sub = lax.broadcasted_iota(i32, (8, DEPTH), 0)
+    out = {}
+    for n in range(2):
+        if low:
+            out[n, 1] = jnp.where(sub >= 4, tiles[n], 0.0)
+            out[n, 2] = jnp.where(sub >= 5, pltpu.roll(tiles[n], 4, 0), 0.0)
+            out[n, 3] = jnp.where(sub >= 6, pltpu.roll(tiles[2], 2 * n, 0) if n else tiles[2], 0.0)
+            out[n, 4] = jnp.where(sub == 7, pltpu.roll(tiles[n], 7, 0), 0.0)
+        else:
+            out[n, 1] = jnp.where(sub < 4, tiles[n], 0.0)
+            out[n, 2] = jnp.where(sub < 3, pltpu.roll(tiles[n], 4, 0), 0.0)
+            out[n, 3] = jnp.where(sub < 2, pltpu.roll(tiles[2], 6, 0) if n else tiles[2], 0.0)
+            out[n, 4] = jnp.where(sub == 0, pltpu.roll(tiles[n], 1, 0), 0.0)
+    return out
 
 
 def gather_kernel(elec, rec_in, pot_in, guess, cond, out, rec, pot, sems):
@@ -103,33 +141,42 @@
     out[2 * HALO] = pot[jnp.where(gx == 0, WX - 1, 0)]
 
 
-def spare(n):
-    return WX // 2 + n // 3, n % 3
-
-
-def pack_kernel(mine, theirs, pot, guess, cond, up, down, partial):
+def pack_kernel(mine, pot, guess, cond, up, down, partial, sem):
+    load = pltpu.make_async_copy(mine.at[2 * HALO + 1, pl.ds(0, 8)], partial, sem)
+    load.start()
     sub = lax.broadcasted_iota(i32, (1, 8, DEPTH), 1)
-    own = slice(0, WX // 2)
     for out, span, keep, turn in ((up, slice(8, 16), sub >= 3, 3), (down, slice(0, 8), sub < 5, 7)):
         g, p, c = (ref[:, span].reshape(WX // 2, 2, 8, DEPTH) for ref in (guess, pot, cond))
         at_pot = sub == (2 if turn == 3 else 7)
         roll = lambda value, by: pltpu.roll(value, by, 1)
         rest = jnp.where(at_pot, roll(p[:, 0], turn), roll(c[:, 1], 2))
-        out[own, 0] = jnp.where(keep, g[:, 0], roll(c[:, 1], 5))
-        out[own, 1] = jnp.where(keep, g[:, 1], rest)
-        out[own, 2] = jnp.where(keep, c[:, 0], roll(p[:, 1], turn))
-    total = mine[2 * HALO + 1, 0:8] + theirs[2 * HALO + 1, 0:8]
-    for n in range(2 * HALO):
-        down[spare(n)] = theirs[n, 0:8]
-        up[spare(n)] = theirs[n, 8:16]
-    for n in range(2 * HALO, 12):
-        up[spare(n)] = total
-        down[spare(n)] = total
-    partial[...] = total
+        out[:, 0] = jnp.where(keep, g[:, 0], roll(c[:, 1], 5))
+        out[:, 1] = jnp.where(keep, g[:, 1], rest)
+        out[:, 2] = jnp.where(keep, c[:, 0], roll(p[:, 1], turn))
+    load.wait()
+
+
+def corner_kernel(own, theirs, spots):
+    gx, gy = lax.axis_index("gx"), lax.axis_index("gy")
+
+    def near(half):
+        def tile(n, k):
+            x = n * HALO + jnp.where(gx == 0, k - 1, HALO - k)
+            return theirs[x, 8 * half : 8 * half + 8]
+
+        return tile
+
+    count = spots.shape[0]
+    total = own[...] + theirs[2 * HALO + 1, 0:8]
+    high, low = corner(near(1), True), corner(near(0), False)
+    for j in range(count):
+        for k in range(3):
+            spots[j, k] = jnp.where(j > gy, high[k], low[k])
+        spots[j, 3] = total
 
 
 def smooth_kernel(
-    rec, elec, obs, pot, guess, cond, across, from_low, from_high, own_sum, far_sum,
+    rec, elec, obs, pot, guess, cond, across, from_low, from_high, spots,
     adjoint, term, squares,
     c, v, r, d0, d1, fx, fy, fz, diag, inv, phi, final, sem,
 ):
@@ -170,12 +217,18 @@
     for k in range(HALO):
         for ref in (v, phi, c):
             ref[empty + k] = blank
-        for ref, n in ((v, k), (c, HALO + k)):
-            ref[there + k, 0:8] = jnp.where(low_keep, from_low[spare(n)], 0.0)
-            ref[there + k, 8:24] = across[n]
-            ref[there + k, 24:32] = jnp.where(high_keep, from_high[spare(n)], 0.0)
-        phi[there + k] = blank
+        for ref in (v, phi, c):
+            ref[there + k] = blank
+        v[there + k, 8:24] = across[k]
+        c[there + k, 8:24] = across[HALO + k]
     phi[jnp.where(gx == 0, WX + HALO, HALO - 1), 8:24] = across[2 * HALO]
+    count = spots.shape[0]
+    before, after = jnp.maximum(gy - 1, 0), jnp.minimum(gy + 1, count - 1)
+    for on, source, start, is_low in ((low_on, before, 0, True), (high_on, after, 24, False)):
+        tiles = uncorner([spots[source, k] for k in range(3)], is_low)
+        for (n, k), tile in tiles.items():
+            x = jnp.where(gx == 0, WX + HALO + k - 1, HALO - k)
+            (v, c)[n][x, start : start + 8] = jnp.where(on, tile, 0.0)
 
     lane = lax.broadcasted_iota(i32, (1, EY, DEPTH), 2)
     last, first = lane == DEPTH - 1, lane == 0
@@ -201,7 +254,9 @@
     ly = rec[1:2, :] - gy * WY + 8
     near = (lx >= 0) & (lx < EX) & (ly >= 0) & (ly < EY)
     row = jnp.where(near, lx * EY + ly, -1)
-    total = own_sum[...] + far_sum[...] + from_low[spare(2 * HALO)] + from_high[spare(2 * HALO)]
+    total = spots[0, 3]
+    for k in range(1, count):
+        total = total + spots[k, 3]
     anchor = total[4:5, :]
     pieces = [
         total[k : k + 1, :] - anchor - obs[:, DEPTH * k : DEPTH * (k + 1)]
@@ -367,19 +422,23 @@
         limit=GRANT,
     )
     theirs = lax.ppermute(mine, "gx", swap_x)
-    faces = (WX // 2 + 4, 3, 8, DEPTH)
+    faces = (WX // 2, 3, 8, DEPTH)
     up, down, partial = call(
-        pack_kernel, [faces, faces, tile], [VM] * 5, mine, theirs, pot, guess, conductivity
+        pack_kernel, [faces, faces, tile], [HB] + [VM] * 3, mine, pot, guess, conductivity,
+        scratch=[pltpu.SemaphoreType.DMA],
     )
     ring = lambda step: [(i, (i + step) % 4) for i in range(4)]
     from_low = lax.ppermute(up, "gy", ring(1))
     from_high = lax.ppermute(down, "gy", ring(3))
-    far = lax.ppermute(partial, "gy", ring(2))
+    (spots,) = call(
+        corner_kernel, [(lax.axis_size("gy"), 4, 8, DEPTH)], [VM] * 2, partial, theirs
+    )
+    spots = lax.all_to_all(spots, "gy", 0, 0, tiled=True)
     block = (WX, WY, DEPTH)
     adjoint, term, squares = call(
-        smooth_kernel, [block, block, tile], [VM, SM] + [VM] * 9,
+        smooth_kernel, [block, block, tile], [VM, SM] + [VM] * 8,
         receiver_cells, elec, observed, pot, guess, conductivity,
-        theirs, from_low, from_high, partial, far,
+        theirs, from_low, from_high, spots,
         scratch=[pltpu.VMEM((EX, EY, DEPTH), f32)] * 11
         + [pltpu.VMEM(block, f32), pltpu.SemaphoreType.DMA],
         outs=[HB, VM, VM],

time: 127 us -> 125 us (0.984)
  starting transfers between devices: 66.9 us -> 64.2 us
  blocking collectives: 23.7 us -> 25.6 us
    all_to_all x0 -> x1, blocking collectives: none -> 7.31 us  [body(): spots = lax.all_to_all(spots, 'gy', 0, 0, tiled=True)]
    all_to_all x1, blocking collectives: 23.7 us -> 18.3 us  [exchange(): lax.all_to_all(value, 'src', 0, 0, axis_index_groups=groups, tiled=True)]
    ppermute x1 -> x0, waiting for transfers between devices: 4.14 us -> none  [body(): far = lax.ppermute(partial, 'gy', ring(2))]
    all_to_all x3, starting transfers between devices: 20 us -> 23.8 us  [exchange(): lax.all_to_all(value, 'src', 0, 0, axis_index_groups=groups, tiled=True)]
    ppermute x1 -> x0, starting transfers between devices: 3.54 us -> none  [body(): far = lax.ppermute(partial, 'gy', ring(2))]
    ppermute x1, waiting for transfers between devices: 1.32 us -> 3.23 us  [body(): other = lax.ppermute(squares, 'gy', [(0, 2), (2, 0), (1, 3), (3, 1)])]
    ppermute x1, starting transfers between devices: 4.52 us -> 2.61 us  [body(): other = lax.ppermute(squares, 'gy', [(0, 2), (2, 0), (1, 3), (3, 1)])]
    ppermute x1, starting transfers between devices: 3.98 us -> 2.18 us  [body(): other = lax.ppermute(squares, 'gy', [(0, 1), (1, 0), (2, 3), (3, 2)])]
  transfers between devices with their start and end apart: 10 -> 9, of which waited for: 8 -> 6; matrix products, arithmetic and copies ran while one was open for 0% -> 0% of each run, Pallas kernels for 0% -> 0%
where the time goes in v4:
time: 125 us
  starting transfers between devices  64.2 us (51%)
  blocking collectives  25.6 us (20%)
  waiting for transfers between devices  17.1 us (14%)
  Pallas kernels  15.2 us (12%)
  local copies, waits for them, and re-layouts  1.71 us (1%)
    all_to_all x3, starting transfers between devices, exchange(): lax.all_to_all(value, 'src', 0, 0, axis_index_groups=groups, tiled=True)  23.8 us
    all_to_all x1, blocking collectives, exchange(): lax.all_to_all(value, 'src', 0, 0, axis_index_groups=groups, tiled=True)  18.3 us
    ppermute x1, starting transfers between devices, body(): theirs = lax.ppermute(mine, 'gx', swap_x)  15.4 us
    pallas_call x8, Pallas kernels, call(): pl.pallas_call(kernel, out_shape=[jax.ShapeDtypeStruct(shape, f32) for sh...  15.2 us
    ppermute x1, starting transfers between devices, body(): other = lax.ppermute(squares, 'gx', swap_x)  12.8 us
    all_to_all x3, waiting for transfers between devices, exchange(): lax.all_to_all(value, 'src', 0, 0, axis_index_groups=groups, tiled=True)  8.47 us
    all_to_all x1, blocking collectives, body(): spots = lax.all_to_all(spots, 'gy', 0, 0, tiled=True)  7.31 us
    ppermute x1, starting transfers between devices, body(): from_low = lax.ppermute(up, 'gy', ring(1))  4.03 us
  transfers between devices with their start and end apart: 9, of which 6 were waited for; matrix products, arithmetic and copies ran while one was open for 0% of the time, Pallas kernels for 0%

profile of v4, /device:TPU:1, one launch (start us, length us, event | category | flops | bytes accessed | tf_op | source)
XLA Modules:
  0.0 124.6 jit_solution(8963670445715635942)
XLA Ops:
  0.7 3.3 %shard_map.85.mine = f32[12,16,128]{2,1,0:T(8,128)} custom-call(s32[1,3]{1,0:T(1,128)} %bitcast.14, s32[3,512]{1,0:T(4,128)} %rec.1, f32[64,16,128]{2,1,0:T(8,128)} %bitcast.8, f32[64,16,128]{2,1,0:T(8,128)} %bitcast.11, f32[64,16,128]{2,1,0:T(8,128)} %cond.5), custom_call_target="tpu_custom_call" | custom-call | tf_op jit(solution)/shard_map/pallas_call | solution.py:398
  4.0 0.0 copy-start.3
  4.0 0.9 copy-done.3
  4.9 0.1 shard_map.86
  5.0 4.0 %collective-permute-start.1 = (f32[32,3,8,128]{3,2,1,0:T(8,128)S(1)}, f32[32,3,8,128]{3,2,1,0:T(8,128)S(1)}, u32[]{:S(2)}, u32[]{:S(2)}) collective-permute-start(f32[32,3,8,128]{3,2,1,0:T(8,128)S(1)} %get-tuple-element.13), channel_id=1, source_target_pairs={{0,1},{1,2},{2,3},{3,0},{4,5},{5,6},{6,7},{7,4},{8,9},{9,10},{10,1... | collective-permute-start | bytes 1179656 | tf_op jit(solution)/shard_map/ppermute | solution.py:431
  9.1 3.4 %collective-permute-start.2 = (f32[32,3,8,128]{3,2,1,0:T(8,128)S(1)}, f32[32,3,8,128]{3,2,1,0:T(8,128)S(1)}, u32[]{:S(2)}, u32[]{:S(2)}) collective-permute-start(f32[32,3,8,128]{3,2,1,0:T(8,128)S(1)} %get-tuple-element.14), channel_id=1, source_target_pairs={{0,3},{1,0},{2,1},{3,2},{4,7},{5,4},{6,5},{7,6},{8,11},{9,8},{10,9... | collective-permute-start | bytes 1179656 | tf_op jit(solution)/shard_map/ppermute | solution.py:432
  12.4 15.4 %collective-permute-start = (f32[12,16,128]{2,1,0:T(8,128)S(1)}, f32[12,16,128]{2,1,0:T(8,128)S(1)}, u32[]{:S(2)}, u32[]{:S(2)}) collective-permute-start(f32[12,16,128]{2,1,0:T(8,128)S(1)} %copy-done.3), channel_id=1, source_target_pairs={{0,4},{4,0},{1,5},{5,1},{2,6},{6,2},{3,7},{7,3},{8,12},{12,8},{9,1... | collective-permute-start | bytes 294920 | tf_op jit(solution)/shard_map/ppermute | solution.py:424
  27.9 2.3 %collective-permute-done.theirs.across = f32[12,16,128]{2,1,0:T(8,128)S(1)} collective-permute-done((f32[12,16,128]{2,1,0:T(8,128)S(1)}, f32[12,16,128]{2,1,0:T(8,128)S(1)}, u32[]{:S(2)}, u32[]{:S(2)}) %collective-permute-start) | collective-permute-done | bytes 98336 | tf_op jit(solution)/shard_map/ppermute | solution.py:424
  30.2 0.0 copy-start.4
  30.2 0.0 copy-start.5
  30.2 0.0 copy-start.6
  30.2 7.3 %all_to_all.25.spots = f32[4,4,8,128]{3,2,1,0:T(8,128)S(1)} all-to-all(f32[4,4,8,128]{3,2,1,0:T(8,128)S(1)} %shard_map.87), channel_id=1, replica_groups=mesh['src'=64,'gx'=2,'gy'=4] {'gy'}, dimensions={0} | all-to-all | bytes 131072 | tf_op jit(solution)/shard_map/all_to_all | solution.py:436
  37.5 0.0 collective-permute-done.1.from_low
  37.5 0.0 collective-permute-done.2.from_high
  37.6 9.6 %shard_map.88 = (f32[64,16,128]{2,1,0:T(8,128)}, f32[64,16,128]{2,1,0:T(8,128)}, f32[8,128]{1,0:T(8,128)S(1)}) custom-call(s32[3,512]{1,0:T(4,128)S(1)} %copy-done.4, s32[1,3]{1,0:T(1,128)S(1)} %bitcast.15, f32[1,512]{1,0:T(1,128)S(1)} %copy-done.5, f32[64,16,128]{2,1,0:T(8,128)S(1)} %bitcast.10, f32[64,16,128]{2,1,0:T(8,128)S(1)} %bitcast.13, ...), custom_call_target="tpu_custom_call" | custom-call | tf_op jit(solution)/shard_map/pallas_call | solution.py:398
  47.2 11.3 %all-to-all-start.1 = ((f32[8,8,16,128]{3,2,1,0:T(8,128)}), f32[8,8,16,128]{3,2,1,0:T(8,128)S(1)}, u32[]{:S(2)}, u32[]{:S(2)}) async-start(f32[8,8,16,128]{3,2,1,0:T(8,128)} %bitcast.4), calls=%async_computation.1 | async-start | bytes 1048576 | tf_op jit(solution)/shard_map/all_to_all | solution.py:450
  58.5 12.8 %collective-permute-start.3 = (f32[8,128]{1,0:T(8,128)S(1)}, f32[8,128]{1,0:T(8,128)S(1)}, u32[]{:S(2)}, u32[]{:S(2)}) collective-permute-start(f32[8,128]{1,0:T(8,128)S(1)} %get-tuple-element.18.own), channel_id=1, source_target_pairs={{0,4},{4,0},{1,5},{5,1},{2,6},{6,2},{3,7},{7,3},{8,12},{12,8},{9,1... | collective-permute-start | bytes 12296 | tf_op jit(solution)/shard_map/ppermute | solution.py:452
  71.3 1.0 collective-permute-done.3.got
  72.3 0.1 shard_map.89
  72.3 18.3 %all_to_all.26.refs_0_ = f32[8,2,16,128]{3,2,1,0:T(8,128)S(1)} all-to-all(f32[8,2,16,128]{3,2,1,0:T(8,128)S(1)} %get-tuple-element.19), channel_id=1, replica_groups={{0,64,128,192,256,320,384,448},{8,72,136,200,264,328,392,456},{16,80,14..., dimensions={0} | all-to-all | bytes 262144 | tf_op jit(solution)/shard_map/all_to_all | solution.py:450
  90.6 0.7 shard_map.90
  91.3 5.3 %all-to-all-start.3 = ((f32[8,16,128]{2,1,0:T(8,128)}), f32[8,16,128]{2,1,0:T(8,128)S(1)}, u32[]{:S(2)}, u32[]{:S(2)}) async-start(f32[8,16,128]{2,1,0:T(8,128)} %shard_map.90), calls=%async_computation.3 | async-start | bytes 131072 | tf_op jit(solution)/shard_map/all_to_all | solution.py:450
  96.5 2.2 %collective-permute-start.4 = (f32[8,128]{1,0:T(8,128)S(1)}, f32[8,128]{1,0:T(8,128)S(1)}, u32[]{:S(2)}, u32[]{:S(2)}) collective-permute-start(f32[8,128]{1,0:T(8,128)S(1)} %get-tuple-element.20.own), channel_id=1, source_target_pairs={{0,1},{1,0},{2,3},{3,2},{4,5},{5,4},{6,7},{7,6},{8,9},{9,8},{10,11... | collective-permute-start | bytes 12296 | tf_op jit(solution)/shard_map/ppermute | solution.py:461
  98.7 2.1 %collective-permute-done.4.got = f32[8,128]{1,0:T(8,128)S(1)} collective-permute-done((f32[8,128]{1,0:T(8,128)S(1)}, f32[8,128]{1,0:T(8,128)S(1)}, u32[]{:S(2)}, u32[]{:S(2)}) %collective-permute-start.4) | collective-permute-done | bytes 4128 | tf_op jit(solution)/shard_map/ppermute | solution.py:461
  100.9 5.4 %all-to-all-done.3.rows = f32[8,16,128]{2,1,0:T(8,128)S(1)} async-done(((f32[8,16,128]{2,1,0:T(8,128)}), f32[8,16,128]{2,1,0:T(8,128)S(1)}, u32[]{:S(2)}, u32[]{:S(2)}) %all-to-all-start.3) | async-done | bytes 65568 | tf_op jit(solution)/shard_map/all_to_all | solution.py:450
  106.3 0.8 shard_map.91
  107.1 7.2 %all-to-all-start.4 = ((f32[8,8,16,128]{3,2,1,0:T(8,128)}), f32[8,8,16,128]{3,2,1,0:T(8,128)S(1)}, u32[]{:S(2)}, u32[]{:S(2)}) async-start(f32[8,8,16,128]{3,2,1,0:T(8,128)} %get-tuple-element.22), calls=%async_computation.4 | async-start | bytes 1048576 | tf_op jit(solution)/shard_map/all_to_all | solution.py:450
  114.3 2.6 %collective-permute-start.5 = (f32[8,128]{1,0:T(8,128)S(1)}, f32[8,128]{1,0:T(8,128)S(1)}, u32[]{:S(2)}, u32[]{:S(2)}) collective-permute-start(f32[8,128]{1,0:T(8,128)S(1)} %get-tuple-element.21.refs_0_), channel_id=1, source_target_pairs={{0,2},{2,0},{1,3},{3,1},{4,6},{6,4},{5,7},{7,5},{8,10},{10,8},{9,1... | collective-permute-start | bytes 12296 | tf_op jit(solution)/shard_map/ppermute | solution.py:466
  117.0 3.2 %collective-permute-done.5.refs_1_ = f32[8,128]{1,0:T(8,128)S(1)} collective-permute-done((f32[8,128]{1,0:T(8,128)S(1)}, f32[8,128]{1,0:T(8,128)S(1)}, u32[]{:S(2)}, u32[]{:S(2)}) %collective-permute-start.5) | collective-permute-done | bytes 4128 | tf_op jit(solution)/shard_map/ppermute | solution.py:466
  120.2 0.6 shard_map.92
  120.8 3.0 %all-to-all-done.4 = f32[8,8,16,128]{3,2,1,0:T(8,128)S(1)} async-done(((f32[8,8,16,128]{3,2,1,0:T(8,128)}), f32[8,8,16,128]{3,2,1,0:T(8,128)S(1)}, u32[]{:S(2)}, u32[]{:S(2)}) %all-to-all-start.4) | async-done | bytes 524320 | tf_op jit(solution)/shard_map/all_to_all | solution.py:450
  123.8 0.8 copy.10
  (11 shorter events, 0.0 us)
Async XLA Ops:
  0.6 3.3 %copy-start = (f32[1,64,16,128]{3,2,1,0:T(8,128)S(1)}, f32[1,64,16,128]{3,2,1,0:T(8,128)}, u32[]{:S(2)}) copy-start(f32[1,64,16,128]{3,2,1,0:T(8,128)} %param.7) | copy-start | bytes 1572868
  0.6 3.3 %copy-start.1 = (f32[1,64,16,128]{3,2,1,0:T(8,128)S(1)}, f32[1,64,16,128]{3,2,1,0:T(8,128)}, u32[]{:S(2)}) copy-start(f32[1,64,16,128]{3,2,1,0:T(8,128)} %param.8) | copy-start | bytes 1572868
  0.7 3.3 %copy-start.2 = (f32[64,16,128]{2,1,0:T(8,128)S(1)}, f32[64,16,128]{2,1,0:T(8,128)}, u32[]{:S(2)}) copy-start(f32[64,16,128]{2,1,0:T(8,128)} %cond.5) | copy-start | bytes 1572868
  4.0 0.9 copy-start.3
  5.0 32.5 %collective-permute-start.1 = (f32[32,3,8,128]{3,2,1,0:T(8,128)S(1)}, f32[32,3,8,128]{3,2,1,0:T(8,128)S(1)}, u32[]{:S(2)}, u32[]{:S(2)}) collective-permute-start(f32[32,3,8,128]{3,2,1,0:T(8,128)S(1)} %get-tuple-element.13), channel_id=1, source_target_pairs={{0,1},{1,2},{2,3},{3,0},{4,5},{5,6},{6,7},{7,4},{8,9},{9,10},{10,1... | collective-permute-start | bytes 1179656 | tf_op jit(solution)/shard_map/ppermute | solution.py:431
  9.1 28.5 %collective-permute-start.2 = (f32[32,3,8,128]{3,2,1,0:T(8,128)S(1)}, f32[32,3,8,128]{3,2,1,0:T(8,128)S(1)}, u32[]{:S(2)}, u32[]{:S(2)}) collective-permute-start(f32[32,3,8,128]{3,2,1,0:T(8,128)S(1)} %get-tuple-element.14), channel_id=1, source_target_pairs={{0,3},{1,0},{2,1},{3,2},{4,7},{5,4},{6,5},{7,6},{8,11},{9,8},{10,9... | collective-permute-start | bytes 1179656 | tf_op jit(solution)/shard_map/ppermute | solution.py:432
  12.4 17.7 %collective-permute-start = (f32[12,16,128]{2,1,0:T(8,128)S(1)}, f32[12,16,128]{2,1,0:T(8,128)S(1)}, u32[]{:S(2)}, u32[]{:S(2)}) collective-permute-start(f32[12,16,128]{2,1,0:T(8,128)S(1)} %copy-done.3), channel_id=1, source_target_pairs={{0,4},{4,0},{1,5},{5,1},{2,6},{6,2},{3,7},{7,3},{8,12},{12,8},{9,1... | collective-permute-start | bytes 294920 | tf_op jit(solution)/shard_map/ppermute | solution.py:424
  30.2 7.4 %copy-start.4 = (s32[3,512]{1,0:T(4,128)S(1)}, s32[3,512]{1,0:T(4,128)}, u32[]{:S(2)}) copy-start(s32[3,512]{1,0:T(4,128)} %rec.1) | copy-start | bytes 18436
  30.2 7.4 %copy-start.5 = (f32[1,512]{1,0:T(1,128)S(1)}, f32[1,512]{1,0:T(1,128)}, u32[]{:S(2)}) copy-start(f32[1,512]{1,0:T(1,128)} %obs.1) | copy-start | bytes 6148
  30.2 7.3 %copy-start.6 = (s32[3,1]{0,1:T(1,128)S(1)}, s32[3,1]{0,1:T(1,128)}, u32[]{:S(2)}) copy-start(s32[3,1]{0,1:T(1,128)} %param.11) | copy-start | bytes 40
  47.2 25.1 %all-to-all-start.1 = ((f32[8,8,16,128]{3,2,1,0:T(8,128)}), f32[8,8,16,128]{3,2,1,0:T(8,128)S(1)}, u32[]{:S(2)}, u32[]{:S(2)}) async-start(f32[8,8,16,128]{3,2,1,0:T(8,128)} %bitcast.4), calls=%async_computation.1 | async-start | bytes 1048576 | tf_op jit(solution)/shard_map/all_to_all | solution.py:450
  58.5 13.8 %collective-permute-start.3 = (f32[8,128]{1,0:T(8,128)S(1)}, f32[8,128]{1,0:T(8,128)S(1)}, u32[]{:S(2)}, u32[]{:S(2)}) collective-permute-start(f32[8,128]{1,0:T(8,128)S(1)} %get-tuple-element.18.own), channel_id=1, source_target_pairs={{0,4},{4,0},{1,5},{5,1},{2,6},{6,2},{3,7},{7,3},{8,12},{12,8},{9,1... | collective-permute-start | bytes 12296 | tf_op jit(solution)/shard_map/ppermute | solution.py:452
  91.3 15.1 %all-to-all-start.3 = ((f32[8,16,128]{2,1,0:T(8,128)}), f32[8,16,128]{2,1,0:T(8,128)S(1)}, u32[]{:S(2)}, u32[]{:S(2)}) async-start(f32[8,16,128]{2,1,0:T(8,128)} %shard_map.90), calls=%async_computation.3 | async-start | bytes 131072 | tf_op jit(solution)/shard_map/all_to_all | solution.py:450
  96.5 4.3 %collective-permute-start.4 = (f32[8,128]{1,0:T(8,128)S(1)}, f32[8,128]{1,0:T(8,128)S(1)}, u32[]{:S(2)}, u32[]{:S(2)}) collective-permute-start(f32[8,128]{1,0:T(8,128)S(1)} %get-tuple-element.20.own), channel_id=1, source_target_pairs={{0,1},{1,0},{2,3},{3,2},{4,5},{5,4},{6,7},{7,6},{8,9},{9,8},{10,11... | collective-permute-start | bytes 12296 | tf_op jit(solution)/shard_map/ppermute | solution.py:461
  107.1 16.7 %all-to-all-start.4 = ((f32[8,8,16,128]{3,2,1,0:T(8,128)}), f32[8,8,16,128]{3,2,1,0:T(8,128)S(1)}, u32[]{:S(2)}, u32[]{:S(2)}) async-start(f32[8,8,16,128]{3,2,1,0:T(8,128)} %get-tuple-element.22), calls=%async_computation.4 | async-start | bytes 1048576 | tf_op jit(solution)/shard_map/all_to_all | solution.py:450
  114.3 5.8 %collective-permute-start.5 = (f32[8,128]{1,0:T(8,128)S(1)}, f32[8,128]{1,0:T(8,128)S(1)}, u32[]{:S(2)}, u32[]{:S(2)}) collective-permute-start(f32[8,128]{1,0:T(8,128)S(1)} %get-tuple-element.21.refs_0_), channel_id=1, source_target_pairs={{0,2},{2,0},{1,3},{3,1},{4,6},{6,4},{5,7},{7,5},{8,10},{10,8},{9,1... | collective-permute-start | bytes 12296 | tf_op jit(solution)/shard_map/ppermute | solution.py:466

commit v5 on v4

--- a/solution.py
+++ b/solution.py
@@ -95,11 +95,11 @@
     return out
 
 
-def gather_kernel(elec, rec_in, pot_in, guess, cond, out, rec, pot, sems):
+def gather_kernel(elec_in, rec_in, pot_in, guess, cond, out, elec, rec, pot, sems):
     gx, gy = lax.axis_index("gx"), lax.axis_index("gy")
     base = jnp.where(gx == 0, WX - HALO, 0)
     step = WX // LOADS
-    pairs = [(rec_in, rec)]
+    pairs = [(rec_in, rec), (elec_in, elec)]
     for k in range(LOADS):
         pairs.append((pot_in.at[pl.ds(k * step, step)], pot.at[pl.ds(k * step, step)]))
     pairs.append((guess.at[pl.ds(base, HALO)], out.at[pl.ds(0, HALO)]))
@@ -412,12 +412,13 @@
     tile = (8, DEPTH)
     swap_x = [(0, 1), (1, 0)]
     (mine,) = call(
-        gather_kernel, [(2 * HALO + 2, WY, DEPTH)], [SM, HB, HB, HB, HB],
+        gather_kernel, [(2 * HALO + 2, WY, DEPTH)], [HB] * 5,
         elec, receiver_cells, pot, guess, conductivity,
         scratch=[
+            pltpu.SMEM((1, 3), i32),
             pltpu.VMEM((3, NREC), i32),
             pltpu.VMEM((WX, WY, DEPTH), f32),
-            pltpu.SemaphoreType.DMA((3 + LOADS,)),
+            pltpu.SemaphoreType.DMA((4 + LOADS,)),
         ],
         limit=GRANT,
     )

time: 125 us -> 125 us (level)
  no operation moved by 1% of the time
where the time goes in v5:
time: 125 us; the launch traced here: 124 us
  starting transfers between devices  64.2 us (51%)
  blocking collectives  25.6 us (20%)
  waiting for transfers between devices  17.1 us (14%)
  Pallas kernels  14.5 us (12%)
  local copies, waits for them, and re-layouts  1.71 us (1%)
    all_to_all x3, starting transfers between devices, exchange(): lax.all_to_all(value, 'src', 0, 0, axis_index_groups=groups, tiled=True)  23.8 us
    all_to_all x1, blocking collectives, exchange(): lax.all_to_all(value, 'src', 0, 0, axis_index_groups=groups, tiled=True)  18.3 us
    ppermute x1, starting transfers between devices, body(): theirs = lax.ppermute(mine, 'gx', swap_x)  15.4 us
    pallas_call x8, Pallas kernels, call(): pl.pallas_call(kernel, out_shape=[jax.ShapeDtypeStruct(shape, f32) for sh...  14.5 us
    ppermute x1, starting transfers between devices, body(): other = lax.ppermute(squares, 'gx', swap_x)  12.8 us
    all_to_all x3, waiting for transfers between devices, exchange(): lax.all_to_all(value, 'src', 0, 0, axis_index_groups=groups, tiled=True)  8.47 us
    all_to_all x1, blocking collectives, body(): spots = lax.all_to_all(spots, 'gy', 0, 0, tiled=True)  7.31 us
    ppermute x1, starting transfers between devices, body(): from_low = lax.ppermute(up, 'gy', ring(1))  4.03 us
  transfers between devices with their start and end apart: 9, of which 6 were waited for; matrix products, arithmetic and copies ran while one was open for 0% of the time, Pallas kernels for 0%

profile of v5, /device:TPU:1, one launch (start us, length us, event | category | flops | bytes accessed | tf_op | source)
XLA Modules:
  0.0 123.9 jit_solution(1913619221236908346)
XLA Ops:
  0.7 2.6 %shard_map.85.mine = f32[12,16,128]{2,1,0:T(8,128)} custom-call(s32[1,3]{1,0:T(1,128)} %bitcast.14, s32[3,512]{1,0:T(4,128)} %rec.1, f32[64,16,128]{2,1,0:T(8,128)} %bitcast.8, f32[64,16,128]{2,1,0:T(8,128)} %bitcast.11, f32[64,16,128]{2,1,0:T(8,128)} %cond.5), custom_call_target="tpu_custom_call" | custom-call | tf_op jit(solution)/shard_map/pallas_call | solution.py:398
  3.3 0.0 copy-start.3
  3.3 0.9 copy-done.3
  4.2 0.1 shard_map.86
  4.3 4.0 %collective-permute-start.1 = (f32[32,3,8,128]{3,2,1,0:T(8,128)S(1)}, f32[32,3,8,128]{3,2,1,0:T(8,128)S(1)}, u32[]{:S(2)}, u32[]{:S(2)}) collective-permute-start(f32[32,3,8,128]{3,2,1,0:T(8,128)S(1)} %get-tuple-element.13), channel_id=1, source_target_pairs={{0,1},{1,2},{2,3},{3,0},{4,5},{5,6},{6,7},{7,4},{8,9},{9,10},{10,1... | collective-permute-start | bytes 1179656 | tf_op jit(solution)/shard_map/ppermute | solution.py:432
  8.4 3.4 %collective-permute-start.2 = (f32[32,3,8,128]{3,2,1,0:T(8,128)S(1)}, f32[32,3,8,128]{3,2,1,0:T(8,128)S(1)}, u32[]{:S(2)}, u32[]{:S(2)}) collective-permute-start(f32[32,3,8,128]{3,2,1,0:T(8,128)S(1)} %get-tuple-element.14), channel_id=1, source_target_pairs={{0,3},{1,0},{2,1},{3,2},{4,7},{5,4},{6,5},{7,6},{8,11},{9,8},{10,9... | collective-permute-start | bytes 1179656 | tf_op jit(solution)/shard_map/ppermute | solution.py:433
  11.8 15.4 %collective-permute-start = (f32[12,16,128]{2,1,0:T(8,128)S(1)}, f32[12,16,128]{2,1,0:T(8,128)S(1)}, u32[]{:S(2)}, u32[]{:S(2)}) collective-permute-start(f32[12,16,128]{2,1,0:T(8,128)S(1)} %copy-done.3), channel_id=1, source_target_pairs={{0,4},{4,0},{1,5},{5,1},{2,6},{6,2},{3,7},{7,3},{8,12},{12,8},{9,1... | collective-permute-start | bytes 294920 | tf_op jit(solution)/shard_map/ppermute | solution.py:425
  27.2 2.3 %collective-permute-done.theirs.across = f32[12,16,128]{2,1,0:T(8,128)S(1)} collective-permute-done((f32[12,16,128]{2,1,0:T(8,128)S(1)}, f32[12,16,128]{2,1,0:T(8,128)S(1)}, u32[]{:S(2)}, u32[]{:S(2)}) %collective-permute-start) | collective-permute-done | bytes 98336 | tf_op jit(solution)/shard_map/ppermute | solution.py:425
  29.5 0.0 copy-start.4
  29.5 0.0 copy-start.5
  29.5 0.0 copy-start.6
  29.5 7.3 %all_to_all.25.spots = f32[4,4,8,128]{3,2,1,0:T(8,128)S(1)} all-to-all(f32[4,4,8,128]{3,2,1,0:T(8,128)S(1)} %shard_map.87), channel_id=1, replica_groups=mesh['src'=64,'gx'=2,'gy'=4] {'gy'}, dimensions={0} | all-to-all | bytes 131072 | tf_op jit(solution)/shard_map/all_to_all | solution.py:437
  36.9 0.0 collective-permute-done.1.from_low
  36.9 0.0 collective-permute-done.2.from_high
  36.9 9.6 %shard_map.88 = (f32[64,16,128]{2,1,0:T(8,128)}, f32[64,16,128]{2,1,0:T(8,128)}, f32[8,128]{1,0:T(8,128)S(1)}) custom-call(s32[3,512]{1,0:T(4,128)S(1)} %copy-done.4, s32[1,3]{1,0:T(1,128)S(1)} %bitcast.15, f32[1,512]{1,0:T(1,128)S(1)} %copy-done.5, f32[64,16,128]{2,1,0:T(8,128)S(1)} %bitcast.10, f32[64,16,128]{2,1,0:T(8,128)S(1)} %bitcast.13, ...), custom_call_target="tpu_custom_call" | custom-call | tf_op jit(solution)/shard_map/pallas_call | solution.py:398
  46.5 11.3 %all-to-all-start.1 = ((f32[8,8,16,128]{3,2,1,0:T(8,128)}), f32[8,8,16,128]{3,2,1,0:T(8,128)S(1)}, u32[]{:S(2)}, u32[]{:S(2)}) async-start(f32[8,8,16,128]{3,2,1,0:T(8,128)} %bitcast.4), calls=%async_computation.1 | async-start | bytes 1048576 | tf_op jit(solution)/shard_map/all_to_all | solution.py:451
  57.8 12.8 %collective-permute-start.3 = (f32[8,128]{1,0:T(8,128)S(1)}, f32[8,128]{1,0:T(8,128)S(1)}, u32[]{:S(2)}, u32[]{:S(2)}) collective-permute-start(f32[8,128]{1,0:T(8,128)S(1)} %get-tuple-element.18.own), channel_id=1, source_target_pairs={{0,4},{4,0},{1,5},{5,1},{2,6},{6,2},{3,7},{7,3},{8,12},{12,8},{9,1... | collective-permute-start | bytes 12296 | tf_op jit(solution)/shard_map/ppermute | solution.py:453
  70.6 1.0 collective-permute-done.3.got
  71.6 0.1 shard_map.89
  71.6 18.3 %all_to_all.26.refs_0_ = f32[8,2,16,128]{3,2,1,0:T(8,128)S(1)} all-to-all(f32[8,2,16,128]{3,2,1,0:T(8,128)S(1)} %get-tuple-element.19), channel_id=1, replica_groups={{0,64,128,192,256,320,384,448},{8,72,136,200,264,328,392,456},{16,80,14..., dimensions={0} | all-to-all | bytes 262144 | tf_op jit(solution)/shard_map/all_to_all | solution.py:451
  89.9 0.7 shard_map.90
  90.6 5.3 %all-to-all-start.3 = ((f32[8,16,128]{2,1,0:T(8,128)}), f32[8,16,128]{2,1,0:T(8,128)S(1)}, u32[]{:S(2)}, u32[]{:S(2)}) async-start(f32[8,16,128]{2,1,0:T(8,128)} %shard_map.90), calls=%async_computation.3 | async-start | bytes 131072 | tf_op jit(solution)/shard_map/all_to_all | solution.py:451
  95.9 2.2 %collective-permute-start.4 = (f32[8,128]{1,0:T(8,128)S(1)}, f32[8,128]{1,0:T(8,128)S(1)}, u32[]{:S(2)}, u32[]{:S(2)}) collective-permute-start(f32[8,128]{1,0:T(8,128)S(1)} %get-tuple-element.20.own), channel_id=1, source_target_pairs={{0,1},{1,0},{2,3},{3,2},{4,5},{5,4},{6,7},{7,6},{8,9},{9,8},{10,11... | collective-permute-start | bytes 12296 | tf_op jit(solution)/shard_map/ppermute | solution.py:462
  98.1 2.1 %collective-permute-done.4.got = f32[8,128]{1,0:T(8,128)S(1)} collective-permute-done((f32[8,128]{1,0:T(8,128)S(1)}, f32[8,128]{1,0:T(8,128)S(1)}, u32[]{:S(2)}, u32[]{:S(2)}) %collective-permute-start.4) | collective-permute-done | bytes 4128 | tf_op jit(solution)/shard_map/ppermute | solution.py:462
  100.2 5.4 %all-to-all-done.3.rows = f32[8,16,128]{2,1,0:T(8,128)S(1)} async-done(((f32[8,16,128]{2,1,0:T(8,128)}), f32[8,16,128]{2,1,0:T(8,128)S(1)}, u32[]{:S(2)}, u32[]{:S(2)}) %all-to-all-start.3) | async-done | bytes 65568 | tf_op jit(solution)/shard_map/all_to_all | solution.py:451
  105.6 0.8 shard_map.91
  106.5 7.2 %all-to-all-start.4 = ((f32[8,8,16,128]{3,2,1,0:T(8,128)}), f32[8,8,16,128]{3,2,1,0:T(8,128)S(1)}, u32[]{:S(2)}, u32[]{:S(2)}) async-start(f32[8,8,16,128]{3,2,1,0:T(8,128)} %get-tuple-element.22), calls=%async_computation.4 | async-start | bytes 1048576 | tf_op jit(solution)/shard_map/all_to_all | solution.py:451
  113.7 2.6 %collective-permute-start.5 = (f32[8,128]{1,0:T(8,128)S(1)}, f32[8,128]{1,0:T(8,128)S(1)}, u32[]{:S(2)}, u32[]{:S(2)}) collective-permute-start(f32[8,128]{1,0:T(8,128)S(1)} %get-tuple-element.21.refs_0_), channel_id=1, source_target_pairs={{0,2},{2,0},{1,3},{3,1},{4,6},{6,4},{5,7},{7,5},{8,10},{10,8},{9,1... | collective-permute-start | bytes 12296 | tf_op jit(solution)/shard_map/ppermute | solution.py:467
  116.3 3.2 %collective-permute-done.5.refs_1_ = f32[8,128]{1,0:T(8,128)S(1)} collective-permute-done((f32[8,128]{1,0:T(8,128)S(1)}, f32[8,128]{1,0:T(8,128)S(1)}, u32[]{:S(2)}, u32[]{:S(2)}) %collective-permute-start.5) | collective-permute-done | bytes 4128 | tf_op jit(solution)/shard_map/ppermute | solution.py:467
  119.5 0.6 shard_map.92
  120.1 3.0 %all-to-all-done.4 = f32[8,8,16,128]{3,2,1,0:T(8,128)S(1)} async-done(((f32[8,8,16,128]{3,2,1,0:T(8,128)}), f32[8,8,16,128]{3,2,1,0:T(8,128)S(1)}, u32[]{:S(2)}, u32[]{:S(2)}) %all-to-all-start.4) | async-done | bytes 524320 | tf_op jit(solution)/shard_map/all_to_all | solution.py:451
  123.1 0.8 copy.10
  (11 shorter events, 0.0 us)
Async XLA Ops:
  0.6 2.7 %copy-start = (f32[1,64,16,128]{3,2,1,0:T(8,128)S(1)}, f32[1,64,16,128]{3,2,1,0:T(8,128)}, u32[]{:S(2)}) copy-start(f32[1,64,16,128]{3,2,1,0:T(8,128)} %param.7) | copy-start | bytes 1572868
  0.6 2.7 %copy-start.1 = (f32[1,64,16,128]{3,2,1,0:T(8,128)S(1)}, f32[1,64,16,128]{3,2,1,0:T(8,128)}, u32[]{:S(2)}) copy-start(f32[1,64,16,128]{3,2,1,0:T(8,128)} %param.8) | copy-start | bytes 1572868
  0.7 2.7 %copy-start.2 = (f32[64,16,128]{2,1,0:T(8,128)S(1)}, f32[64,16,128]{2,1,0:T(8,128)}, u32[]{:S(2)}) copy-start(f32[64,16,128]{2,1,0:T(8,128)} %cond.5) | copy-start | bytes 1572868
  3.3 0.9 copy-start.3
  4.3 32.5 %collective-permute-start.1 = (f32[32,3,8,128]{3,2,1,0:T(8,128)S(1)}, f32[32,3,8,128]{3,2,1,0:T(8,128)S(1)}, u32[]{:S(2)}, u32[]{:S(2)}) collective-permute-start(f32[32,3,8,128]{3,2,1,0:T(8,128)S(1)} %get-tuple-element.13), channel_id=1, source_target_pairs={{0,1},{1,2},{2,3},{3,0},{4,5},{5,6},{6,7},{7,4},{8,9},{9,10},{10,1... | collective-permute-start | bytes 1179656 | tf_op jit(solution)/shard_map/ppermute | solution.py:432
  8.4 28.5 %collective-permute-start.2 = (f32[32,3,8,128]{3,2,1,0:T(8,128)S(1)}, f32[32,3,8,128]{3,2,1,0:T(8,128)S(1)}, u32[]{:S(2)}, u32[]{:S(2)}) collective-permute-start(f32[32,3,8,128]{3,2,1,0:T(8,128)S(1)} %get-tuple-element.14), channel_id=1, source_target_pairs={{0,3},{1,0},{2,1},{3,2},{4,7},{5,4},{6,5},{7,6},{8,11},{9,8},{10,9... | collective-permute-start | bytes 1179656 | tf_op jit(solution)/shard_map/ppermute | solution.py:433
  11.8 17.7 %collective-permute-start = (f32[12,16,128]{2,1,0:T(8,128)S(1)}, f32[12,16,128]{2,1,0:T(8,128)S(1)}, u32[]{:S(2)}, u32[]{:S(2)}) collective-permute-start(f32[12,16,128]{2,1,0:T(8,128)S(1)} %copy-done.3), channel_id=1, source_target_pairs={{0,4},{4,0},{1,5},{5,1},{2,6},{6,2},{3,7},{7,3},{8,12},{12,8},{9,1... | collective-permute-start | bytes 294920 | tf_op jit(solution)/shard_map/ppermute | solution.py:425
  29.5 7.4 %copy-start.4 = (s32[3,512]{1,0:T(4,128)S(1)}, s32[3,512]{1,0:T(4,128)}, u32[]{:S(2)}) copy-start(s32[3,512]{1,0:T(4,128)} %rec.1) | copy-start | bytes 18436
  29.5 7.4 %copy-start.5 = (f32[1,512]{1,0:T(1,128)S(1)}, f32[1,512]{1,0:T(1,128)}, u32[]{:S(2)}) copy-start(f32[1,512]{1,0:T(1,128)} %obs.1) | copy-start | bytes 6148
  29.5 7.3 %copy-start.6 = (s32[3,1]{0,1:T(1,128)S(1)}, s32[3,1]{0,1:T(1,128)}, u32[]{:S(2)}) copy-start(s32[3,1]{0,1:T(1,128)} %param.11) | copy-start | bytes 40
  46.5 25.1 %all-to-all-start.1 = ((f32[8,8,16,128]{3,2,1,0:T(8,128)}), f32[8,8,16,128]{3,2,1,0:T(8,128)S(1)}, u32[]{:S(2)}, u32[]{:S(2)}) async-start(f32[8,8,16,128]{3,2,1,0:T(8,128)} %bitcast.4), calls=%async_computation.1 | async-start | bytes 1048576 | tf_op jit(solution)/shard_map/all_to_all | solution.py:451
  57.8 13.8 %collective-permute-start.3 = (f32[8,128]{1,0:T(8,128)S(1)}, f32[8,128]{1,0:T(8,128)S(1)}, u32[]{:S(2)}, u32[]{:S(2)}) collective-permute-start(f32[8,128]{1,0:T(8,128)S(1)} %get-tuple-element.18.own), channel_id=1, source_target_pairs={{0,4},{4,0},{1,5},{5,1},{2,6},{6,2},{3,7},{7,3},{8,12},{12,8},{9,1... | collective-permute-start | bytes 12296 | tf_op jit(solution)/shard_map/ppermute | solution.py:453
  90.6 15.1 %all-to-all-start.3 = ((f32[8,16,128]{2,1,0:T(8,128)}), f32[8,16,128]{2,1,0:T(8,128)S(1)}, u32[]{:S(2)}, u32[]{:S(2)}) async-start(f32[8,16,128]{2,1,0:T(8,128)} %shard_map.90), calls=%async_computation.3 | async-start | bytes 131072 | tf_op jit(solution)/shard_map/all_to_all | solution.py:451
  95.9 4.3 %collective-permute-start.4 = (f32[8,128]{1,0:T(8,128)S(1)}, f32[8,128]{1,0:T(8,128)S(1)}, u32[]{:S(2)}, u32[]{:S(2)}) collective-permute-start(f32[8,128]{1,0:T(8,128)S(1)} %get-tuple-element.20.own), channel_id=1, source_target_pairs={{0,1},{1,0},{2,3},{3,2},{4,5},{5,4},{6,7},{7,6},{8,9},{9,8},{10,11... | collective-permute-start | bytes 12296 | tf_op jit(solution)/shard_map/ppermute | solution.py:462
  106.5 16.7 %all-to-all-start.4 = ((f32[8,8,16,128]{3,2,1,0:T(8,128)}), f32[8,8,16,128]{3,2,1,0:T(8,128)S(1)}, u32[]{:S(2)}, u32[]{:S(2)}) async-start(f32[8,8,16,128]{3,2,1,0:T(8,128)} %get-tuple-element.22), calls=%async_computation.4 | async-start | bytes 1048576 | tf_op jit(solution)/shard_map/all_to_all | solution.py:451
  113.7 5.8 %collective-permute-start.5 = (f32[8,128]{1,0:T(8,128)S(1)}, f32[8,128]{1,0:T(8,128)S(1)}, u32[]{:S(2)}, u32[]{:S(2)}) collective-permute-start(f32[8,128]{1,0:T(8,128)S(1)} %get-tuple-element.21.refs_0_), channel_id=1, source_target_pairs={{0,2},{2,0},{1,3},{3,1},{4,6},{6,4},{5,7},{7,5},{8,10},{10,8},{9,1... | collective-permute-start | bytes 12296 | tf_op jit(solution)/shard_map/ppermute | solution.py:467

commit v6 on v5

--- a/solution.py
+++ b/solution.py
@@ -450,7 +450,7 @@
     def exchange(value, groups):
         return lax.all_to_all(value, "src", 0, 0, axis_index_groups=groups, tiled=True)
 
-    other = lax.ppermute(squares, "gx", swap_x)
+    other = lax.ppermute(squares, "gy", [(0, 1), (1, 0), (2, 3), (3, 2)])
     got = exchange(term.reshape(PLANE, LINE, WY, DEPTH), planes)
     sums, squares = call(
         plane_kernel, [(LINE, 2, WY, DEPTH), tile], [VM] * 3, got, squares, other
@@ -459,7 +459,7 @@
     (scaled,) = call(
         lambda *refs: scale_kernel(sources, *refs), [(LINE, WY, DEPTH)], [VM], got
     )
-    other = lax.ppermute(squares, "gy", [(0, 1), (1, 0), (2, 3), (3, 2)])
+    other = lax.ppermute(squares, "gx", swap_x)
     got = exchange(scaled, lines)
     spread, squares = call(
         spread_kernel, [(PLANE, LINE, WY, DEPTH), tile], [VM] * 3, got, squares, other

time: 125 us -> 123 us (0.984)
  starting transfers between devices: 64.2 us -> 59.8 us
  waiting for transfers between devices: 17.1 us -> 19.5 us
    ppermute x1, starting transfers between devices: 12.8 us -> 9.39 us  [body(): other = lax.ppermute(squares, 'gx', swap_x)]
    ppermute x1, waiting for transfers between devices: 0.98 us -> 3.66 us  [body(): other = lax.ppermute(squares, 'gx', swap_x)]
  transfers between devices with their start and end apart: 9 -> 9, of which waited for: 6 -> 6; matrix products, arithmetic and copies ran while one was open for 0% -> 0% of each run, Pallas kernels for 0% -> 1%
where the time goes in v6:
time: 123 us
  starting transfers between devices  59.8 us (49%)
  blocking collectives  26.3 us (21%)
  waiting for transfers between devices  19.5 us (16%)
  Pallas kernels  14.5 us (12%)
  local copies, waits for them, and re-layouts  1.71 us (1%)
    all_to_all x3, starting transfers between devices, exchange(): lax.all_to_all(value, 'src', 0, 0, axis_index_groups=groups, tiled=True)  22.7 us
    all_to_all x1, blocking collectives, exchange(): lax.all_to_all(value, 'src', 0, 0, axis_index_groups=groups, tiled=True)  19 us
    ppermute x1, starting transfers between devices, body(): theirs = lax.ppermute(mine, 'gx', swap_x)  15.4 us
    pallas_call x8, Pallas kernels, call(): pl.pallas_call(kernel, out_shape=[jax.ShapeDtypeStruct(shape, f32) for sh...  14.5 us
    ppermute x1, starting transfers between devices, body(): other = lax.ppermute(squares, 'gx', swap_x)  9.39 us
    all_to_all x3, waiting for transfers between devices, exchange(): lax.all_to_all(value, 'src', 0, 0, axis_index_groups=groups, tiled=True)  7.9 us
    all_to_all x1, blocking collectives, body(): spots = lax.all_to_all(spots, 'gy', 0, 0, tiled=True)  7.31 us
    ppermute x1, starting transfers between devices, body(): from_low = lax.ppermute(up, 'gy', ring(1))  4.03 us
  transfers between devices with their start and end apart: 9, of which 6 were waited for; matrix products, arithmetic and copies ran while one was open for 0% of the time, Pallas kernels for 1%

profile of v6, /device:TPU:1, one launch (start us, length us, event | category | flops | bytes accessed | tf_op | source)
XLA Modules:
  0.0 122.6 jit_solution(8497873504584752246)
XLA Ops:
  0.7 2.6 %shard_map.85.mine = f32[12,16,128]{2,1,0:T(8,128)} custom-call(s32[1,3]{1,0:T(1,128)} %bitcast.14, s32[3,512]{1,0:T(4,128)} %rec.1, f32[64,16,128]{2,1,0:T(8,128)} %bitcast.8, f32[64,16,128]{2,1,0:T(8,128)} %bitcast.11, f32[64,16,128]{2,1,0:T(8,128)} %cond.5), custom_call_target="tpu_custom_call" | custom-call | tf_op jit(solution)/shard_map/pallas_call | solution.py:398
  3.3 0.0 copy-start.3
  3.3 0.9 copy-done.3
  4.2 0.1 shard_map.86
  4.3 4.0 %collective-permute-start.1 = (f32[32,3,8,128]{3,2,1,0:T(8,128)S(1)}, f32[32,3,8,128]{3,2,1,0:T(8,128)S(1)}, u32[]{:S(2)}, u32[]{:S(2)}) collective-permute-start(f32[32,3,8,128]{3,2,1,0:T(8,128)S(1)} %get-tuple-element.13), channel_id=1, source_target_pairs={{0,1},{1,2},{2,3},{3,0},{4,5},{5,6},{6,7},{7,4},{8,9},{9,10},{10,1... | collective-permute-start | bytes 1179656 | tf_op jit(solution)/shard_map/ppermute | solution.py:432
  8.4 3.4 %collective-permute-start.2 = (f32[32,3,8,128]{3,2,1,0:T(8,128)S(1)}, f32[32,3,8,128]{3,2,1,0:T(8,128)S(1)}, u32[]{:S(2)}, u32[]{:S(2)}) collective-permute-start(f32[32,3,8,128]{3,2,1,0:T(8,128)S(1)} %get-tuple-element.14), channel_id=1, source_target_pairs={{0,3},{1,0},{2,1},{3,2},{4,7},{5,4},{6,5},{7,6},{8,11},{9,8},{10,9... | collective-permute-start | bytes 1179656 | tf_op jit(solution)/shard_map/ppermute | solution.py:433
  11.8 15.4 %collective-permute-start = (f32[12,16,128]{2,1,0:T(8,128)S(1)}, f32[12,16,128]{2,1,0:T(8,128)S(1)}, u32[]{:S(2)}, u32[]{:S(2)}) collective-permute-start(f32[12,16,128]{2,1,0:T(8,128)S(1)} %copy-done.3), channel_id=1, source_target_pairs={{0,4},{4,0},{1,5},{5,1},{2,6},{6,2},{3,7},{7,3},{8,12},{12,8},{9,1... | collective-permute-start | bytes 294920 | tf_op jit(solution)/shard_map/ppermute | solution.py:425
  27.2 2.3 %collective-permute-done.theirs.across = f32[12,16,128]{2,1,0:T(8,128)S(1)} collective-permute-done((f32[12,16,128]{2,1,0:T(8,128)S(1)}, f32[12,16,128]{2,1,0:T(8,128)S(1)}, u32[]{:S(2)}, u32[]{:S(2)}) %collective-permute-start) | collective-permute-done | bytes 98336 | tf_op jit(solution)/shard_map/ppermute | solution.py:425
  29.5 0.0 copy-start.4
  29.5 0.0 copy-start.5
  29.5 0.0 copy-start.6
  29.5 7.3 %all_to_all.25.spots = f32[4,4,8,128]{3,2,1,0:T(8,128)S(1)} all-to-all(f32[4,4,8,128]{3,2,1,0:T(8,128)S(1)} %shard_map.87), channel_id=1, replica_groups=mesh['src'=64,'gx'=2,'gy'=4] {'gy'}, dimensions={0} | all-to-all | bytes 131072 | tf_op jit(solution)/shard_map/all_to_all | solution.py:437
  36.9 0.0 collective-permute-done.1.from_low
  36.9 9.6 %shard_map.88 = (f32[64,16,128]{2,1,0:T(8,128)}, f32[64,16,128]{2,1,0:T(8,128)}, f32[8,128]{1,0:T(8,128)S(1)}) custom-call(s32[3,512]{1,0:T(4,128)S(1)} %copy-done.4, s32[1,3]{1,0:T(1,128)S(1)} %bitcast.15, f32[1,512]{1,0:T(1,128)S(1)} %copy-done.5, f32[64,16,128]{2,1,0:T(8,128)S(1)} %bitcast.10, f32[64,16,128]{2,1,0:T(8,128)S(1)} %bitcast.13, ...), custom_call_target="tpu_custom_call" | custom-call | tf_op jit(solution)/shard_map/pallas_call | solution.py:398
  46.5 11.3 %all-to-all-start.1 = ((f32[8,8,16,128]{3,2,1,0:T(8,128)}), f32[8,8,16,128]{3,2,1,0:T(8,128)S(1)}, u32[]{:S(2)}, u32[]{:S(2)}) async-start(f32[8,8,16,128]{3,2,1,0:T(8,128)} %bitcast.4), calls=%async_computation.1 | async-start | bytes 1048576 | tf_op jit(solution)/shard_map/all_to_all | solution.py:451
  57.8 2.2 %collective-permute-start.3 = (f32[8,128]{1,0:T(8,128)S(1)}, f32[8,128]{1,0:T(8,128)S(1)}, u32[]{:S(2)}, u32[]{:S(2)}) collective-permute-start(f32[8,128]{1,0:T(8,128)S(1)} %get-tuple-element.18.own), channel_id=1, source_target_pairs={{0,1},{1,0},{2,3},{3,2},{4,5},{5,4},{6,7},{7,6},{8,9},{9,8},{10,11... | collective-permute-start | bytes 12296 | tf_op jit(solution)/shard_map/ppermute | solution.py:453
  60.0 2.4 %collective-permute-done.3.got = f32[8,128]{1,0:T(8,128)S(1)} collective-permute-done((f32[8,128]{1,0:T(8,128)S(1)}, f32[8,128]{1,0:T(8,128)S(1)}, u32[]{:S(2)}, u32[]{:S(2)}) %collective-permute-start.3) | collective-permute-done | bytes 4128 | tf_op jit(solution)/shard_map/ppermute | solution.py:453
  62.4 4.8 %all-to-all-done.1.parts = f32[8,8,16,128]{3,2,1,0:T(8,128)S(1)} async-done(((f32[8,8,16,128]{3,2,1,0:T(8,128)}), f32[8,8,16,128]{3,2,1,0:T(8,128)S(1)}, u32[]{:S(2)}, u32[]{:S(2)}) %all-to-all-start.1) | async-done | bytes 524320 | tf_op jit(solution)/shard_map/all_to_all | solution.py:451
  67.3 0.1 shard_map.89
  67.4 19.0 %all_to_all.26.refs_0_ = f32[8,2,16,128]{3,2,1,0:T(8,128)S(1)} all-to-all(f32[8,2,16,128]{3,2,1,0:T(8,128)S(1)} %get-tuple-element.19), channel_id=1, replica_groups={{0,64,128,192,256,320,384,448},{8,72,136,200,264,328,392,456},{16,80,14..., dimensions={0} | all-to-all | bytes 262144 | tf_op jit(solution)/shard_map/all_to_all | solution.py:451
  86.4 0.7 shard_map.90
  87.0 5.6 %all-to-all-start.3 = ((f32[8,16,128]{2,1,0:T(8,128)}), f32[8,16,128]{2,1,0:T(8,128)S(1)}, u32[]{:S(2)}, u32[]{:S(2)}) async-start(f32[8,16,128]{2,1,0:T(8,128)} %shard_map.90), calls=%async_computation.3 | async-start | bytes 131072 | tf_op jit(solution)/shard_map/all_to_all | solution.py:451
  92.7 9.4 %collective-permute-start.4 = (f32[8,128]{1,0:T(8,128)S(1)}, f32[8,128]{1,0:T(8,128)S(1)}, u32[]{:S(2)}, u32[]{:S(2)}) collective-permute-start(f32[8,128]{1,0:T(8,128)S(1)} %get-tuple-element.20.own), channel_id=1, source_target_pairs={{0,4},{4,0},{1,5},{5,1},{2,6},{6,2},{3,7},{7,3},{8,12},{12,8},{9,1... | collective-permute-start | bytes 12296 | tf_op jit(solution)/shard_map/ppermute | solution.py:462
  102.1 3.7 %collective-permute-done.4.got = f32[8,128]{1,0:T(8,128)S(1)} collective-permute-done((f32[8,128]{1,0:T(8,128)S(1)}, f32[8,128]{1,0:T(8,128)S(1)}, u32[]{:S(2)}, u32[]{:S(2)}) %collective-permute-start.4) | collective-permute-done | bytes 4128 | tf_op jit(solution)/shard_map/ppermute | solution.py:462
  105.7 0.0 all-to-all-done.3.rows
  105.7 0.8 shard_map.91
  106.5 5.8 %all-to-all-start.4 = ((f32[8,8,16,128]{3,2,1,0:T(8,128)}), f32[8,8,16,128]{3,2,1,0:T(8,128)S(1)}, u32[]{:S(2)}, u32[]{:S(2)}) async-start(f32[8,8,16,128]{3,2,1,0:T(8,128)} %get-tuple-element.22), calls=%async_computation.4 | async-start | bytes 1048576 | tf_op jit(solution)/shard_map/all_to_all | solution.py:451
  112.3 2.6 %collective-permute-start.5 = (f32[8,128]{1,0:T(8,128)S(1)}, f32[8,128]{1,0:T(8,128)S(1)}, u32[]{:S(2)}, u32[]{:S(2)}) collective-permute-start(f32[8,128]{1,0:T(8,128)S(1)} %get-tuple-element.21.refs_0_), channel_id=1, source_target_pairs={{0,2},{2,0},{1,3},{3,1},{4,6},{6,4},{5,7},{7,5},{8,10},{10,8},{9,1... | collective-permute-start | bytes 12296 | tf_op jit(solution)/shard_map/ppermute | solution.py:467
  114.9 3.2 %collective-permute-done.5.refs_1_ = f32[8,128]{1,0:T(8,128)S(1)} collective-permute-done((f32[8,128]{1,0:T(8,128)S(1)}, f32[8,128]{1,0:T(8,128)S(1)}, u32[]{:S(2)}, u32[]{:S(2)}) %collective-permute-start.5) | collective-permute-done | bytes 4128 | tf_op jit(solution)/shard_map/ppermute | solution.py:467
  118.2 0.6 shard_map.92
  118.8 3.1 %all-to-all-done.4 = f32[8,8,16,128]{3,2,1,0:T(8,128)S(1)} async-done(((f32[8,8,16,128]{3,2,1,0:T(8,128)}), f32[8,8,16,128]{3,2,1,0:T(8,128)S(1)}, u32[]{:S(2)}, u32[]{:S(2)}) %all-to-all-start.4) | async-done | bytes 524320 | tf_op jit(solution)/shard_map/all_to_all | solution.py:451
  121.8 0.8 copy.10
  (11 shorter events, 0.0 us)
Async XLA Ops:
  0.6 2.7 %copy-start = (f32[1,64,16,128]{3,2,1,0:T(8,128)S(1)}, f32[1,64,16,128]{3,2,1,0:T(8,128)}, u32[]{:S(2)}) copy-start(f32[1,64,16,128]{3,2,1,0:T(8,128)} %param.7) | copy-start | bytes 1572868
  0.6 2.7 %copy-start.1 = (f32[1,64,16,128]{3,2,1,0:T(8,128)S(1)}, f32[1,64,16,128]{3,2,1,0:T(8,128)}, u32[]{:S(2)}) copy-start(f32[1,64,16,128]{3,2,1,0:T(8,128)} %param.8) | copy-start | bytes 1572868
  0.7 2.7 %copy-start.2 = (f32[64,16,128]{2,1,0:T(8,128)S(1)}, f32[64,16,128]{2,1,0:T(8,128)}, u32[]{:S(2)}) copy-start(f32[64,16,128]{2,1,0:T(8,128)} %cond.5) | copy-start | bytes 1572868
  3.3 0.9 copy-start.3
  4.3 32.5 %collective-permute-start.1 = (f32[32,3,8,128]{3,2,1,0:T(8,128)S(1)}, f32[32,3,8,128]{3,2,1,0:T(8,128)S(1)}, u32[]{:S(2)}, u32[]{:S(2)}) collective-permute-start(f32[32,3,8,128]{3,2,1,0:T(8,128)S(1)} %get-tuple-element.13), channel_id=1, source_target_pairs={{0,1},{1,2},{2,3},{3,0},{4,5},{5,6},{6,7},{7,4},{8,9},{9,10},{10,1... | collective-permute-start | bytes 1179656 | tf_op jit(solution)/shard_map/ppermute | solution.py:432
  8.4 28.5 %collective-permute-start.2 = (f32[32,3,8,128]{3,2,1,0:T(8,128)S(1)}, f32[32,3,8,128]{3,2,1,0:T(8,128)S(1)}, u32[]{:S(2)}, u32[]{:S(2)}) collective-permute-start(f32[32,3,8,128]{3,2,1,0:T(8,128)S(1)} %get-tuple-element.14), channel_id=1, source_target_pairs={{0,3},{1,0},{2,1},{3,2},{4,7},{5,4},{6,5},{7,6},{8,11},{9,8},{10,9... | collective-permute-start | bytes 1179656 | tf_op jit(solution)/shard_map/ppermute | solution.py:433
  11.8 17.7 %collective-permute-start = (f32[12,16,128]{2,1,0:T(8,128)S(1)}, f32[12,16,128]{2,1,0:T(8,128)S(1)}, u32[]{:S(2)}, u32[]{:S(2)}) collective-permute-start(f32[12,16,128]{2,1,0:T(8,128)S(1)} %copy-done.3), channel_id=1, source_target_pairs={{0,4},{4,0},{1,5},{5,1},{2,6},{6,2},{3,7},{7,3},{8,12},{12,8},{9,1... | collective-permute-start | bytes 294920 | tf_op jit(solution)/shard_map/ppermute | solution.py:425
  29.5 7.4 %copy-start.4 = (s32[3,512]{1,0:T(4,128)S(1)}, s32[3,512]{1,0:T(4,128)}, u32[]{:S(2)}) copy-start(s32[3,512]{1,0:T(4,128)} %rec.1) | copy-start | bytes 18436
  29.5 7.4 %copy-start.5 = (f32[1,512]{1,0:T(1,128)S(1)}, f32[1,512]{1,0:T(1,128)}, u32[]{:S(2)}) copy-start(f32[1,512]{1,0:T(1,128)} %obs.1) | copy-start | bytes 6148
  29.5 7.3 %copy-start.6 = (s32[3,1]{0,1:T(1,128)S(1)}, s32[3,1]{0,1:T(1,128)}, u32[]{:S(2)}) copy-start(s32[3,1]{0,1:T(1,128)} %param.11) | copy-start | bytes 40
  46.5 20.8 %all-to-all-start.1 = ((f32[8,8,16,128]{3,2,1,0:T(8,128)}), f32[8,8,16,128]{3,2,1,0:T(8,128)S(1)}, u32[]{:S(2)}, u32[]{:S(2)}) async-start(f32[8,8,16,128]{3,2,1,0:T(8,128)} %bitcast.4), calls=%async_computation.1 | async-start | bytes 1048576 | tf_op jit(solution)/shard_map/all_to_all | solution.py:451
  57.8 4.6 %collective-permute-start.3 = (f32[8,128]{1,0:T(8,128)S(1)}, f32[8,128]{1,0:T(8,128)S(1)}, u32[]{:S(2)}, u32[]{:S(2)}) collective-permute-start(f32[8,128]{1,0:T(8,128)S(1)} %get-tuple-element.18.own), channel_id=1, source_target_pairs={{0,1},{1,0},{2,3},{3,2},{4,5},{5,4},{6,7},{7,6},{8,9},{9,8},{10,11... | collective-permute-start | bytes 12296 | tf_op jit(solution)/shard_map/ppermute | solution.py:453
  87.0 18.7 %all-to-all-start.3 = ((f32[8,16,128]{2,1,0:T(8,128)}), f32[8,16,128]{2,1,0:T(8,128)S(1)}, u32[]{:S(2)}, u32[]{:S(2)}) async-start(f32[8,16,128]{2,1,0:T(8,128)} %shard_map.90), calls=%async_computation.3 | async-start | bytes 131072 | tf_op jit(solution)/shard_map/all_to_all | solution.py:451
  92.7 13.1 %collective-permute-start.4 = (f32[8,128]{1,0:T(8,128)S(1)}, f32[8,128]{1,0:T(8,128)S(1)}, u32[]{:S(2)}, u32[]{:S(2)}) collective-permute-start(f32[8,128]{1,0:T(8,128)S(1)} %get-tuple-element.20.own), channel_id=1, source_target_pairs={{0,4},{4,0},{1,5},{5,1},{2,6},{6,2},{3,7},{7,3},{8,12},{12,8},{9,1... | collective-permute-start | bytes 12296 | tf_op jit(solution)/shard_map/ppermute | solution.py:462
  106.5 15.3 %all-to-all-start.4 = ((f32[8,8,16,128]{3,2,1,0:T(8,128)}), f32[8,8,16,128]{3,2,1,0:T(8,128)S(1)}, u32[]{:S(2)}, u32[]{:S(2)}) async-start(f32[8,8,16,128]{3,2,1,0:T(8,128)} %get-tuple-element.22), calls=%async_computation.4 | async-start | bytes 1048576 | tf_op jit(solution)/shard_map/all_to_all | solution.py:451
  112.3 5.8 %collective-permute-start.5 = (f32[8,128]{1,0:T(8,128)S(1)}, f32[8,128]{1,0:T(8,128)S(1)}, u32[]{:S(2)}, u32[]{:S(2)}) collective-permute-start(f32[8,128]{1,0:T(8,128)S(1)} %get-tuple-element.21.refs_0_), channel_id=1, source_target_pairs={{0,2},{2,0},{1,3},{3,1},{4,6},{6,4},{5,7},{7,5},{8,10},{10,8},{9,1... | collective-permute-start | bytes 12296 | tf_op jit(solution)/shard_map/ppermute | solution.py:467
